TPU v7x, 256 devices: a whole 4x4x8 slice. The times are simulated.
256 devices in a mesh: batch: 2 (over core), queue: 128 (over x, y, z).
Axes of the slice: x: 4, y: 4, z: 8, core: 2. Of those that a mesh axis runs over, the one named last changes fastest.
Arguments:
- queries: bfloat16 [2048, 1024], P('batch'), may hold values from -128 to 128
- queue: bfloat16 [196608, 1024], P('queue'), may hold values from -8 to 8
- mentor_logit_grid: bfloat16 [2048, 196608], P('batch', 'queue'), may hold values from -40 to 260
- positives: int32 [2048], P('batch'), may hold values from 0 to 196607
Outputs:
- query_grad: float32 [2048, 1024], P('batch')
- loss: float32 [], replicated
All inputs are finite; a program needn't handle non-finite values.
Results may differ from a plain program's by a relative error of at most 0.0026.
Values sent between devices are 32-bit elements; how exact they have to be, the bound alone decides.
No kernel may reach another device: no remote copies, remote signals or barrier semaphores. Data moves between devices by JAX's collectives and lax.ppermute only.
A program may use at most 64 MiB of HBM per device.

v0:
```python
import math

import jax
import jax.numpy as jnp
from jax import lax
from jax.sharding import Mesh
from jax.sharding import PartitionSpec as P

QUEUE = ("queue_0", "queue_1", "queue_2")


score_factor = 3.0
reward_value = 12.0


def collected_together(shard, axis):
    leaves = jax.tree.leaves(shard)
    order = sorted(range(len(leaves)), key=lambda k: -leaves[k].size)
    width = (1, *leaves[order[0]].shape)[-1]
    lines = [
        jnp.pad(leaves[k].reshape(-1), (0, -leaves[k].size % width)).reshape(-1, width)
        for k in order
    ]
    both, at, found = (lax.all_gather(jnp.concatenate(lines), axis), 0, {})
    for k, line in zip(order, lines):
        share = both[:, at : at + len(line)].reshape(len(both), -1)
        found[k] = share[:, : leaves[k].size].reshape(-1, *leaves[k].shape)
        at += len(line)
    numbers = iter(range(len(leaves)))
    return jax.tree.map(lambda _: found[next(numbers)], shard)


def merged_by_axis(shard, axes, combine):
    for axis in axes:
        pieces = collected_together(shard, axis)
        shard = jax.tree.map(lambda part: part[0], pieces)
        for k in range(1, lax.axis_size(axis)):
            shard = combine(shard, jax.tree.map(lambda part: part[k], pieces))
    return shard


def total_of_pieces(shard, axis):
    return lax.all_gather(shard, axis).sum(0)


def merge_stats(earlier, latter):
    stud_top = jnp.maximum(earlier[0], latter[0])
    stud_total = earlier[1] * jnp.exp(earlier[0] - stud_top) + latter[1] * jnp.exp(
        latter[0] - stud_top
    )
    teach_top = jnp.maximum(earlier[2], latter[2])
    early_factor = jnp.exp(earlier[2] - teach_top)
    late_factor = jnp.exp(latter[2] - teach_top)
    teach_total = earlier[3] * early_factor + latter[3] * late_factor
    cross_total = earlier[4] * early_factor + latter[4] * late_factor
    return (stud_top, stud_total, teach_top, teach_total, cross_total)


def local(queries, queue, mentor_logit_grid, positives):
    row_count = queries.shape[0]
    key_count = queue.shape[0]
    score_scale = score_factor / math.sqrt(queries.shape[1])
    scores = score_scale * jnp.einsum(
        "rd,kd->rk", queries, queue, preferred_element_type=jnp.float32
    )
    key_index = lax.axis_index(QUEUE) * key_count + jnp.arange(key_count, dtype=jnp.int32)
    positive_match = (key_index[None, :] == positives[:, None]).astype(jnp.float32)
    mentor_model = mentor_logit_grid.astype(jnp.float32) + reward_value * positive_match
    stud_max = jnp.max(scores, axis=1)
    stud_sum = jnp.sum(jnp.exp(scores - stud_max[:, None]), axis=1)
    teach_max = jnp.max(mentor_model, axis=1)
    teach_exp = jnp.exp(mentor_model - teach_max[:, None])
    teach_sum = jnp.sum(teach_exp, axis=1)
    cross_sum = jnp.sum(teach_exp * (mentor_model - scores), axis=1)
    stud_top, stud_total, teach_top, teach_total, cross_total = merged_by_axis(
        (stud_max, stud_sum, teach_max, teach_sum, cross_sum), QUEUE, merge_stats
    )
    stud_log = stud_top + jnp.log(stud_total)
    teach_log = teach_top + jnp.log(teach_total)
    divergence = cross_total / teach_total - teach_log + stud_log
    weights = (
        jnp.exp(scores - stud_log[:, None]) - jnp.exp(mentor_model - teach_log[:, None])
    ).astype(jnp.bfloat16)
    partial_value = jnp.dot(weights, queue, preferred_element_type=jnp.float32)
    query_grad = lax.psum(partial_value, QUEUE)
    loss_total = total_of_pieces(jnp.sum(divergence), "batch")
    loss_value = loss_total / (row_count * lax.axis_size("batch"))
    return (query_grad, loss_value)


def solution(mesh):
    finer = Mesh(
        mesh.devices.reshape(mesh.shape["batch"], 4, 4, 8),
        ("batch", "queue_0", "queue_1", "queue_2"),
    )
    return jax.shard_map(
        local,
        mesh=finer,
        in_specs=(P("batch", None), P(QUEUE, None), P("batch", QUEUE), P("batch")),
        out_specs=(P("batch", None), P()),
        check_vma=False,
    )
```

profile of v0, /device:TPU:2, one launch (start us, length us, event | category | flops | bytes accessed | tf_op | source)
XLA Modules:
  0.0 328.8 jit_solution(2055025822654297718)
XLA Ops:
  7.2 0.0 copy-start
  7.2 0.0 all-reduce.3.cloned.1.call-start
  7.2 1.8 copy-done
  9.1 0.0 copy-start.1
  9.1 0.0 copy-start.3
  9.1 5.3 %multiply_reduce_fusion.1 = (f32[1024]{0:T(1024)S(1)}, f32[1024,1536]{1,0:T(8,128)S(1)}) fusion(bf16[1024,1024]{1,0:T(8,128)(2,1)} %param.4, bf16[1536,1024]{1,0:T(8,128)(2,1)S(1)} %copy-done), kind=kOutput, calls=%fused_computation.7 | convolution fusion | flops 3224370176 | bytes 11538432 | tf_op jit(solution)/shard_map/rd,kd->rk/dot_general | solution.py:63
  14.3 0.0 copy-done.1
  14.3 0.0 copy-done.3
  14.4 0.0 copy-start.2
  14.4 1.2 fusion.1
  15.6 4.2 %multiply_reduce_fusion = (f32[1024]{0:T(1024)S(1)}, f32[1024]{0:T(1024)S(1)}, f32[1024]{0:T(1024)S(1)}) fusion(bf16[1024,1536]{1,0:T(8,128)(2,1)S(1)} %copy-done.1, f32[1024,1536]{1,0:T(8,128)S(1)} %get-tuple-element.58, f32[1024]{0:T(1024)S(1)} %fusion.1, s32[1536]{0:T(1024)S(1)} %iota_add_fusion, s32[1024]{0:T(1024)S(1)} %copy-done.3, ...), kind=kLoop, calls=%fused_computation.1 | loop fusion | flops 18871296 | bytes 9467904 | tf_op jit(solution)/shard_map/reduce_sum | solution.py:74
  19.8 0.0 copy-done.2
  19.8 12.1 %all-gather.3 = f32[4,5,1024]{2,1,0:T(8,128)S(1)} all-gather(f32[1,5,1024]{2,1,0:T(8,128)S(1)} %bitcast.449), channel_id=2, replica_groups=mesh['batch'=2,'queue_0'=4,'queue_1'=4,'queue_2'=8] {'queue_0'}, dimensions={0}, use_global_device_ids=true | all-gather | bytes 102400 | tf_op jit(solution)/shard_map/all_gather | solution.py:24
  31.9 0.1 fusion.31
  31.9 0.1 fusion.49
  32.1 12.5 %all-gather.4 = f32[4,5,1024]{2,1,0:T(8,128)S(1)} all-gather(f32[1,5,1024]{2,1,0:T(8,128)S(1)} %bitcast.450), channel_id=3, replica_groups=mesh['batch'=2,'queue_0'=4,'queue_1'=4,'queue_2'=8] {'queue_1'}, dimensions={0}, use_global_device_ids=true | all-gather | bytes 102400 | tf_op jit(solution)/shard_map/all_gather | solution.py:24
  44.6 0.1 fusion.4
  44.7 0.1 fusion.22
  44.8 28.4 %all-gather.5 = f32[8,5,1024]{2,1,0:T(8,128)S(1)} all-gather(f32[1,5,1024]{2,1,0:T(8,128)S(1)} %bitcast.451), channel_id=4, replica_groups=mesh['batch'=2,'queue_0'=4,'queue_1'=4,'queue_2'=8] {'queue_2'}, dimensions={0}, use_global_device_ids=true | all-gather | bytes 184320 | tf_op jit(solution)/shard_map/all_gather | solution.py:24
  73.3 0.1 fusion.94
  73.3 0.1 fusion.95
  73.4 0.7 add_reduce_fusion
  74.1 0.0 copy-start.4
  74.1 8.5 %fusion.2 = f32[1024,1024]{1,0:T(8,128)} fusion(bf16[1536,1024]{1,0:T(8,128)(2,1)S(1)} %copy-done, bf16[1024,1536]{1,0:T(8,128)(2,1)} %param.6, f32[1024,1536]{1,0:T(8,128)} %copy-done.2, f32[1024]{0:T(1024)S(1)} %log_add_fusion, f32[1024]{0:T(1024)S(1)} %get-tuple-element.6, s32[1536]{0:T(1024)S(1)} %iota_add_fusion, s32[1024]{0:T(1024)S(1)} %copy-done.3), kind=kOutput, calls=%fused_computation.8 | convolution fusion | flops 3235381248 | bytes 16795648 | tf_op jit(solution)/shard_map/dot_general | solution.py:84
  82.6 0.0 all-reduce.3.cloned.1.call-update
  82.6 0.0 copy-done.4
  82.6 0.6 dynamic-slice
  83.2 1.4 dynamic-update-slice
  84.6 2.4 all-reduce
  87.0 0.6 reduce_sum.49
  88.3 227.7 %all-reduce.3.cloned.1.call-done = f32[1024,1024]{1,0:T(8,128)} async-done(((f32[1024,1024]{1,0:T(8,128)}), f32[1024,1024]{1,0:T(8,128)}) %all-reduce.3.cloned.1.call-update) | async-done | bytes 4194320 | tf_op jit(solution)/shard_map/psum | solution.py:85
  316.0 4.8 %copy.8 = f32[1024,1024]{1,0:T(8,128)} copy(f32[1024,1024]{1,0:T(8,128)} %all-reduce.3.cloned.1.call-done) | data formatting | bytes 8388608
  (7 shorter events, 0.2 us)
Async XLA Ops:
  7.2 1.9 copy-start
  7.2 308.8 %all-reduce.3.cloned.1.call-start = ((), (), s32[]{:S(2)}) async-start(), calls=%async_computation | async-start | bytes 8388608 | tf_op jit(solution)/shard_map/psum | solution.py:85
  9.1 5.3 %copy-start.1 = (bf16[1024,1536]{1,0:T(8,128)(2,1)S(1)}, bf16[1024,1536]{1,0:T(8,128)(2,1)}, u32[]{:S(2)}) copy-start(bf16[1024,1536]{1,0:T(8,128)(2,1)} %param.6) | copy-start | bytes 9437188
  9.1 5.3 %copy-start.3 = (s32[1024]{0:T(1024)S(1)}, s32[1024]{0:T(1024)}, u32[]{:S(2)}) copy-start(s32[1024]{0:T(1024)} %param.7) | copy-start | bytes 12292
  14.4 5.4 %copy-start.2 = (f32[1024,1536]{1,0:T(8,128)}, f32[1024,1536]{1,0:T(8,128)S(1)}, u32[]{:S(2)}) copy-start(f32[1024,1536]{1,0:T(8,128)S(1)} %get-tuple-element.58) | copy-start | bytes 18874372
  74.1 8.5 %copy-start.4 = (u32[256]{0:T(256)S(1)}, u32[256]{0:T(256)}, u32[]{:S(2)}) copy-start(u32[256]{0:T(256)} %constant.33) | copy-start | bytes 3076
Sparse Core Ops, SparseCore 0:
  82.7 233.2 all-reduce.2
where the time goes:
time: 329 us
  waiting for transfers between devices  228 us (69%)
  blocking collectives  55.4 us (17%)
  between operations  15.9 us (5%)
  matrix products  13.8 us (4%)
  local copies, waits for them, and re-layouts  8.86 us (3%)
  other arithmetic  7.03 us (2%)
    psum x1, waiting for transfers between devices, local(): query_grad = lax.psum(partial_value, QUEUE)  228 us
    all_gather x3, blocking collectives, collected_together(): both, at, found = (lax.all_gather(jnp.concatenate(lines), axis), 0, {})  53 us
    unnamed x14, local copies, waits for them, and re-layouts  8.59 us
    dot_general x1, matrix products, local(): partial_value = jnp.dot(weights, queue, preferred_element_type=jnp.float32)  8.49 us
  transfers between devices with their start and end apart: 1, of which 1 were waited for; matrix products, arithmetic and copies ran while one was open for 1% of the time, Pallas kernels for 0%

commit v1 on v0

v1 whole, which is shorter than its diff:
```python
import math

import jax
import jax.numpy as jnp
from jax import lax
from jax.sharding import Mesh
from jax.sharding import PartitionSpec as P

X, Y, Z = "queue_0", "queue_1", "queue_2"
QUEUE = (X, Y, Z)

score_factor = 3.0
reward_value = 12.0


def exchanged(part, axis, k):
    n = lax.axis_size(axis)
    return lax.ppermute(part, axis, [(i, i ^ k) for i in range(n)])


def scattered_sum(parts, axis):
    me = lax.axis_index(axis)
    total = lax.dynamic_index_in_dim(parts, me, 0, False)
    for k in (2, 1, 3):
        mine = lax.dynamic_index_in_dim(parts, me ^ k, 0, False)
        total = total + exchanged(mine, axis, k)
    return total


def gathered(part, axis):
    me = lax.axis_index(axis)
    out = jnp.zeros((lax.axis_size(axis), *part.shape), part.dtype)
    for k, piece in [(k, exchanged(part, axis, k)) for k in (2, 1, 3)] + [(0, part)]:
        out = lax.dynamic_update_index_in_dim(out, piece, me ^ k, 0)
    return out


def spread(part, axes):
    n = math.prod(lax.axis_size(a) for a in axes)
    return lax.all_to_all(jnp.broadcast_to(part[None], (n, *part.shape)), axes, 0, 0)


def summed_everywhere(value):
    rows, width = value.shape
    half = rows // 2
    first = value[:half].reshape(4, -1, width)
    second = value[half:].reshape(4, -1, width)
    first = scattered_sum(first, X)
    second = scattered_sum(second, Y)
    first = scattered_sum(first.reshape(4, -1, width), Y)
    second = scattered_sum(second.reshape(4, -1, width), X)
    n = lax.axis_size(Z)
    both = jnp.concatenate(
        [first.reshape(n, -1, width), second.reshape(n, -1, width)], 1
    )
    mine = lax.all_to_all(both, Z, 0, 0).sum(0)
    both = spread(mine, (Z,))
    at = both.shape[1] // 2
    first = both[:, :at].reshape(-1, width)
    second = both[:, at:].reshape(-1, width)
    first = gathered(first, Y).reshape(-1, width)
    second = gathered(second, X).reshape(-1, width)
    first = gathered(first, X).reshape(-1, width)
    second = gathered(second, Y).reshape(-1, width)
    return jnp.concatenate([first, second], 0)


def merged(stats, axes):
    pieces = spread(stats, axes)
    logs = pieces[:, :2]
    top = logs.max(0)
    factor = jnp.exp(logs - top)
    total = factor.sum(0)
    mean = (factor[:, 1] * pieces[:, 2]).sum(0) / total[1]
    return jnp.concatenate([top + jnp.log(total), mean[None]], 0)


def local(queries, queue, mentor_logit_grid, positives):
    row_count = queries.shape[0]
    key_count = queue.shape[0]
    score_scale = score_factor / math.sqrt(queries.shape[1])
    scores = score_scale * jnp.einsum(
        "rd,kd->rk", queries, queue, preferred_element_type=jnp.float32
    )
    key_index = lax.axis_index(QUEUE) * key_count + jnp.arange(key_count, dtype=jnp.int32)
    positive_match = (key_index[None, :] == positives[:, None]).astype(jnp.float32)
    mentor_model = mentor_logit_grid.astype(jnp.float32) + reward_value * positive_match
    stud_max = jnp.max(scores, axis=1)
    stud_sum = jnp.sum(jnp.exp(scores - stud_max[:, None]), axis=1)
    teach_max = jnp.max(mentor_model, axis=1)
    teach_exp = jnp.exp(mentor_model - teach_max[:, None])
    teach_sum = jnp.sum(teach_exp, axis=1)
    cross_sum = jnp.sum(teach_exp * (mentor_model - scores), axis=1)
    stats = jnp.stack(
        [
            (stud_max + jnp.log(stud_sum)).reshape(8, -1),
            (teach_max + jnp.log(teach_sum)).reshape(8, -1),
            (cross_sum / teach_sum).reshape(8, -1),
        ]
    )
    stud_log, teach_log, cross = merged(merged(stats, (X, Y)), (Z,))
    divergence = jnp.sum(cross - teach_log + stud_log)
    stud_log = stud_log.reshape(-1)
    teach_log = teach_log.reshape(-1)
    weights = (
        jnp.exp(scores - stud_log[:, None]) - jnp.exp(mentor_model - teach_log[:, None])
    ).astype(jnp.bfloat16)
    partial_value = jnp.dot(weights, queue, preferred_element_type=jnp.float32)
    query_grad = summed_everywhere(partial_value)
    loss_total = divergence + lax.ppermute(divergence, "batch", [(0, 1), (1, 0)])
    loss_value = loss_total / (row_count * lax.axis_size("batch"))
    return (query_grad, loss_value)


def solution(mesh):
    finer = Mesh(
        mesh.devices.reshape(mesh.shape["batch"], 4, 4, 8),
        ("batch", X, Y, Z),
    )
    return jax.shard_map(
        local,
        mesh=finer,
        in_specs=(P("batch", None), P(QUEUE, None), P("batch", QUEUE), P("batch")),
        out_specs=(P("batch", None), P()),
        check_vma=False,
    )
```

time: 329 us -> 183 us (0.56)
  waiting for transfers between devices: 228 us -> 61.4 us
  starting transfers between devices: 0.04 us -> 42.6 us
  blocking collectives: 55.4 us -> 26.7 us
  between operations: 15.9 us -> 3.44 us
  other arithmetic: 7.03 us -> 17.1 us
  local copies, waits for them, and re-layouts: 8.86 us -> 18.8 us
    psum x1 -> x0, waiting for transfers between devices: 228 us -> none  [local(): query_grad = lax.psum(partial_value, QUEUE)]
    all_gather x3 -> x0, blocking collectives: 53 us -> none  [collected_together(): both, at, found = (lax.all_gather(jnp.concatenate(lines), axis), 0, {})]
    ppermute x0 -> x25, waiting for transfers between devices: none -> 42.3 us  [the longest x24 40.9 us: exchanged(): return lax.ppermute(part, axis, [(i, i ^ k) for i in range(n)])]
    ppermute x0 -> x25, starting transfers between devices: none -> 30.7 us  [the longest x24 30.7 us: exchanged(): return lax.ppermute(part, axis, [(i, i ^ k) for i in range(n)])]
    all_to_all x0 -> x2, blocking collectives: none -> 26.7 us  [spread(): lax.all_to_all(jnp.broadcast_to(part[None], (n, *part.shape)), axes, 0, 0)]
    all_to_all x0 -> x2, waiting for transfers between devices: none -> 19.1 us  [the longest x1 10.4 us: summed_everywhere(): mine = lax.all_to_all(both, Z, 0, 0).sum(0)]
    all_to_all x0 -> x2, starting transfers between devices: none -> 11.9 us  [the longest x1 8.46 us: spread(): lax.all_to_all(jnp.broadcast_to(part[None], (n, *part.shape)), axes, 0, 0)]
    dynamic_update_slice x0 -> x16, local copies, waits for them, and re-layouts: none -> 5.02 us  [gathered(): out = lax.dynamic_update_index_in_dim(out, piece, me ^ k, 0)]
  transfers between devices with their start and end apart: 1 -> 27, of which waited for: 1 -> 13; matrix products, arithmetic and copies ran while one was open for 1% -> 8% of each run, Pallas kernels for 0% -> 0%
where the time goes in v1:
time: 183 us
  waiting for transfers between devices  61.4 us (34%)
  starting transfers between devices  42.6 us (23%)
  blocking collectives  26.7 us (15%)
  local copies, waits for them, and re-layouts  18.8 us (10%)
  other arithmetic  17.1 us (9%)
  matrix products  12.5 us (7%)
  between operations  3.44 us (2%)
    ppermute x24, waiting for transfers between devices, exchanged(): return lax.ppermute(part, axis, [(i, i ^ k) for i in range(n)])  40.9 us
    ppermute x24, starting transfers between devices, exchanged(): return lax.ppermute(part, axis, [(i, i ^ k) for i in range(n)])  30.7 us
    all_to_all x2, blocking collectives, spread(): lax.all_to_all(jnp.broadcast_to(part[None], (n, *part.shape)), axes, 0, 0)  26.7 us
    all_to_all x1, waiting for transfers between devices, summed_everywhere(): mine = lax.all_to_all(both, Z, 0, 0).sum(0)  10.4 us
    all_to_all x1, waiting for transfers between devices, spread(): lax.all_to_all(jnp.broadcast_to(part[None], (n, *part.shape)), axes, 0, 0)  8.73 us
    all_to_all x1, starting transfers between devices, spread(): lax.all_to_all(jnp.broadcast_to(part[None], (n, *part.shape)), axes, 0, 0)  8.46 us
    dot_general x1, matrix products, local(): partial_value = jnp.dot(weights, queue, preferred_element_type=jnp.float32)  7.19 us
    dot_general x1, matrix products, local(): jnp.einsum('rd,kd->rk', queries, queue, preferred_element_type=jnp.float32)  5.27 us
  transfers between devices with their start and end apart: 27, of which 13 were waited for; matrix products, arithmetic and copies ran while one was open for 8% of the time, Pallas kernels for 0%

profile of v1, /device:TPU:2, one launch (start us, length us, event | category | flops | bytes accessed | tf_op | source)
XLA Modules:
  0.0 182.5 jit_solution(15846233494434483033)
XLA Ops:
  0.7 1.9 %copy-done = bf16[1536,1024]{1,0:T(8,128)(2,1)S(1)} copy-done((bf16[1536,1024]{1,0:T(8,128)(2,1)S(1)}, bf16[1536,1024]{1,0:T(8,128)(2,1)}, u32[]{:S(2)}) %copy-start) | copy-done | bytes 3145752
  2.5 5.3 %multiply_reduce_fusion.1 = (f32[1024]{0:T(1024)S(1)}, f32[1024,1536]{1,0:T(8,128)S(1)}) fusion(bf16[1024,1024]{1,0:T(8,128)(2,1)} %param.4, bf16[1536,1024]{1,0:T(8,128)(2,1)S(1)} %copy-done), kind=kOutput, calls=%fused_computation.7 | convolution fusion | flops 3224370176 | bytes 11538432 | tf_op jit(solution)/shard_map/rd,kd->rk/dot_general | solution.py:82
  7.8 1.2 fusion.1
  9.1 5.0 %exponential_reduce_fusion = (f32[1024]{0:T(1024)S(1)}, f32[1024]{0:T(1024)S(1)}, f32[1024]{0:T(1024)S(1)}) fusion(f32[1024,1536]{1,0:T(8,128)S(1)} %get-tuple-element.30, f32[1024]{0:T(1024)S(1)} %get-tuple-element.29, f32[1024]{0:T(1024)S(1)} %fusion.1, s32[1024]{0:T(1024)S(1)} %copy-done.5, s32[1536]{0:T(1024)S(1)} %iota_add_fusion, ...), kind=kLoop, calls=%fused_computation.6 | loop fusion | flops 18871296 | bytes 9467904 | tf_op jit(solution)/shard_map/reduce_sum | solution.py:89
  14.1 13.9 %all_to_all.20 = f32[16,3,8,128]{3,2,1,0:T(8,128)S(1)} all-to-all(f32[16,3,8,128]{3,2,1,0:T(8,128)S(1)} %broadcast_in_dim.75), channel_id=1, replica_groups=mesh['batch'=2,'queue_0'=4,'queue_1'=4,'queue_2'=8] {'queue_0','queue_1'}, dimensions={0} | all-to-all | bytes 393216 | tf_op jit(solution)/shard_map/all_to_all | solution.py:40
  28.1 0.6 broadcast_in_dim.76
  28.7 8.5 %all-to-all-start.1 = ((f32[8,3,8,128]{3,2,1,0:T(8,128)}), f32[8,3,8,128]{3,2,1,0:T(8,128)S(1)}, u32[]{:S(2)}, u32[]{:S(2)}) async-start(f32[8,3,8,128]{3,2,1,0:T(8,128)} %broadcast_in_dim.76), calls=%async_computation.1 | async-start | bytes 196608 | tf_op jit(solution)/shard_map/all_to_all | solution.py:40
  37.2 8.7 %all-to-all-done.1 = f32[8,3,8,128]{3,2,1,0:T(8,128)S(1)} async-done(((f32[8,3,8,128]{3,2,1,0:T(8,128)}), f32[8,3,8,128]{3,2,1,0:T(8,128)S(1)}, u32[]{:S(2)}, u32[]{:S(2)}) %all-to-all-start.1) | async-done | bytes 98336 | tf_op jit(solution)/shard_map/all_to_all | solution.py:40
  45.9 0.6 fusion.20
  46.6 7.2 %fusion.2 = f32[1024,1024]{1,0:T(8,128)S(1)} fusion(bf16[1536,1024]{1,0:T(8,128)(2,1)S(1)} %copy-done, bf16[1024,1536]{1,0:T(8,128)(2,1)} %param.6, f32[1024,1536]{1,0:T(8,128)} %copy-done.3, f32[1024]{0:T(1024)S(1)} %get-tuple-element.26, f32[1024]{0:T(1024)S(1)} %get-tuple-element.25, s32[1536]{0:T(1024)S(1)} %iota_add_fusion, s32[1024]{0:T(1024)S(1)} %copy-done.5), kind=kOutput, calls=%fused_computation.9 | convolution fusion | flops 3235381248 | bytes 16795648 | tf_op jit(solution)/shard_map/dot_general | solution.py:108
  53.8 1.7 fusion.22
  55.5 1.3 copy-done.2
  56.9 1.2 dynamic-slice_bitcast_fusion.5
  58.1 1.6 collective-permute-start
  59.6 1.4 collective-permute-start.1
  61.0 1.1 collective-permute-start.2
  62.1 2.6 %dynamic-slice_bitcast_fusion.2 = (f32[128,1024]{1,0:T(8,128)}, f32[128,1024]{1,0:T(8,128)}, f32[128,1024]{1,0:T(8,128)}) fusion(f32[4,128,1024]{2,1,0:T(8,128)} %bitcast.119, s32[]{:T(128)S(6)} %select_n.57, s32[]{:T(128)S(6)} %select_n.59, s32[]{:T(128)S(6)} %select_n.58), kind=kLoop, calls=%fused_computation.26 | loop fusion | bytes 3145740 | tf_op jit(solution)/shard_map/jit(dynamic_index_in_dim)/squeeze | solution.py:25
  64.7 1.6 collective-permute-start.6
  66.6 8.1 %collective-permute-done = f32[128,1024]{1,0:T(8,128)} collective-permute-done((f32[128,1024]{1,0:T(8,128)}, f32[128,1024]{1,0:T(8,128)}, u32[]{:S(2)}, u32[]{:S(2)}) %collective-permute-start) | collective-permute-done | bytes 524320 | tf_op jit(solution)/shard_map/ppermute | solution.py:18
  74.7 1.1 collective-permute-start.8
  75.8 5.9 %collective-permute-done.1 = f32[128,1024]{1,0:T(8,128)} collective-permute-done((f32[128,1024]{1,0:T(8,128)}, f32[128,1024]{1,0:T(8,128)}, u32[]{:S(2)}, u32[]{:S(2)}) %collective-permute-start.1) | collective-permute-done | bytes 524320 | tf_op jit(solution)/shard_map/ppermute | solution.py:18
  82.0 1.7 fusion.6
  83.7 2.0 %collective-permute-start.3 = (f32[32,1024]{1,0:T(8,128)S(1)}, f32[32,1024]{1,0:T(8,128)S(1)}, u32[]{:S(2)}, u32[]{:S(2)}) collective-permute-start(f32[32,1024]{1,0:T(8,128)S(1)} %get-tuple-element.17), channel_id=1, source_target_pairs={{0,16},{8,24},{16,0},{24,8},{1,17},{9,25},{17,1},{25,9},{2,18},{10... | collective-permute-start | bytes 393224 | tf_op jit(solution)/shard_map/ppermute | solution.py:18
  85.9 2.0 %collective-permute-start.5 = (f32[32,1024]{1,0:T(8,128)S(1)}, f32[32,1024]{1,0:T(8,128)S(1)}, u32[]{:S(2)}, u32[]{:S(2)}) collective-permute-start(f32[32,1024]{1,0:T(8,128)S(1)} %get-tuple-element.18), channel_id=1, source_target_pairs={{0,24},{8,16},{16,8},{24,0},{1,25},{9,17},{17,9},{25,1},{2,26},{10... | collective-permute-start | bytes 393224 | tf_op jit(solution)/shard_map/ppermute | solution.py:18
  87.9 1.7 fusion.4
  89.6 0.8 copy-done.4
  90.4 0.8 dynamic-slice_bitcast_fusion.8
  91.1 1.8 collective-permute-start.10
  92.9 0.6 collective-permute-start.11
  93.5 1.7 collective-permute-start.9
  95.3 1.8 %collective-permute-done.10 = f32[32,1024]{1,0:T(8,128)} collective-permute-done((f32[32,1024]{1,0:T(8,128)}, f32[32,1024]{1,0:T(8,128)}, u32[]{:S(2)}, u32[]{:S(2)}) %collective-permute-start.10) | collective-permute-done | bytes 131104 | tf_op jit(solution)/shard_map/ppermute | solution.py:18
  97.1 3.8 %collective-permute-done.11 = f32[32,1024]{1,0:T(8,128)} collective-permute-done((f32[32,1024]{1,0:T(8,128)}, f32[32,1024]{1,0:T(8,128)}, u32[]{:S(2)}, u32[]{:S(2)}) %collective-permute-start.11) | collective-permute-done | bytes 131104 | tf_op jit(solution)/shard_map/ppermute | solution.py:18
  100.9 1.1 fusion.8
  102.0 0.7 reshape.128
  102.7 1.7 pad_maximum_fusion.1
  104.4 3.4 %all-to-all-start.2 = ((f32[8,8,1024]{2,1,0:T(8,128)}), f32[8,8,1024]{2,1,0:T(8,128)S(1)}, u32[]{:S(2)}, u32[]{:S(2)}) async-start(f32[8,8,1024]{2,1,0:T(8,128)} %pad_maximum_fusion.1), calls=%async_computation.2 | async-start | bytes 524288 | tf_op jit(solution)/shard_map/all_to_all | solution.py:56
  107.8 10.4 %all-to-all-done.2 = f32[8,8,1024]{2,1,0:T(8,128)S(1)} async-done(((f32[8,8,1024]{2,1,0:T(8,128)}), f32[8,8,1024]{2,1,0:T(8,128)S(1)}, u32[]{:S(2)}, u32[]{:S(2)}) %all-to-all-start.2) | async-done | bytes 262176 | tf_op jit(solution)/shard_map/all_to_all | solution.py:56
  118.3 12.9 %all_to_all.21 = f32[8,8,1024]{2,1,0:T(8,128)S(1)} all-to-all(f32[8,8,1024]{2,1,0:T(8,128)S(1)} %broadcast_in_dim.77), channel_id=1, replica_groups=mesh['batch'=2,'queue_0'=4,'queue_1'=4,'queue_2'=8] {'queue_2'}, dimensions={0} | all-to-all | bytes 524288 | tf_op jit(solution)/shard_map/all_to_all | solution.py:40
  131.2 0.7 reshape.129
  131.9 1.6 collective-permute-start.12
  133.5 0.8 fusion.12
  134.3 0.6 fusion.16
  134.9 1.4 collective-permute-done.24
  137.8 2.3 %collective-permute-start.14 = (f32[32,1024]{1,0:T(8,128)}, f32[32,1024]{1,0:T(8,128)}, u32[]{:S(2)}, u32[]{:S(2)}) collective-permute-start(f32[32,1024]{1,0:T(8,128)} %reshape.129), channel_id=1, source_target_pairs={{0,24},{8,16},{16,8},{24,0},{1,25},{9,17},{17,9},{25,1},{2,26},{10... | collective-permute-start | bytes 393224 | tf_op jit(solution)/shard_map/ppermute | solution.py:18
  140.2 0.7 reshape.132
  140.9 1.9 %collective-permute-start.18 = (f32[32,1024]{1,0:T(8,128)}, f32[32,1024]{1,0:T(8,128)}, u32[]{:S(2)}, u32[]{:S(2)}) collective-permute-start(f32[32,1024]{1,0:T(8,128)} %reshape.132), channel_id=1, source_target_pairs={{0,64},{32,96},{64,0},{96,32},{1,65},{33,97},{65,1},{97,33},{2,66}... | collective-permute-start | bytes 393224 | tf_op jit(solution)/shard_map/ppermute | solution.py:18
  142.7 1.0 collective-permute-start.19
  143.8 1.3 collective-permute-start.20
  145.2 0.9 bitcast_dynamic-update-slice_fusion.13
  146.1 0.9 bitcast_dynamic-update-slice_fusion.12
  147.0 0.9 bitcast_dynamic-update-slice_fusion.11
  148.0 2.0 %collective-permute-start.15 = (f32[128,1024]{1,0:T(8,128)S(1)}, f32[128,1024]{1,0:T(8,128)S(1)}, u32[]{:S(2)}, u32[]{:S(2)}) collective-permute-start(f32[128,1024]{1,0:T(8,128)S(1)} %bitcast.125), channel_id=1, source_target_pairs={{0,64},{32,96},{64,0},{96,32},{1,65},{33,97},{65,1},{97,33},{2,66}... | collective-permute-start | bytes 1572872 | tf_op jit(solution)/shard_map/ppermute | solution.py:18
  149.9 1.0 collective-permute-start.16
  151.0 1.2 collective-permute-start.17
  152.2 0.9 bitcast_dynamic-update-slice_fusion.10
  153.2 0.9 bitcast_dynamic-update-slice_fusion.9
  154.1 1.7 collective-permute-start.21
  156.0 8.5 %collective-permute-done.15 = f32[128,1024]{1,0:T(8,128)S(1)} collective-permute-done((f32[128,1024]{1,0:T(8,128)S(1)}, f32[128,1024]{1,0:T(8,128)S(1)}, u32[]{:S(2)}, u32[]{:S(2)}) %collective-permute-start.15) | collective-permute-done | bytes 524320 | tf_op jit(solution)/shard_map/ppermute | solution.py:18
  164.5 0.9 collective-permute-start.23
  165.7 7.2 %collective-permute-done.16 = f32[128,1024]{1,0:T(8,128)S(1)} collective-permute-done((f32[128,1024]{1,0:T(8,128)S(1)}, f32[128,1024]{1,0:T(8,128)S(1)}, u32[]{:S(2)}, u32[]{:S(2)}) %collective-permute-start.16) | collective-permute-done | bytes 524320 | tf_op jit(solution)/shard_map/ppermute | solution.py:18
  172.9 0.5 collective-permute-done.17
  173.9 3.3 %collective-permute-done.22 = f32[128,1024]{1,0:T(8,128)S(1)} collective-permute-done((f32[128,1024]{1,0:T(8,128)S(1)}, f32[128,1024]{1,0:T(8,128)S(1)}, u32[]{:S(2)}, u32[]{:S(2)}) %collective-permute-start.22) | collective-permute-done | bytes 524320 | tf_op jit(solution)/shard_map/ppermute | solution.py:18
  177.2 1.5 collective-permute-done.23
  178.9 2.5 %pad_maximum_fusion = f32[1024,1024]{1,0:T(8,128)} fusion(f32[512,1024]{1,0:T(8,128)S(1)} %bitcast.123, f32[512,1024]{1,0:T(8,128)S(1)} %bitcast.124), kind=kLoop, calls=%fused_computation.8 | loop fusion | flops 1048576 | bytes 8388608 | tf_op jit(solution)/shard_map/concatenate | solution.py:65
  (65 shorter events, 2.8 us)
Async XLA Ops:
  0.6 1.9 %copy-start = (bf16[1536,1024]{1,0:T(8,128)(2,1)S(1)}, bf16[1536,1024]{1,0:T(8,128)(2,1)}, u32[]{:S(2)}) copy-start(bf16[1536,1024]{1,0:T(8,128)(2,1)} %param.5) | copy-start | bytes 9437188
  2.5 5.3 %copy-start.1 = (bf16[1024,1536]{1,0:T(8,128)(2,1)S(1)}, bf16[1024,1536]{1,0:T(8,128)(2,1)}, u32[]{:S(2)}) copy-start(bf16[1024,1536]{1,0:T(8,128)(2,1)} %param.6) | copy-start | bytes 9437188
  2.5 5.3 %copy-start.5 = (s32[1024]{0:T(1024)S(1)}, s32[1024]{0:T(1024)}, u32[]{:S(2)}) copy-start(s32[1024]{0:T(1024)} %param.7) | copy-start | bytes 12292
  7.8 6.2 %copy-start.3 = (f32[1024,1536]{1,0:T(8,128)}, f32[1024,1536]{1,0:T(8,128)S(1)}, u32[]{:S(2)}) copy-start(f32[1024,1536]{1,0:T(8,128)S(1)} %get-tuple-element.30) | copy-start | bytes 18874372
  28.7 17.2 %all-to-all-start.1 = ((f32[8,3,8,128]{3,2,1,0:T(8,128)}), f32[8,3,8,128]{3,2,1,0:T(8,128)S(1)}, u32[]{:S(2)}, u32[]{:S(2)}) async-start(f32[8,3,8,128]{3,2,1,0:T(8,128)} %broadcast_in_dim.76), calls=%async_computation.1 | async-start | bytes 196608 | tf_op jit(solution)/shard_map/all_to_all | solution.py:40
  55.5 1.3 copy-start.2
  58.1 16.7 %collective-permute-start = (f32[128,1024]{1,0:T(8,128)}, f32[128,1024]{1,0:T(8,128)}, u32[]{:S(2)}, u32[]{:S(2)}) collective-permute-start(f32[128,1024]{1,0:T(8,128)} %get-tuple-element.11), channel_id=1, source_target_pairs={{0,64},{32,96},{64,0},{96,32},{1,65},{33,97},{65,1},{97,33},{2,66}... | collective-permute-start | bytes 1572872 | tf_op jit(solution)/shard_map/ppermute | solution.py:18
  59.6 22.1 %collective-permute-start.1 = (f32[128,1024]{1,0:T(8,128)}, f32[128,1024]{1,0:T(8,128)}, u32[]{:S(2)}, u32[]{:S(2)}) collective-permute-start(f32[128,1024]{1,0:T(8,128)} %get-tuple-element.13), channel_id=1, source_target_pairs={{0,32},{32,0},{64,96},{96,64},{1,33},{33,1},{65,97},{97,65},{2,34}... | collective-permute-start | bytes 1572872 | tf_op jit(solution)/shard_map/ppermute | solution.py:18
  61.0 21.0 %collective-permute-start.2 = (f32[128,1024]{1,0:T(8,128)}, f32[128,1024]{1,0:T(8,128)}, u32[]{:S(2)}, u32[]{:S(2)}) collective-permute-start(f32[128,1024]{1,0:T(8,128)} %get-tuple-element.12), channel_id=1, source_target_pairs={{0,96},{32,64},{64,32},{96,0},{1,97},{33,65},{65,33},{97,1},{2,98}... | collective-permute-start | bytes 1572872 | tf_op jit(solution)/shard_map/ppermute | solution.py:18
  64.7 21.2 %collective-permute-start.6 = (f32[128,1024]{1,0:T(8,128)}, f32[128,1024]{1,0:T(8,128)}, u32[]{:S(2)}, u32[]{:S(2)}) collective-permute-start(f32[128,1024]{1,0:T(8,128)} %get-tuple-element.14), channel_id=1, source_target_pairs={{0,16},{8,24},{16,0},{24,8},{1,17},{9,25},{17,1},{25,9},{2,18},{10... | collective-permute-start | bytes 1572872 | tf_op jit(solution)/shard_map/ppermute | solution.py:18
  66.3 21.6 %collective-permute-start.7 = (f32[128,1024]{1,0:T(8,128)}, f32[128,1024]{1,0:T(8,128)}, u32[]{:S(2)}, u32[]{:S(2)}) collective-permute-start(f32[128,1024]{1,0:T(8,128)} %get-tuple-element.16), channel_id=1, source_target_pairs={{0,8},{8,0},{16,24},{24,16},{1,9},{9,1},{17,25},{25,17},{2,10},{10... | collective-permute-start | bytes 1572872 | tf_op jit(solution)/shard_map/ppermute | solution.py:18
  74.7 13.2 %collective-permute-start.8 = (f32[128,1024]{1,0:T(8,128)}, f32[128,1024]{1,0:T(8,128)}, u32[]{:S(2)}, u32[]{:S(2)}) collective-permute-start(f32[128,1024]{1,0:T(8,128)} %get-tuple-element.15), channel_id=1, source_target_pairs={{0,24},{8,16},{16,8},{24,0},{1,25},{9,17},{17,9},{25,1},{2,26},{10... | collective-permute-start | bytes 1572872 | tf_op jit(solution)/shard_map/ppermute | solution.py:18
  83.7 9.8 %collective-permute-start.3 = (f32[32,1024]{1,0:T(8,128)S(1)}, f32[32,1024]{1,0:T(8,128)S(1)}, u32[]{:S(2)}, u32[]{:S(2)}) collective-permute-start(f32[32,1024]{1,0:T(8,128)S(1)} %get-tuple-element.17), channel_id=1, source_target_pairs={{0,16},{8,24},{16,0},{24,8},{1,17},{9,25},{17,1},{25,9},{2,18},{10... | collective-permute-start | bytes 393224 | tf_op jit(solution)/shard_map/ppermute | solution.py:18
  85.7 9.5 %collective-permute-start.4 = (f32[32,1024]{1,0:T(8,128)S(1)}, f32[32,1024]{1,0:T(8,128)S(1)}, u32[]{:S(2)}, u32[]{:S(2)}) collective-permute-start(f32[32,1024]{1,0:T(8,128)S(1)} %get-tuple-element.19), channel_id=1, source_target_pairs={{0,8},{8,0},{16,24},{24,16},{1,9},{9,1},{17,25},{25,17},{2,10},{10... | collective-permute-start | bytes 393224 | tf_op jit(solution)/shard_map/ppermute | solution.py:18
  85.9 9.3 %collective-permute-start.5 = (f32[32,1024]{1,0:T(8,128)S(1)}, f32[32,1024]{1,0:T(8,128)S(1)}, u32[]{:S(2)}, u32[]{:S(2)}) collective-permute-start(f32[32,1024]{1,0:T(8,128)S(1)} %get-tuple-element.18), channel_id=1, source_target_pairs={{0,24},{8,16},{16,8},{24,0},{1,25},{9,17},{17,9},{25,1},{2,26},{10... | collective-permute-start | bytes 393224 | tf_op jit(solution)/shard_map/ppermute | solution.py:18
  89.6 0.8 copy-start.4
  91.1 6.0 %collective-permute-start.10 = (f32[32,1024]{1,0:T(8,128)}, f32[32,1024]{1,0:T(8,128)}, u32[]{:S(2)}, u32[]{:S(2)}) collective-permute-start(f32[32,1024]{1,0:T(8,128)} %get-tuple-element.22), channel_id=1, source_target_pairs={{0,32},{32,0},{64,96},{96,64},{1,33},{33,1},{65,97},{97,65},{2,34}... | collective-permute-start | bytes 393224 | tf_op jit(solution)/shard_map/ppermute | solution.py:18
  92.9 8.0 %collective-permute-start.11 = (f32[32,1024]{1,0:T(8,128)}, f32[32,1024]{1,0:T(8,128)}, u32[]{:S(2)}, u32[]{:S(2)}) collective-permute-start(f32[32,1024]{1,0:T(8,128)} %get-tuple-element.21), channel_id=1, source_target_pairs={{0,96},{32,64},{64,32},{96,0},{1,97},{33,65},{65,33},{97,1},{2,98}... | collective-permute-start | bytes 393224 | tf_op jit(solution)/shard_map/ppermute | solution.py:18
  93.5 7.4 %collective-permute-start.9 = (f32[32,1024]{1,0:T(8,128)}, f32[32,1024]{1,0:T(8,128)}, u32[]{:S(2)}, u32[]{:S(2)}) collective-permute-start(f32[32,1024]{1,0:T(8,128)} %get-tuple-element.20), channel_id=1, source_target_pairs={{0,64},{32,96},{64,0},{96,32},{1,65},{33,97},{65,1},{97,33},{2,66}... | collective-permute-start | bytes 393224 | tf_op jit(solution)/shard_map/ppermute | solution.py:18
  104.4 13.8 %all-to-all-start.2 = ((f32[8,8,1024]{2,1,0:T(8,128)}), f32[8,8,1024]{2,1,0:T(8,128)S(1)}, u32[]{:S(2)}, u32[]{:S(2)}) async-start(f32[8,8,1024]{2,1,0:T(8,128)} %pad_maximum_fusion.1), calls=%async_computation.2 | async-start | bytes 524288 | tf_op jit(solution)/shard_map/all_to_all | solution.py:56
  131.9 11.9 %collective-permute-start.12 = (f32[32,1024]{1,0:T(8,128)}, f32[32,1024]{1,0:T(8,128)}, u32[]{:S(2)}, u32[]{:S(2)}) collective-permute-start(f32[32,1024]{1,0:T(8,128)} %reshape.129), channel_id=1, source_target_pairs={{0,16},{8,24},{16,0},{24,8},{1,17},{9,25},{17,1},{25,9},{2,18},{10... | collective-permute-start | bytes 393224 | tf_op jit(solution)/shard_map/ppermute | solution.py:18
  134.9 1.4 collective-permute-start.24
  137.5 8.6 %collective-permute-start.13 = (f32[32,1024]{1,0:T(8,128)}, f32[32,1024]{1,0:T(8,128)}, u32[]{:S(2)}, u32[]{:S(2)}) collective-permute-start(f32[32,1024]{1,0:T(8,128)} %reshape.129), channel_id=1, source_target_pairs={{0,8},{8,0},{16,24},{24,16},{1,9},{9,1},{17,25},{25,17},{2,10},{10... | collective-permute-start | bytes 393224 | tf_op jit(solution)/shard_map/ppermute | solution.py:18
  137.8 9.2 %collective-permute-start.14 = (f32[32,1024]{1,0:T(8,128)}, f32[32,1024]{1,0:T(8,128)}, u32[]{:S(2)}, u32[]{:S(2)}) collective-permute-start(f32[32,1024]{1,0:T(8,128)} %reshape.129), channel_id=1, source_target_pairs={{0,24},{8,16},{16,8},{24,0},{1,25},{9,17},{17,9},{25,1},{2,26},{10... | collective-permute-start | bytes 393224 | tf_op jit(solution)/shard_map/ppermute | solution.py:18
  140.9 10.1 %collective-permute-start.18 = (f32[32,1024]{1,0:T(8,128)}, f32[32,1024]{1,0:T(8,128)}, u32[]{:S(2)}, u32[]{:S(2)}) collective-permute-start(f32[32,1024]{1,0:T(8,128)} %reshape.132), channel_id=1, source_target_pairs={{0,64},{32,96},{64,0},{96,32},{1,65},{33,97},{65,1},{97,33},{2,66}... | collective-permute-start | bytes 393224 | tf_op jit(solution)/shard_map/ppermute | solution.py:18
  142.7 10.4 %collective-permute-start.19 = (f32[32,1024]{1,0:T(8,128)}, f32[32,1024]{1,0:T(8,128)}, u32[]{:S(2)}, u32[]{:S(2)}) collective-permute-start(f32[32,1024]{1,0:T(8,128)} %reshape.132), channel_id=1, source_target_pairs={{0,32},{32,0},{64,96},{96,64},{1,33},{33,1},{65,97},{97,65},{2,34}... | collective-permute-start | bytes 393224 | tf_op jit(solution)/shard_map/ppermute | solution.py:18
  143.8 10.2 %collective-permute-start.20 = (f32[32,1024]{1,0:T(8,128)}, f32[32,1024]{1,0:T(8,128)S(1)}, u32[]{:S(2)}, u32[]{:S(2)}) collective-permute-start(f32[32,1024]{1,0:T(8,128)} %reshape.132), channel_id=1, source_target_pairs={{0,96},{32,64},{64,32},{96,0},{1,97},{33,65},{65,33},{97,1},{2,98}... | collective-permute-start | bytes 393224 | tf_op jit(solution)/shard_map/ppermute | solution.py:18
  148.0 16.5 %collective-permute-start.15 = (f32[128,1024]{1,0:T(8,128)S(1)}, f32[128,1024]{1,0:T(8,128)S(1)}, u32[]{:S(2)}, u32[]{:S(2)}) collective-permute-start(f32[128,1024]{1,0:T(8,128)S(1)} %bitcast.125), channel_id=1, source_target_pairs={{0,64},{32,96},{64,0},{96,32},{1,65},{33,97},{65,1},{97,33},{2,66}... | collective-permute-start | bytes 1572872 | tf_op jit(solution)/shard_map/ppermute | solution.py:18
  149.9 22.9 %collective-permute-start.16 = (f32[128,1024]{1,0:T(8,128)S(1)}, f32[128,1024]{1,0:T(8,128)S(1)}, u32[]{:S(2)}, u32[]{:S(2)}) collective-permute-start(f32[128,1024]{1,0:T(8,128)S(1)} %bitcast.126), channel_id=1, source_target_pairs={{0,32},{32,0},{64,96},{96,64},{1,33},{33,1},{65,97},{97,65},{2,34}... | collective-permute-start | bytes 1572872 | tf_op jit(solution)/shard_map/ppermute | solution.py:18
  151.0 22.5 %collective-permute-start.17 = (f32[128,1024]{1,0:T(8,128)S(1)}, f32[128,1024]{1,0:T(8,128)S(1)}, u32[]{:S(2)}, u32[]{:S(2)}) collective-permute-start(f32[128,1024]{1,0:T(8,128)S(1)} %bitcast.127), channel_id=1, source_target_pairs={{0,96},{32,64},{64,32},{96,0},{1,97},{33,65},{65,33},{97,1},{2,98}... | collective-permute-start | bytes 1572872 | tf_op jit(solution)/shard_map/ppermute | solution.py:18
  154.1 19.4 %collective-permute-start.21 = (f32[128,1024]{1,0:T(8,128)S(1)}, f32[128,1024]{1,0:T(8,128)S(1)}, u32[]{:S(2)}, u32[]{:S(2)}) collective-permute-start(f32[128,1024]{1,0:T(8,128)S(1)} %bitcast.129), channel_id=1, source_target_pairs={{0,16},{8,24},{16,0},{24,8},{1,17},{9,25},{17,1},{25,9},{2,18},{10... | collective-permute-start | bytes 1572872 | tf_op jit(solution)/shard_map/ppermute | solution.py:18
  155.8 21.4 %collective-permute-start.22 = (f32[128,1024]{1,0:T(8,128)S(1)}, f32[128,1024]{1,0:T(8,128)S(1)}, u32[]{:S(2)}, u32[]{:S(2)}) collective-permute-start(f32[128,1024]{1,0:T(8,128)S(1)} %bitcast.130), channel_id=1, source_target_pairs={{0,8},{8,0},{16,24},{24,16},{1,9},{9,1},{17,25},{25,17},{2,10},{10... | collective-permute-start | bytes 1572872 | tf_op jit(solution)/shard_map/ppermute | solution.py:18
  164.5 14.3 %collective-permute-start.23 = (f32[128,1024]{1,0:T(8,128)S(1)}, f32[128,1024]{1,0:T(8,128)S(1)}, u32[]{:S(2)}, u32[]{:S(2)}) collective-permute-start(f32[128,1024]{1,0:T(8,128)S(1)} %bitcast.131), channel_id=1, source_target_pairs={{0,24},{8,16},{16,8},{24,0},{1,25},{9,17},{17,9},{25,1},{2,26},{10... | collective-permute-start | bytes 1572872 | tf_op jit(solution)/shard_map/ppermute | solution.py:18

commit v2 on v0

v2 whole, which is shorter than its diff:
```python
import functools
import math

import jax
import jax.numpy as jnp
from jax import lax
from jax.experimental import pallas as pl
from jax.experimental.pallas import tpu as pltpu
from jax.sharding import Mesh
from jax.sharding import PartitionSpec as P

X, Y, Z = "queue_0", "queue_1", "queue_2"
QUEUE = (X, Y, Z)

score_factor = 3.0
reward_value = 12.0


def exchanged(part, axis, k):
    n = lax.axis_size(axis)
    return lax.ppermute(part, axis, [(i, i ^ k) for i in range(n)])


SHARE_LIMIT = 56 * 1024 * 1024
SMALL_LIMIT = 16 * 1024 * 1024

BLOCK = 128
TILE = 512
LIMIT = 60 * 1024 * 1024
ORDER = (2, 1, 3)


def as_column(row):
    return jnp.broadcast_to(row, (BLOCK, BLOCK)).T[:, :1]


def teacher_logits(mentor, wanted):
    column = lax.broadcasted_iota(jnp.int32, mentor.shape, 1)
    return mentor.astype(jnp.float32) + jnp.where(column == wanted, reward_value, 0.0)


def stats_kernel(
    base_ref, queries_ref, queue_ref, mentor_ref, positives_ref, scores_ref, sent_ref
):
    step = pl.program_id(0)
    scale = score_factor / math.sqrt(queries_ref.shape[1])
    tile = scale * lax.dot_general(
        queries_ref[...], queue_ref[...], (((1,), (1,)), ((), ())),
        preferred_element_type=jnp.float32,
    )
    scores_ref[...] = tile
    for part in range(TILE // BLOCK):
        at = slice(part * BLOCK, (part + 1) * BLOCK)
        number = step * (TILE // BLOCK) + part
        scores = tile[at, :]
        stud_max = jnp.max(scores, axis=1, keepdims=True)
        stud_sum = jnp.sum(jnp.exp(scores - stud_max), axis=1, keepdims=True)
        wanted = as_column(positives_ref[pl.ds(number, 1), :]) - base_ref[0]
        teacher = teacher_logits(mentor_ref[at, :], wanted)
        teach_max = jnp.max(teacher, axis=1, keepdims=True)
        teach_exp = jnp.exp(teacher - teach_max)
        teach_sum = jnp.sum(teach_exp, axis=1, keepdims=True)
        cross_sum = jnp.sum(teach_exp * (teacher - scores), axis=1, keepdims=True)
        lane = lax.broadcasted_iota(jnp.int32, (BLOCK, BLOCK), 1)
        packed = jnp.zeros((BLOCK, BLOCK), jnp.float32)
        for k, column in enumerate((stud_max, stud_sum, teach_max, teach_sum, cross_sum)):
            packed = jnp.where(lane == k, column, packed)
        rows = packed.T
        stud_max, stud_sum = rows[0:1, :], rows[1:2, :]
        teach_max, teach_sum, cross_sum = rows[2:3, :], rows[3:4, :], rows[4:5, :]
        sent = (stud_max, stud_sum, teach_max + jnp.log(teach_sum), cross_sum / teach_sum)
        for k, row in enumerate(sent):
            sent_ref[:, pl.ds(8 * k + number, 1), :] = jnp.broadcast_to(
                row[None], (sent_ref.shape[0], 1, BLOCK)
            )


def local_stats(base, queries, queue, mentor, positives, copies):
    rows, width = queries.shape
    keys = queue.shape[0]
    return pl.pallas_call(
        stats_kernel,
        grid=(rows // TILE,),
        in_specs=[
            pl.BlockSpec(memory_space=pltpu.SMEM),
            pl.BlockSpec((TILE, width), lambda i: (i, 0)),
            pl.BlockSpec((keys, width), lambda i: (0, 0)),
            pl.BlockSpec((TILE, keys), lambda i: (i, 0)),
            pl.BlockSpec((8, BLOCK), lambda i: (0, 0)),
        ],
        out_specs=[
            pl.BlockSpec((TILE, keys), lambda i: (i, 0)),
            pl.BlockSpec((copies, 32, BLOCK), lambda i: (0, 0, 0)),
        ],
        out_shape=[
            jax.ShapeDtypeStruct((rows, keys), jnp.float32),
            jax.ShapeDtypeStruct((copies, 32, BLOCK), jnp.float32),
        ],
        compiler_params=pltpu.CompilerParams(vmem_limit_bytes=LIMIT),
        name="local_stats",
    )(base, queries, queue, mentor, positives)


def merge(pieces):
    tops, totals, logs, means = (pieces[:, 8 * k : 8 * k + 8] for k in range(4))
    stud_top = tops.max(0)
    stud_total = (totals * jnp.exp(tops - stud_top)).sum(0)
    teach_top = logs.max(0)
    factor = jnp.exp(logs - teach_top)
    total = factor.sum(0)
    return stud_top, stud_total, teach_top + jnp.log(total), (factor * means).sum(0) / total


def merge_kernel(pieces_ref, out_ref):
    for k, value in enumerate(merge(pieces_ref[...])):
        out_ref[:, 8 * k : 8 * k + 8, :] = jnp.broadcast_to(
            value[None], (out_ref.shape[0], 8, BLOCK)
        )


def logs_kernel(pieces_ref, logs_ref, total_ref):
    stud_top, stud_total, teach_log, cross = merge(pieces_ref[...])
    stud_log = stud_top + jnp.log(stud_total)
    logs_ref[0:8, :] = stud_log
    logs_ref[8:16, :] = teach_log
    total = jnp.sum(cross - teach_log + stud_log)
    total_ref[...] = jnp.broadcast_to(total, total_ref.shape)


def share_kernel(count, numbers_ref, base_ref, logs_ref, positives_ref, *refs):
    scores, mentor = refs[:count], refs[count : 2 * count]
    queue_ref, outs, weights_ref = refs[2 * count], refs[2 * count + 1 : -1], refs[-1]

    @pl.when(pl.program_id(0) == 0)
    def _():
        for k in range(count):
            number = numbers_ref[k]
            stud_log = as_column(logs_ref[pl.ds(number, 1), :])
            teach_log = as_column(logs_ref[pl.ds(8 + number, 1), :])
            wanted = as_column(positives_ref[pl.ds(number, 1), :]) - base_ref[0]
            weights = jnp.exp(scores[k][...] - stud_log) - jnp.exp(
                teacher_logits(mentor[k][...], wanted) - teach_log
            )
            weights_ref[k * BLOCK : (k + 1) * BLOCK, :] = weights.astype(jnp.bfloat16)

    out = jnp.dot(weights_ref[...], queue_ref[...], preferred_element_type=jnp.float32)
    for k in range(count):
        outs[k][...] = out[k * BLOCK : (k + 1) * BLOCK, :]


def shares(numbers, base, logs, positives, scores, mentor, queue):
    count = numbers.shape[0]
    keys, width = queue.shape
    part = 512

    def rows(k):
        return pl.BlockSpec((BLOCK, keys), lambda i, numbers, base: (numbers[k], 0))

    return pl.pallas_call(
        functools.partial(share_kernel, count),
        grid_spec=pltpu.PrefetchScalarGridSpec(
            num_scalar_prefetch=2,
            grid=(width // part,),
            in_specs=[
                pl.BlockSpec((16, BLOCK), lambda i, numbers, base: (0, 0)),
                pl.BlockSpec((8, BLOCK), lambda i, numbers, base: (0, 0)),
                *(rows(k) for k in range(count)),
                *(rows(k) for k in range(count)),
                pl.BlockSpec((keys, part), lambda i, numbers, base: (0, i)),
            ],
            out_specs=[pl.BlockSpec((BLOCK, part), lambda i, numbers, base: (0, i))] * count,
            scratch_shapes=[pltpu.VMEM((count * BLOCK, keys), jnp.bfloat16)],
        ),
        out_shape=[jax.ShapeDtypeStruct((BLOCK, width), jnp.float32)] * count,
        compiler_params=pltpu.CompilerParams(vmem_limit_bytes=SHARE_LIMIT),
        cost_estimate=pl.CostEstimate(flops=0, bytes_accessed=0, transcendentals=0),
        name="shares",
    )(numbers, base, logs, positives, *[scores] * count, *[mentor] * count, queue)


def split_kernel(me_ref, a, b, c, d, own_ref, *outs):
    rows = own_ref.shape[0]
    for k, out in zip((0, *ORDER), (own_ref, *outs)):
        at = pl.ds(pl.multiple_of((me_ref[0] ^ k) * rows, rows), rows)
        out[...] = (a[at, :] + b[at, :]) + (c[at, :] + d[at, :])


def split_sum(me, parts):
    rows, width = parts[0].shape
    whole = pl.BlockSpec(memory_space=pltpu.VMEM)
    return pl.pallas_call(
        split_kernel,
        in_specs=[pl.BlockSpec(memory_space=pltpu.SMEM), *[whole] * 4],
        out_specs=[whole] * 4,
        out_shape=[jax.ShapeDtypeStruct((rows // 4, width), jnp.float32)] * 4,
        compiler_params=pltpu.CompilerParams(vmem_limit_bytes=SMALL_LIMIT),
        name="split_sum",
    )(me, *parts)


def columns_kernel(*refs):
    out = refs[-1]
    rows = refs[0].shape[0]
    for half in range(2):
        a, b, c, d = (ref[...] for ref in refs[4 * half : 4 * half + 4])
        total = (a + b) + (c + d)
        for k in range(out.shape[0]):
            out[k, half * rows : (half + 1) * rows, :] = total[:, k * BLOCK : (k + 1) * BLOCK]


def column_blocks(first, second):
    rows, width = first[0].shape
    whole = pl.BlockSpec(memory_space=pltpu.VMEM)
    return pl.pallas_call(
        columns_kernel,
        in_specs=[whole] * 8,
        out_specs=whole,
        out_shape=jax.ShapeDtypeStruct((width // BLOCK, 2 * rows, BLOCK), jnp.float32),
        compiler_params=pltpu.CompilerParams(vmem_limit_bytes=SMALL_LIMIT),
        name="column_blocks",
    )(*first, *second)


def total_kernel(pieces_ref, out_ref):
    total = pieces_ref[...].sum(0)
    out_ref[...] = jnp.broadcast_to(total[None], out_ref.shape)


def rows_kernel(blocks_ref, first_ref, second_ref):
    rows = first_ref.shape[0]
    for k in range(blocks_ref.shape[0]):
        at = slice(k * BLOCK, (k + 1) * BLOCK)
        first_ref[:, at] = blocks_ref[k, :rows, :]
        second_ref[:, at] = blocks_ref[k, rows:, :]


def assemble_kernel(x_ref, y_ref, *refs):
    out, sem = refs[-2], refs[-1]
    rows = refs[0].shape[0]
    part = rows // 4
    copies = []
    for half, (outer, inner) in enumerate(((x_ref[0], y_ref[0]), (y_ref[0], x_ref[0]))):
        for i, k in enumerate((0, *ORDER)):
            for j, m in enumerate((0, *ORDER)):
                at = 4 * rows * half + (outer ^ k) * rows + (inner ^ m) * part
                copies.append(
                    pltpu.make_async_copy(
                        refs[4 * half + i].at[j * part : (j + 1) * part, :],
                        out.at[pl.ds(pl.multiple_of(at, part), part), :],
                        sem.at[len(copies)],
                    )
                )
    for copy in copies:
        copy.start()
    for copy in copies:
        copy.wait()


def assembled(x, y, first, second):
    rows, width = first[0].shape
    return pl.pallas_call(
        assemble_kernel,
        in_specs=[pl.BlockSpec(memory_space=pltpu.SMEM)] * 2
        + [pl.BlockSpec(memory_space=pl.ANY)] * 8,
        out_specs=pl.BlockSpec(memory_space=pl.ANY),
        out_shape=jax.ShapeDtypeStruct((8 * rows, width), jnp.float32),
        scratch_shapes=[pltpu.SemaphoreType.DMA((32,))],
        compiler_params=pltpu.CompilerParams(vmem_limit_bytes=SMALL_LIMIT),
        name="assembled",
    )(x, y, *first, *second)


def received(part, axis):
    return [exchanged(part, axis, k) for k in ORDER]


def local(queries, queue, mentor_logit_grid, positives):
    row_count = queries.shape[0]
    key_count = queue.shape[0]
    whole = pl.BlockSpec(memory_space=pltpu.VMEM)
    x, y = (lax.axis_index(axis).astype(jnp.int32) for axis in (X, Y))
    base = (lax.axis_index(QUEUE) * key_count).astype(jnp.int32).reshape(1)
    positives = positives.reshape(8, BLOCK)
    scores, sent = local_stats(base, queries, queue, mentor_logit_grid, positives, 16)
    pieces = lax.all_to_all(sent, (X, Y), 0, 0)
    sent = pl.pallas_call(
        merge_kernel,
        out_shape=jax.ShapeDtypeStruct((8, 32, BLOCK), jnp.float32),
        name="merge_plane",
    )(pieces)
    pieces = lax.all_to_all(sent, Z, 0, 0)
    logs, divergence = pl.pallas_call(
        logs_kernel,
        out_shape=[
            jax.ShapeDtypeStruct((16, BLOCK), jnp.float32),
            jax.ShapeDtypeStruct((8, BLOCK), jnp.float32),
        ],
        name="merge_all",
    )(pieces)

    def share(partners):
        numbers = jnp.stack([n for k in partners for n in (x ^ k, 4 + (y ^ k))])
        return shares(numbers, base, logs, positives, scores, mentor_logit_grid, queue)

    early = share(ORDER[:1])
    late = share((*ORDER[1:], 0))
    sent = [*early, *late]
    first = [sent[6]] + [exchanged(sent[2 * i], X, k) for i, k in enumerate(ORDER)]
    second = [sent[7]] + [exchanged(sent[2 * i + 1], Y, k) for i, k in enumerate(ORDER)]
    first = split_sum(y.reshape(1), first)
    second = split_sum(x.reshape(1), second)
    first = [first[0]] + [exchanged(p, Y, k) for p, k in zip(first[1:], ORDER)]
    second = [second[0]] + [exchanged(p, X, k) for p, k in zip(second[1:], ORDER)]
    blocks = column_blocks(first, second)
    pieces = lax.all_to_all(blocks, Z, 0, 0)
    total = pl.pallas_call(
        total_kernel,
        out_shape=jax.ShapeDtypeStruct(pieces.shape, jnp.float32),
        name="total",
    )(pieces)
    blocks = lax.all_to_all(total, Z, 0, 0)
    rows, width = blocks.shape[1] // 2, queries.shape[1]
    first, second = pl.pallas_call(
        rows_kernel,
        out_shape=[jax.ShapeDtypeStruct((rows, width), jnp.float32)] * 2,
        name="row_blocks",
    )(blocks)
    first = jnp.concatenate([first, *received(first, Y)], 0)
    second = jnp.concatenate([second, *received(second, X)], 0)
    first = [first, *received(first, X)]
    second = [second, *received(second, Y)]
    query_grad = assembled(x.reshape(1), y.reshape(1), first, second)
    divergence = divergence[0, 0]
    loss_total = divergence + lax.ppermute(divergence, "batch", [(0, 1), (1, 0)])
    loss_value = loss_total / (row_count * lax.axis_size("batch"))
    return (query_grad, loss_value)


def solution(mesh):
    finer = Mesh(
        mesh.devices.reshape(mesh.shape["batch"], 4, 4, 8),
        ("batch", X, Y, Z),
    )
    return jax.shard_map(
        local,
        mesh=finer,
        in_specs=(P("batch", None), P(QUEUE, None), P("batch", QUEUE), P("batch")),
        out_specs=(P("batch", None), P()),
        check_vma=False,
    )
```

time: 329 us -> 219 us (0.67)
  waiting for transfers between devices: 228 us -> 57 us
  Pallas kernels: 0 us -> 66.5 us
  starting transfers between devices: 0.04 us -> 40.3 us
  matrix products: 13.8 us -> 0 us
  between operations: 15.9 us -> 3.14 us
  blocking collectives: 55.4 us -> 43.9 us
  other arithmetic: 7.03 us -> 0.67 us
    psum x1 -> x0, waiting for transfers between devices: 228 us -> none  [local(): query_grad = lax.psum(partial_value, QUEUE)]
    pallas_call x0 -> x11, Pallas kernels: none -> 66.5 us  [the longest x1 33.2 us: assembled(): pl.pallas_call(assemble_kernel, in_specs=[pl.BlockSpec(memory_space=pltpu...]
    all_gather x3 -> x0, blocking collectives: 53 us -> none  [collected_together(): both, at, found = (lax.all_gather(jnp.concatenate(lines), axis), 0, {})]
    ppermute x0 -> x25, waiting for transfers between devices: none -> 48.6 us  [the longest x24 48.6 us: exchanged(): return lax.ppermute(part, axis, [(i, i ^ k) for i in range(n)])]
    all_to_all x0 -> x3, blocking collectives: none -> 43.9 us  [the longest x1 15 us: local(): pieces = lax.all_to_all(blocks, Z, 0, 0)]
    ppermute x0 -> x25, starting transfers between devices: none -> 31.8 us  [the longest x24 31.8 us: exchanged(): return lax.ppermute(part, axis, [(i, i ^ k) for i in range(n)])]
    dot_general x2 -> x0, matrix products: 13.8 us -> none  [the longest x1 8.49 us: local(): partial_value = jnp.dot(weights, queue, preferred_element_type=jnp.float32)]
    all_to_all x0 -> x1, starting transfers between devices: none -> 8.46 us  [local(): pieces = lax.all_to_all(sent, Z, 0, 0)]
  transfers between devices with their start and end apart: 1 -> 26, of which waited for: 1 -> 17; matrix products, arithmetic and copies ran while one was open for 1% -> 2% of each run, Pallas kernels for 0% -> 5%
where the time goes in v2:
time: 219 us; the launch traced here: 218 us
  Pallas kernels  66.5 us (30%)
  waiting for transfers between devices  57 us (26%)
  blocking collectives  43.9 us (20%)
  starting transfers between devices  40.3 us (18%)
  local copies, waits for them, and re-layouts  6.5 us (3%)
  between operations  3.14 us (1%)
    ppermute x24, waiting for transfers between devices, exchanged(): return lax.ppermute(part, axis, [(i, i ^ k) for i in range(n)])  48.6 us
    pallas_call x1, Pallas kernels, assembled(): pl.pallas_call(assemble_kernel, in_specs=[pl.BlockSpec(memory_space=pltpu...  33.2 us
    ppermute x24, starting transfers between devices, exchanged(): return lax.ppermute(part, axis, [(i, i ^ k) for i in range(n)])  31.8 us
    pallas_call x2, Pallas kernels, shares(): pl.pallas_call(functools.partial(share_kernel, count), grid_spec=pltpu.Pr...  16.1 us
    all_to_all x1, blocking collectives, local(): pieces = lax.all_to_all(blocks, Z, 0, 0)  15 us
    all_to_all x1, blocking collectives, local(): blocks = lax.all_to_all(total, Z, 0, 0)  14.5 us
    all_to_all x1, blocking collectives, local(): pieces = lax.all_to_all(sent, (X, Y), 0, 0)  14.4 us
    pallas_call x1, Pallas kernels, local_stats(): pl.pallas_call(stats_kernel, grid=(rows // TILE,), in_specs=[pl.BlockSpec...  10.3 us
  transfers between devices with their start and end apart: 26, of which 17 were waited for; matrix products, arithmetic and copies ran while one was open for 2% of the time, Pallas kernels for 5%

profile of v2, /device:TPU:2, one launch (start us, length us, event | category | flops | bytes accessed | tf_op | source)
XLA Modules:
  0.0 218.0 jit_solution(5525570516359960298)
XLA Ops:
  0.6 10.3 %local_stats.1 = (f32[1024,1536]{1,0:T(8,128)}, f32[16,32,128]{2,1,0:T(8,128)}) custom-call(s32[1]{0:T(128)} %bitcast.7.base_ref, bf16[1024,1024]{1,0:T(8,128)(2,1)} %queries_ref.1, bf16[1536,1024]{1,0:T(8,128)(2,1)} %refs_4_.1, bf16[1024,1536]{1,0:T(8,128)(2,1)} %refs_3_.1, s32[8,128]{1,0:T(8,128)} %bitcast.12), custom_call_target="tpu_custom_call" | custom-call | tf_op jit(solution)/shard_map/local_stats/pallas_call | solution.py:81
  11.0 14.4 %all_to_all.20.pieces_ref = f32[16,32,128]{2,1,0:T(8,128)} all-to-all(f32[16,32,128]{2,1,0:T(8,128)} %get-tuple-element.24), channel_id=1, replica_groups=mesh['batch'=2,'queue_0'=4,'queue_1'=4,'queue_2'=8] {'queue_0','queue_1'}, dimensions={0} | all-to-all | bytes 524288 | tf_op jit(solution)/shard_map/all_to_all | solution.py:285
  25.4 1.7 merge_plane.1
  27.0 8.5 %all-to-all-start.1 = ((f32[8,32,128]{2,1,0:T(8,128)}), f32[8,32,128]{2,1,0:T(8,128)S(1)}, u32[]{:S(2)}, u32[]{:S(2)}) async-start(f32[8,32,128]{2,1,0:T(8,128)} %merge_plane.1), calls=%async_computation.1 | async-start | bytes 262144 | tf_op jit(solution)/shard_map/all_to_all | solution.py:291
  35.5 0.7 pad_add_fusion.numbers_ref
  36.2 8.4 %all-to-all-done.1.pieces_ref = f32[8,32,128]{2,1,0:T(8,128)S(1)} async-done(((f32[8,32,128]{2,1,0:T(8,128)}), f32[8,32,128]{2,1,0:T(8,128)S(1)}, u32[]{:S(2)}, u32[]{:S(2)}) %all-to-all-start.1) | async-done | bytes 131104 | tf_op jit(solution)/shard_map/all_to_all | solution.py:291
  44.6 0.7 copy-done.2
  45.2 1.6 merge_all.1
  46.9 5.6 %shares.3 = (f32[128,1024]{1,0:T(8,128)}, f32[128,1024]{1,0:T(8,128)}) custom-call(s32[2]{0:T(128)} %pad_add_fusion.numbers_ref, s32[1]{0:T(128)} %bitcast.7.base_ref, f32[16,128]{1,0:T(8,128)} %get-tuple-element.25.logs_ref, s32[8,128]{1,0:T(8,128)} %bitcast.13, f32[1024,1536]{1,0:T(8,128)} %get-tuple-element.26.refs_0_.refs_1_.refs_2_.refs_3_.refs_4_.refs_5_, ...), custom_call_target="tpu_custom_call" | custom-call | tf_op jit(solution)/shard_map/shares/pallas_call | solution.py:159
  52.5 1.6 collective-permute-start
  54.1 0.6 stack.33.numbers_ref
  54.7 10.4 %shares.2 = (f32[128,1024]{1,0:T(8,128)}, f32[128,1024]{1,0:T(8,128)}, f32[128,1024]{1,0:T(8,128)}, f32[128,1024]{1,0:T(8,128)}, f32[128,1024]{1,0:T(8,128)}, /*index=5*/f32[128,1024]{1,0:T(8,128)}) custom-call(s32[6]{0:T(128)} %stack.33.numbers_ref, s32[1]{0:T(128)} %bitcast.7.base_ref, f32[16,128]{1,0:T(8,128)} %get-tuple-element.25.logs_ref, ...), custom_call_target="tpu_custom_call" | custom-call | tf_op jit(solution)/shard_map/shares/pallas_call | solution.py:159
  65.2 1.5 collective-permute-start.1
  66.7 1.0 collective-permute-start.2
  67.7 1.7 collective-permute-start.6
  69.4 0.2 collective-permute-start.7
  69.6 2.2 %collective-permute-start.8 = (f32[128,1024]{1,0:T(8,128)}, f32[128,1024]{1,0:T(8,128)S(1)}, u32[]{:S(2)}, u32[]{:S(2)}) collective-permute-start(f32[128,1024]{1,0:T(8,128)} %get-tuple-element.38), channel_id=1, source_target_pairs={{0,24},{8,16},{16,8},{24,0},{1,25},{9,17},{17,9},{25,1},{2,26},{10... | collective-permute-start | bytes 1572872 | tf_op jit(solution)/shard_map/ppermute | solution.py:21
  71.8 4.6 %collective-permute-done.1.c = f32[128,1024]{1,0:T(8,128)S(1)} collective-permute-done((f32[128,1024]{1,0:T(8,128)}, f32[128,1024]{1,0:T(8,128)S(1)}, u32[]{:S(2)}, u32[]{:S(2)}) %collective-permute-start.1) | collective-permute-done | bytes 524320 | tf_op jit(solution)/shard_map/ppermute | solution.py:21
  76.4 1.0 collective-permute-done.2.d
  77.4 1.0 copy-done.1
  78.5 0.1 split_sum.2
  78.6 1.7 collective-permute-start.3
  80.3 0.2 collective-permute-start.4
  80.5 3.5 %collective-permute-done.6.b = f32[128,1024]{1,0:T(8,128)S(1)} collective-permute-done((f32[128,1024]{1,0:T(8,128)S(1)}, f32[128,1024]{1,0:T(8,128)S(1)}, u32[]{:S(2)}, u32[]{:S(2)}) %collective-permute-start.6) | collective-permute-done | bytes 524320 | tf_op jit(solution)/shard_map/ppermute | solution.py:21
  84.1 1.0 collective-permute-start.5
  85.1 6.9 %collective-permute-done.7.c = f32[128,1024]{1,0:T(8,128)S(1)} collective-permute-done((f32[128,1024]{1,0:T(8,128)}, f32[128,1024]{1,0:T(8,128)S(1)}, u32[]{:S(2)}, u32[]{:S(2)}) %collective-permute-start.7) | collective-permute-done | bytes 524320 | tf_op jit(solution)/shard_map/ppermute | solution.py:21
  92.0 0.2 collective-permute-done.8.d
  92.2 1.0 copy-done
  93.2 0.1 split_sum.3
  93.3 1.9 collective-permute-start.9
  95.2 1.3 collective-permute-start.10
  96.5 1.0 collective-permute-start.11
  97.5 3.8 %collective-permute-done.9.refs_5_ = f32[32,1024]{1,0:T(8,128)S(1)} collective-permute-done((f32[32,1024]{1,0:T(8,128)S(1)}, f32[32,1024]{1,0:T(8,128)S(1)}, u32[]{:S(2)}, u32[]{:S(2)}) %collective-permute-start.9) | collective-permute-done | bytes 131104 | tf_op jit(solution)/shard_map/ppermute | solution.py:21
  101.3 1.3 collective-permute-done.10.refs_6_
  102.6 0.4 collective-permute-done.11.refs_7_
  103.1 0.1 column_blocks.1
  103.1 15.0 %all_to_all.21.pieces_ref = f32[8,64,128]{2,1,0:T(8,128)} all-to-all(f32[8,64,128]{2,1,0:T(8,128)S(1)} %column_blocks.1), channel_id=1, replica_groups=mesh['batch'=2,'queue_0'=4,'queue_1'=4,'queue_2'=8] {'queue_2'}, dimensions={0} | all-to-all | bytes 524288 | tf_op jit(solution)/shard_map/all_to_all | solution.py:315
  118.1 1.7 total.1
  119.8 14.5 %all_to_all.22.blocks_ref = f32[8,64,128]{2,1,0:T(8,128)} all-to-all(f32[8,64,128]{2,1,0:T(8,128)} %total.1), channel_id=1, replica_groups=mesh['batch'=2,'queue_0'=4,'queue_1'=4,'queue_2'=8] {'queue_2'}, dimensions={0} | all-to-all | bytes 524288 | tf_op jit(solution)/shard_map/all_to_all | solution.py:321
  134.3 1.7 row_blocks.1
  136.0 1.5 collective-permute-start.18
  137.5 1.5 collective-permute-start.20
  139.0 1.6 collective-permute-start.19
  140.7 0.9 constant_dynamic-update-slice_fusion.7
  141.6 1.1 collective-permute-done.18
  142.8 1.4 collective-permute-done.19
  144.2 0.1 collective-permute-start.23
  144.3 1.4 collective-permute-start.12
  145.8 1.2 slice.3
  147.0 2.3 %collective-permute-start.14 = (f32[32,1024]{1,0:T(8,128)}, f32[32,1024]{1,0:T(8,128)S(1)}, u32[]{:S(2)}, u32[]{:S(2)}) collective-permute-start(f32[32,1024]{1,0:T(8,128)} %get-tuple-element.43), channel_id=1, source_target_pairs={{0,24},{8,16},{16,8},{24,0},{1,25},{9,17},{17,9},{25,1},{2,26},{10... | collective-permute-start | bytes 393224 | tf_op jit(solution)/shard_map/ppermute | solution.py:21
  149.2 0.4 collective-permute-start.13
  149.6 0.9 constant_dynamic-update-slice_fusion.3
  150.6 0.6 collective-permute-done.12
  151.2 1.1 collective-permute-start.22
  152.3 3.5 %collective-permute-done.13 = f32[32,1024]{1,0:T(8,128)S(1)} collective-permute-done((f32[32,1024]{1,0:T(8,128)}, f32[32,1024]{1,0:T(8,128)S(1)}, u32[]{:S(2)}, u32[]{:S(2)}) %collective-permute-start.13) | collective-permute-done | bytes 131104 | tf_op jit(solution)/shard_map/ppermute | solution.py:21
  155.8 2.4 %collective-permute-start.21 = (f32[128,1024]{1,0:T(8,128)S(1)}, f32[128,1024]{1,0:T(8,128)S(1)}, u32[]{:S(2)}, u32[]{:S(2)}) collective-permute-start(f32[128,1024]{1,0:T(8,128)S(1)} %constant_dynamic-update-slice_fusion.4.refs_4_), channel_id=1, source_target_pairs={{0,16},{8,24},{16,0},{24,8},{1,17},{9,25},{17,1},{25,9},{2,18},{10... | collective-permute-start | bytes 1572872 | tf_op jit(solution)/shard_map/ppermute | solution.py:21
  158.2 2.2 %collective-permute-done.14 = f32[32,1024]{1,0:T(8,128)S(1)} collective-permute-done((f32[32,1024]{1,0:T(8,128)}, f32[32,1024]{1,0:T(8,128)S(1)}, u32[]{:S(2)}, u32[]{:S(2)}) %collective-permute-start.14) | collective-permute-done | bytes 131104 | tf_op jit(solution)/shard_map/ppermute | solution.py:21
  160.5 1.4 collective-permute-start.17
  161.8 2.0 collective-permute-start.16
  163.8 0.7 collective-permute-start.15
  165.8 1.3 collective-permute-done.22.refs_6_
  167.0 11.3 %collective-permute-done.21.refs_5_ = f32[128,1024]{1,0:T(8,128)S(1)} collective-permute-done((f32[128,1024]{1,0:T(8,128)S(1)}, f32[128,1024]{1,0:T(8,128)S(1)}, u32[]{:S(2)}, u32[]{:S(2)}) %collective-permute-start.21) | collective-permute-done | bytes 524320 | tf_op jit(solution)/shard_map/ppermute | solution.py:21
  178.3 5.4 %collective-permute-done.15.refs_1_ = f32[128,1024]{1,0:T(8,128)} collective-permute-done((f32[128,1024]{1,0:T(8,128)S(1)}, f32[128,1024]{1,0:T(8,128)}, u32[]{:S(2)}, u32[]{:S(2)}) %collective-permute-start.15) | collective-permute-done | bytes 524320 | tf_op jit(solution)/shard_map/ppermute | solution.py:21
  183.7 33.2 %assembled.1 = f32[1024,1024]{1,0:T(8,128)} custom-call(s32[1]{0:T(128)} %bitcast.me_ref.x_ref, s32[1]{0:T(128)} %bitcast.1.me_ref.y_ref, f32[128,1024]{1,0:T(8,128)S(1)} %constant_dynamic-update-slice_fusion.refs_0_, f32[128,1024]{1,0:T(8,128)} %collective-permute-done.15.refs_1_, f32[128,1024]{1,0:T(8,128)} %collective-permute-done.16.refs_2_, ...), custom_call_target="tpu_custom_call" | custom-call | tf_op jit(solution)/shard_map/assembled/pallas_call | solution.py:261
  (21 shorter events, 0.1 us)
Async XLA Ops:
  27.0 17.5 %all-to-all-start.1 = ((f32[8,32,128]{2,1,0:T(8,128)}), f32[8,32,128]{2,1,0:T(8,128)S(1)}, u32[]{:S(2)}, u32[]{:S(2)}) async-start(f32[8,32,128]{2,1,0:T(8,128)} %merge_plane.1), calls=%async_computation.1 | async-start | bytes 262144 | tf_op jit(solution)/shard_map/all_to_all | solution.py:291
  44.6 0.7 copy-start.2
  52.5 17.1 %collective-permute-start = (f32[128,1024]{1,0:T(8,128)}, f32[128,1024]{1,0:T(8,128)S(1)}, u32[]{:S(2)}, u32[]{:S(2)}) collective-permute-start(f32[128,1024]{1,0:T(8,128)} %get-tuple-element.28), channel_id=1, source_target_pairs={{0,64},{32,96},{64,0},{96,32},{1,65},{33,97},{65,1},{97,33},{2,66}... | collective-permute-start | bytes 1572872 | tf_op jit(solution)/shard_map/ppermute | solution.py:21
  54.7 13.0 %copy-start.3 = (f32[128,1024]{1,0:T(8,128)S(1)}, f32[128,1024]{1,0:T(8,128)}, u32[]{:S(2)}) copy-start(f32[128,1024]{1,0:T(8,128)} %get-tuple-element.36) | copy-start | bytes 1572868
  65.2 11.2 %collective-permute-start.1 = (f32[128,1024]{1,0:T(8,128)}, f32[128,1024]{1,0:T(8,128)S(1)}, u32[]{:S(2)}, u32[]{:S(2)}) collective-permute-start(f32[128,1024]{1,0:T(8,128)} %get-tuple-element.29), channel_id=1, source_target_pairs={{0,32},{32,0},{64,96},{96,64},{1,33},{33,1},{65,97},{97,65},{2,34}... | collective-permute-start | bytes 1572872 | tf_op jit(solution)/shard_map/ppermute | solution.py:21
  66.7 10.7 %collective-permute-start.2 = (f32[128,1024]{1,0:T(8,128)}, f32[128,1024]{1,0:T(8,128)S(1)}, u32[]{:S(2)}, u32[]{:S(2)}) collective-permute-start(f32[128,1024]{1,0:T(8,128)} %get-tuple-element.30), channel_id=1, source_target_pairs={{0,96},{32,64},{64,32},{96,0},{1,97},{33,65},{65,33},{97,1},{2,98}... | collective-permute-start | bytes 1572872 | tf_op jit(solution)/shard_map/ppermute | solution.py:21
  67.7 16.4 %collective-permute-start.6 = (f32[128,1024]{1,0:T(8,128)S(1)}, f32[128,1024]{1,0:T(8,128)S(1)}, u32[]{:S(2)}, u32[]{:S(2)}) collective-permute-start(f32[128,1024]{1,0:T(8,128)S(1)} %copy-done.3), channel_id=1, source_target_pairs={{0,16},{8,24},{16,0},{24,8},{1,17},{9,25},{17,1},{25,9},{2,18},{10... | collective-permute-start | bytes 1572872 | tf_op jit(solution)/shard_map/ppermute | solution.py:21
  69.4 22.6 %collective-permute-start.7 = (f32[128,1024]{1,0:T(8,128)}, f32[128,1024]{1,0:T(8,128)S(1)}, u32[]{:S(2)}, u32[]{:S(2)}) collective-permute-start(f32[128,1024]{1,0:T(8,128)} %get-tuple-element.37), channel_id=1, source_target_pairs={{0,8},{8,0},{16,24},{24,16},{1,9},{9,1},{17,25},{25,17},{2,10},{10... | collective-permute-start | bytes 1572872 | tf_op jit(solution)/shard_map/ppermute | solution.py:21
  69.6 22.6 %collective-permute-start.8 = (f32[128,1024]{1,0:T(8,128)}, f32[128,1024]{1,0:T(8,128)S(1)}, u32[]{:S(2)}, u32[]{:S(2)}) collective-permute-start(f32[128,1024]{1,0:T(8,128)} %get-tuple-element.38), channel_id=1, source_target_pairs={{0,24},{8,16},{16,8},{24,0},{1,25},{9,17},{17,9},{25,1},{2,26},{10... | collective-permute-start | bytes 1572872 | tf_op jit(solution)/shard_map/ppermute | solution.py:21
  77.4 1.0 copy-start.1
  78.6 17.9 %collective-permute-start.3 = (f32[32,1024]{1,0:T(8,128)S(1)}, f32[32,1024]{1,0:T(8,128)S(1)}, u32[]{:S(2)}, u32[]{:S(2)}) collective-permute-start(f32[32,1024]{1,0:T(8,128)S(1)} %get-tuple-element.32), channel_id=1, source_target_pairs={{0,16},{8,24},{16,0},{24,8},{1,17},{9,25},{17,1},{25,9},{2,18},{10... | collective-permute-start | bytes 393224 | tf_op jit(solution)/shard_map/ppermute | solution.py:21
  80.3 17.2 %collective-permute-start.4 = (f32[32,1024]{1,0:T(8,128)S(1)}, f32[32,1024]{1,0:T(8,128)S(1)}, u32[]{:S(2)}, u32[]{:S(2)}) collective-permute-start(f32[32,1024]{1,0:T(8,128)S(1)} %get-tuple-element.33), channel_id=1, source_target_pairs={{0,8},{8,0},{16,24},{24,16},{1,9},{9,1},{17,25},{25,17},{2,10},{10... | collective-permute-start | bytes 393224 | tf_op jit(solution)/shard_map/ppermute | solution.py:21
  84.1 13.4 %collective-permute-start.5 = (f32[32,1024]{1,0:T(8,128)S(1)}, f32[32,1024]{1,0:T(8,128)S(1)}, u32[]{:S(2)}, u32[]{:S(2)}) collective-permute-start(f32[32,1024]{1,0:T(8,128)S(1)} %get-tuple-element.34), channel_id=1, source_target_pairs={{0,24},{8,16},{16,8},{24,0},{1,25},{9,17},{17,9},{25,1},{2,26},{10... | collective-permute-start | bytes 393224 | tf_op jit(solution)/shard_map/ppermute | solution.py:21
  92.2 1.0 copy-start
  93.3 8.0 %collective-permute-start.9 = (f32[32,1024]{1,0:T(8,128)S(1)}, f32[32,1024]{1,0:T(8,128)S(1)}, u32[]{:S(2)}, u32[]{:S(2)}) collective-permute-start(f32[32,1024]{1,0:T(8,128)S(1)} %get-tuple-element.40), channel_id=1, source_target_pairs={{0,64},{32,96},{64,0},{96,32},{1,65},{33,97},{65,1},{97,33},{2,66}... | collective-permute-start | bytes 393224 | tf_op jit(solution)/shard_map/ppermute | solution.py:21
  95.2 7.4 %collective-permute-start.10 = (f32[32,1024]{1,0:T(8,128)S(1)}, f32[32,1024]{1,0:T(8,128)S(1)}, u32[]{:S(2)}, u32[]{:S(2)}) collective-permute-start(f32[32,1024]{1,0:T(8,128)S(1)} %get-tuple-element.41), channel_id=1, source_target_pairs={{0,32},{32,0},{64,96},{96,64},{1,33},{33,1},{65,97},{97,65},{2,34}... | collective-permute-start | bytes 393224 | tf_op jit(solution)/shard_map/ppermute | solution.py:21
  96.5 6.5 %collective-permute-start.11 = (f32[32,1024]{1,0:T(8,128)S(1)}, f32[32,1024]{1,0:T(8,128)S(1)}, u32[]{:S(2)}, u32[]{:S(2)}) collective-permute-start(f32[32,1024]{1,0:T(8,128)S(1)} %get-tuple-element.42), channel_id=1, source_target_pairs={{0,96},{32,64},{64,32},{96,0},{1,97},{33,65},{65,33},{97,1},{2,98}... | collective-permute-start | bytes 393224 | tf_op jit(solution)/shard_map/ppermute | solution.py:21
  136.0 6.8 %collective-permute-start.18 = (f32[32,1024]{1,0:T(8,128)}, f32[32,1024]{1,0:T(8,128)S(1)}, u32[]{:S(2)}, u32[]{:S(2)}) collective-permute-start(f32[32,1024]{1,0:T(8,128)} %get-tuple-element.44), channel_id=1, source_target_pairs={{0,64},{32,96},{64,0},{96,32},{1,65},{33,97},{65,1},{97,33},{2,66}... | collective-permute-start | bytes 393224 | tf_op jit(solution)/shard_map/ppermute | solution.py:21
  137.5 6.7 %collective-permute-start.20 = (f32[32,1024]{1,0:T(8,128)}, f32[32,1024]{1,0:T(8,128)S(1)}, u32[]{:S(2)}, u32[]{:S(2)}) collective-permute-start(f32[32,1024]{1,0:T(8,128)} %get-tuple-element.44), channel_id=1, source_target_pairs={{0,96},{32,64},{64,32},{96,0},{1,97},{33,65},{65,33},{97,1},{2,98}... | collective-permute-start | bytes 393224 | tf_op jit(solution)/shard_map/ppermute | solution.py:21
  139.0 5.2 %collective-permute-start.19 = (f32[32,1024]{1,0:T(8,128)}, f32[32,1024]{1,0:T(8,128)S(1)}, u32[]{:S(2)}, u32[]{:S(2)}) collective-permute-start(f32[32,1024]{1,0:T(8,128)} %get-tuple-element.44), channel_id=1, source_target_pairs={{0,32},{32,0},{64,96},{96,64},{1,33},{33,1},{65,97},{97,65},{2,34}... | collective-permute-start | bytes 393224 | tf_op jit(solution)/shard_map/ppermute | solution.py:21
  144.2 19.6 %collective-permute-start.23 = (f32[128,1024]{1,0:T(8,128)S(1)}, f32[128,1024]{1,0:T(8,128)S(1)}, u32[]{:S(2)}, u32[]{:S(2)}) collective-permute-start(f32[128,1024]{1,0:T(8,128)S(1)} %constant_dynamic-update-slice_fusion.4.refs_4_), channel_id=1, source_target_pairs={{0,24},{8,16},{16,8},{24,0},{1,25},{9,17},{17,9},{25,1},{2,26},{10... | collective-permute-start | bytes 1572872 | tf_op jit(solution)/shard_map/ppermute | solution.py:21
  144.3 6.9 %collective-permute-start.12 = (f32[32,1024]{1,0:T(8,128)}, f32[32,1024]{1,0:T(8,128)S(1)}, u32[]{:S(2)}, u32[]{:S(2)}) collective-permute-start(f32[32,1024]{1,0:T(8,128)} %get-tuple-element.43), channel_id=1, source_target_pairs={{0,16},{8,24},{16,0},{24,8},{1,17},{9,25},{17,1},{25,9},{2,18},{10... | collective-permute-start | bytes 393224 | tf_op jit(solution)/shard_map/ppermute | solution.py:21
  147.0 14.9 %collective-permute-start.24 = (f32[]{:T(128)}, f32[]{:T(128)}, u32[]{:S(2)}, u32[]{:S(2)}) collective-permute-start(f32[]{:T(128)} %bitcast.11), channel_id=1, source_target_pairs={{0,128},{128,0},{1,129},{129,1},{2,130},{130,2},{3,131},{131,3},{4... | collective-permute-start | bytes 20 | tf_op jit(solution)/shard_map/ppermute | solution.py:334
  147.0 13.5 %collective-permute-start.14 = (f32[32,1024]{1,0:T(8,128)}, f32[32,1024]{1,0:T(8,128)S(1)}, u32[]{:S(2)}, u32[]{:S(2)}) collective-permute-start(f32[32,1024]{1,0:T(8,128)} %get-tuple-element.43), channel_id=1, source_target_pairs={{0,24},{8,16},{16,8},{24,0},{1,25},{9,17},{17,9},{25,1},{2,26},{10... | collective-permute-start | bytes 393224 | tf_op jit(solution)/shard_map/ppermute | solution.py:21
  149.2 6.5 %collective-permute-start.13 = (f32[32,1024]{1,0:T(8,128)}, f32[32,1024]{1,0:T(8,128)S(1)}, u32[]{:S(2)}, u32[]{:S(2)}) collective-permute-start(f32[32,1024]{1,0:T(8,128)} %get-tuple-element.43), channel_id=1, source_target_pairs={{0,8},{8,0},{16,24},{24,16},{1,9},{9,1},{17,25},{25,17},{2,10},{10... | collective-permute-start | bytes 393224 | tf_op jit(solution)/shard_map/ppermute | solution.py:21
  151.2 15.8 %collective-permute-start.22 = (f32[128,1024]{1,0:T(8,128)S(1)}, f32[128,1024]{1,0:T(8,128)S(1)}, u32[]{:S(2)}, u32[]{:S(2)}) collective-permute-start(f32[128,1024]{1,0:T(8,128)S(1)} %constant_dynamic-update-slice_fusion.4.refs_4_), channel_id=1, source_target_pairs={{0,8},{8,0},{16,24},{24,16},{1,9},{9,1},{17,25},{25,17},{2,10},{10... | collective-permute-start | bytes 1572872 | tf_op jit(solution)/shard_map/ppermute | solution.py:21
  155.8 22.5 %collective-permute-start.21 = (f32[128,1024]{1,0:T(8,128)S(1)}, f32[128,1024]{1,0:T(8,128)S(1)}, u32[]{:S(2)}, u32[]{:S(2)}) collective-permute-start(f32[128,1024]{1,0:T(8,128)S(1)} %constant_dynamic-update-slice_fusion.4.refs_4_), channel_id=1, source_target_pairs={{0,16},{8,24},{16,0},{24,8},{1,17},{9,25},{17,1},{25,9},{2,18},{10... | collective-permute-start | bytes 1572872 | tf_op jit(solution)/shard_map/ppermute | solution.py:21
  160.5 17.8 %collective-permute-start.17 = (f32[128,1024]{1,0:T(8,128)S(1)}, f32[128,1024]{1,0:T(8,128)S(1)}, u32[]{:S(2)}, u32[]{:S(2)}) collective-permute-start(f32[128,1024]{1,0:T(8,128)S(1)} %constant_dynamic-update-slice_fusion.refs_0_), channel_id=1, source_target_pairs={{0,96},{32,64},{64,32},{96,0},{1,97},{33,65},{65,33},{97,1},{2,98}... | collective-permute-start | bytes 1572872 | tf_op jit(solution)/shard_map/ppermute | solution.py:21
  161.8 16.5 %collective-permute-start.16 = (f32[128,1024]{1,0:T(8,128)S(1)}, f32[128,1024]{1,0:T(8,128)}, u32[]{:S(2)}, u32[]{:S(2)}) collective-permute-start(f32[128,1024]{1,0:T(8,128)S(1)} %constant_dynamic-update-slice_fusion.refs_0_), channel_id=1, source_target_pairs={{0,32},{32,0},{64,96},{96,64},{1,33},{33,1},{65,97},{97,65},{2,34}... | collective-permute-start | bytes 1572872 | tf_op jit(solution)/shard_map/ppermute | solution.py:21
  163.8 19.8 %collective-permute-start.15 = (f32[128,1024]{1,0:T(8,128)S(1)}, f32[128,1024]{1,0:T(8,128)}, u32[]{:S(2)}, u32[]{:S(2)}) collective-permute-start(f32[128,1024]{1,0:T(8,128)S(1)} %constant_dynamic-update-slice_fusion.refs_0_), channel_id=1, source_target_pairs={{0,64},{32,96},{64,0},{96,32},{1,65},{33,97},{65,1},{97,33},{2,66}... | collective-permute-start | bytes 1572872 | tf_op jit(solution)/shard_map/ppermute | solution.py:21

commit v3 on v2

v3 whole, which is shorter than its diff:
```python
import functools
import math

import jax
import jax.numpy as jnp
from jax import lax
from jax.experimental import pallas as pl
from jax.experimental.pallas import tpu as pltpu
from jax.sharding import Mesh
from jax.sharding import PartitionSpec as P

X, Y, Z = "queue_0", "queue_1", "queue_2"
QUEUE = (X, Y, Z)

score_factor = 3.0
reward_value = 12.0


def exchanged(part, axis, k):
    n = lax.axis_size(axis)
    return lax.ppermute(part, axis, [(i, i ^ k) for i in range(n)])


SHARE_LIMIT = 49 * 1024 * 1024
SMALL_LIMIT = 8 * 1024 * 1024

BLOCK = 128
PART = 32
TILE = 512
LIMIT = 60 * 1024 * 1024
ORDER = (2, 1, 3)
WHOLE = pl.BlockSpec(memory_space=pltpu.VMEM)


def as_column(row):
    return jnp.broadcast_to(row, (BLOCK, BLOCK)).T[:, :1]


def teacher_logits(mentor, wanted):
    column = lax.broadcasted_iota(jnp.int32, mentor.shape, 1)
    return mentor.astype(jnp.float32) + jnp.where(column == wanted, reward_value, 0.0)


def stats_kernel(
    base_ref, queries_ref, queue_ref, mentor_ref, positives_ref, logits_ref, sent_ref
):
    step = pl.program_id(0)
    scale = score_factor / math.sqrt(queries_ref.shape[1])
    tile = scale * lax.dot_general(
        queries_ref[...], queue_ref[...], (((1,), (1,)), ((), ())),
        preferred_element_type=jnp.float32,
    )
    logits_ref[0] = tile
    for part in range(TILE // BLOCK):
        at = slice(part * BLOCK, (part + 1) * BLOCK)
        number = step * (TILE // BLOCK) + part
        scores = tile[at, :]
        stud_max = jnp.max(scores, axis=1, keepdims=True)
        stud_sum = jnp.sum(jnp.exp(scores - stud_max), axis=1, keepdims=True)
        wanted = as_column(positives_ref[pl.ds(number, 1), :]) - base_ref[0]
        teacher = teacher_logits(mentor_ref[at, :], wanted)
        logits_ref[1, at, :] = teacher
        teach_max = jnp.max(teacher, axis=1, keepdims=True)
        teach_exp = jnp.exp(teacher - teach_max)
        teach_sum = jnp.sum(teach_exp, axis=1, keepdims=True)
        cross_sum = jnp.sum(teach_exp * (teacher - scores), axis=1, keepdims=True)
        lane = lax.broadcasted_iota(jnp.int32, (BLOCK, BLOCK), 1)
        packed = jnp.zeros((BLOCK, BLOCK), jnp.float32)
        for k, column in enumerate((stud_max, stud_sum, teach_max, teach_sum, cross_sum)):
            packed = jnp.where(lane == k, column, packed)
        rows = packed.T
        stud_max, stud_sum = rows[0:1, :], rows[1:2, :]
        teach_max, teach_sum, cross_sum = rows[2:3, :], rows[3:4, :], rows[4:5, :]
        sent = (stud_max, stud_sum, teach_max + jnp.log(teach_sum), cross_sum / teach_sum)
        for k, row in enumerate(sent):
            sent_ref[:, pl.ds(8 * k + number, 1), :] = jnp.broadcast_to(
                row[None], (sent_ref.shape[0], 1, BLOCK)
            )


def local_stats(base, queries, queue, mentor, positives, copies):
    rows, width = queries.shape
    keys = queue.shape[0]
    return pl.pallas_call(
        stats_kernel,
        grid=(rows // TILE,),
        in_specs=[
            pl.BlockSpec(memory_space=pltpu.SMEM),
            pl.BlockSpec((TILE, width), lambda i: (i, 0)),
            pl.BlockSpec((keys, width), lambda i: (0, 0)),
            pl.BlockSpec((TILE, keys), lambda i: (i, 0)),
            pl.BlockSpec((8, BLOCK), lambda i: (0, 0)),
        ],
        out_specs=[
            pl.BlockSpec((2, TILE, keys), lambda i: (0, i, 0)),
            pl.BlockSpec((copies, 32, BLOCK), lambda i: (0, 0, 0)),
        ],
        out_shape=[
            jax.ShapeDtypeStruct((2, rows, keys), jnp.float32),
            jax.ShapeDtypeStruct((copies, 32, BLOCK), jnp.float32),
        ],
        compiler_params=pltpu.CompilerParams(vmem_limit_bytes=LIMIT),
        name="local_stats",
    )(base, queries, queue, mentor, positives)


def merge(pieces):
    tops, totals, logs, means = (pieces[:, 8 * k : 8 * k + 8] for k in range(4))
    stud_top = tops.max(0)
    stud_total = (totals * jnp.exp(tops - stud_top)).sum(0)
    teach_top = logs.max(0)
    factor = jnp.exp(logs - teach_top)
    total = factor.sum(0)
    return stud_top, stud_total, teach_top + jnp.log(total), (factor * means).sum(0) / total


def merge_kernel(pieces_ref, out_ref):
    for k, value in enumerate(merge(pieces_ref[...])):
        out_ref[:, 8 * k : 8 * k + 8, :] = jnp.broadcast_to(
            value[None], (out_ref.shape[0], 8, BLOCK)
        )


def logs_kernel(pieces_ref, logs_ref, total_ref):
    stud_top, stud_total, teach_log, cross = merge(pieces_ref[...])
    stud_log = stud_top + jnp.log(stud_total)
    logs_ref[0:8, :] = stud_log
    logs_ref[8:16, :] = teach_log
    total = jnp.sum(cross - teach_log + stud_log)
    total_ref[...] = jnp.broadcast_to(total, total_ref.shape)


def share_kernel(numbers_ref, logs_ref, queue_ref, logits_hbm, *refs):
    outs, (logits_ref, weights_ref, sem) = refs[:-3], refs[-3:]
    copies = []
    for k in range(numbers_ref.shape[0]):
        at = pl.ds(pl.multiple_of(numbers_ref[k] * BLOCK, BLOCK), BLOCK)
        copies.append(
            pltpu.make_async_copy(logits_hbm.at[:, at, :], logits_ref.at[k], sem.at[k])
        )
        copies[k].start()
    for k, copy in enumerate(copies):
        number = numbers_ref[k]
        stud_log = as_column(logs_ref[pl.ds(number, 1), :])
        teach_log = as_column(logs_ref[pl.ds(8 + number, 1), :])
        copy.wait()
        weights = jnp.exp(logits_ref[k, 0] - stud_log) - jnp.exp(logits_ref[k, 1] - teach_log)
        weights_ref[k * BLOCK : (k + 1) * BLOCK, :] = weights.astype(jnp.bfloat16)
    total = jnp.dot(weights_ref[...], queue_ref[...], preferred_element_type=jnp.float32)
    rows = outs[0].shape[0]
    for k, out in enumerate(outs):
        out[...] = total[k * rows : (k + 1) * rows, :]


def shares(numbers, parts, logs, queue, logits):
    count = numbers.shape[0]
    keys, width = queue.shape
    out = jax.ShapeDtypeStruct((BLOCK // parts, width), jnp.float32)
    return pl.pallas_call(
        share_kernel,
        in_specs=[
            pl.BlockSpec(memory_space=pltpu.SMEM), WHOLE, WHOLE,
            pl.BlockSpec(memory_space=pl.ANY),
        ],
        out_specs=[WHOLE] * (count * parts),
        out_shape=[out] * (count * parts),
        scratch_shapes=[
            pltpu.VMEM((count, 2, BLOCK, keys), jnp.float32),
            pltpu.VMEM((count * BLOCK, keys), jnp.bfloat16),
            pltpu.SemaphoreType.DMA((count,)),
        ],
        compiler_params=pltpu.CompilerParams(vmem_limit_bytes=SHARE_LIMIT),
        cost_estimate=pl.CostEstimate(flops=0, bytes_accessed=0, transcendentals=0),
        name="shares",
    )(numbers, logs, queue, logits)


def relay_kernel(*refs):
    for k in range(4):
        block, half, out = refs[k], refs[4 + k], refs[8 + k]
        rows = half.shape[0]
        out[...] = block[...]
        at = slice(rows, 2 * rows) if k % 2 == 0 else slice(0, rows)
        out[at, :] = block[at, :] + half[...]


def relayed(blocks, halves):
    return pl.pallas_call(
        relay_kernel,
        in_specs=[WHOLE] * 8,
        out_specs=[WHOLE] * 4,
        out_shape=[jax.ShapeDtypeStruct(b.shape, b.dtype) for b in blocks],
        compiler_params=pltpu.CompilerParams(vmem_limit_bytes=SMALL_LIMIT),
        name="relayed",
    )(*blocks, *halves)


def split_kernel(*refs):
    places, parts, outs = refs[:2], refs[2:8], refs[8:]
    rows = outs[0].shape[0]
    for half in range(2):
        a, b, c = parts[3 * half : 3 * half + 3]
        for i, k in enumerate((0, *ORDER)):
            at = pl.ds(pl.multiple_of((places[half][0] ^ k) * rows, rows), rows)
            outs[4 * half + i][...] = a[at, :] + (b[at, :] + c[at, :])


def split_sums(places, first, second):
    rows, width = first[0].shape
    outs = pl.pallas_call(
        split_kernel,
        in_specs=[pl.BlockSpec(memory_space=pltpu.SMEM)] * 2 + [WHOLE] * 6,
        out_specs=[WHOLE] * 8,
        out_shape=[jax.ShapeDtypeStruct((rows // 4, width), jnp.float32)] * 8,
        compiler_params=pltpu.CompilerParams(vmem_limit_bytes=SMALL_LIMIT),
        name="split_sums",
    )(*places, *first, *second)
    return outs[:4], outs[4:]


def columns_kernel(*refs):
    out = refs[-1]
    rows = refs[0].shape[0]
    for half in range(2):
        a, b, c, d = (ref[...] for ref in refs[4 * half : 4 * half + 4])
        total = (a + b) + (c + d)
        for k in range(out.shape[0]):
            out[k, half * rows : (half + 1) * rows, :] = total[:, k * BLOCK : (k + 1) * BLOCK]


def column_blocks(first, second):
    rows, width = first[0].shape
    return pl.pallas_call(
        columns_kernel,
        in_specs=[WHOLE] * 8,
        out_specs=WHOLE,
        out_shape=jax.ShapeDtypeStruct((width // BLOCK, 2 * rows, BLOCK), jnp.float32),
        compiler_params=pltpu.CompilerParams(vmem_limit_bytes=SMALL_LIMIT),
        name="column_blocks",
    )(*first, *second)


def total_kernel(pieces_ref, out_ref):
    total = pieces_ref[...].sum(0)
    out_ref[...] = jnp.broadcast_to(total[None], out_ref.shape)


def rows_kernel(blocks_ref, first_ref, second_ref):
    rows = first_ref.shape[0]
    for k in range(blocks_ref.shape[0]):
        at = slice(k * BLOCK, (k + 1) * BLOCK)
        first_ref[:, at] = blocks_ref[k, :rows, :]
        second_ref[:, at] = blocks_ref[k, rows:, :]


def stack_kernel(*refs):
    rows = refs[0].shape[0]
    for half, out in enumerate(refs[8:]):
        for k in range(4):
            out[k * rows : (k + 1) * rows, :] = refs[4 * half + k][...]


def stacked(first, second):
    rows, width = first[0].shape
    return pl.pallas_call(
        stack_kernel,
        in_specs=[WHOLE] * 8,
        out_specs=[WHOLE] * 2,
        out_shape=[jax.ShapeDtypeStruct((4 * rows, width), jnp.float32)] * 2,
        compiler_params=pltpu.CompilerParams(vmem_limit_bytes=SMALL_LIMIT),
        name="stacked",
    )(*first, *second)


def halves_kernel(a, b, c, d, *outs):
    for k, ref in enumerate((a, b, c, d)):
        rows = ref.shape[0] // 2
        outs[k][...] = ref[:rows, :] if k % 2 == 0 else ref[rows:, :]


def halves(blocks):
    rows, width = blocks[0].shape
    return pl.pallas_call(
        halves_kernel,
        in_specs=[WHOLE] * 4,
        out_specs=[WHOLE] * 4,
        out_shape=[jax.ShapeDtypeStruct((rows // 2, width), jnp.float32)] * 4,
        compiler_params=pltpu.CompilerParams(vmem_limit_bytes=SMALL_LIMIT),
        name="halves",
    )(*blocks)


def assemble_kernel(kinds, x_ref, y_ref, *refs):
    out, sem = refs[-2], refs[-1]
    places = (x_ref[0], y_ref[0]), (y_ref[0], x_ref[0])
    copies = []
    for (half, k, start), ref in zip(kinds, refs):
        outer, inner = places[half]
        for j in range(ref.shape[0] // PART):
            at = 4 * BLOCK * half + (outer ^ k) * BLOCK + (inner ^ (0, *ORDER)[start + j]) * PART
            copies.append(
                pltpu.make_async_copy(
                    ref.at[j * PART : (j + 1) * PART, :],
                    out.at[pl.ds(pl.multiple_of(at, PART), PART), :],
                    sem.at[len(copies)],
                )
            )
    for copy in copies:
        copy.start()
    for copy in copies:
        copy.wait()


def assembled(kinds, pieces, earlier, x, y):
    count = sum(piece.shape[0] for piece in pieces) // PART
    kept = [] if earlier is None else [earlier]
    return pl.pallas_call(
        functools.partial(assemble_kernel, kinds),
        in_specs=[pl.BlockSpec(memory_space=pltpu.SMEM)] * 2
        + [WHOLE] * len(pieces)
        + [pl.BlockSpec(memory_space=pl.ANY)] * len(kept),
        out_specs=pl.BlockSpec(memory_space=pl.ANY),
        out_shape=jax.ShapeDtypeStruct((8 * BLOCK, pieces[0].shape[1]), jnp.float32),
        scratch_shapes=[pltpu.SemaphoreType.DMA((count,))],
        input_output_aliases={2 + len(pieces): 0} if kept else {},
        compiler_params=pltpu.CompilerParams(vmem_limit_bytes=SMALL_LIMIT),
        name="assembled",
    )(x, y, *pieces, *kept)


def received(part, axis):
    return {k: exchanged(part, axis, k) for k in reversed(ORDER)}


def local(queries, queue, mentor_logit_grid, positives):
    row_count = queries.shape[0]
    key_count = queue.shape[0]
    x, y = (lax.axis_index(axis).astype(jnp.int32) for axis in (X, Y))
    base = (lax.axis_index(QUEUE) * key_count).astype(jnp.int32).reshape(1)
    positives = positives.reshape(8, BLOCK)
    logits, sent = local_stats(base, queries, queue, mentor_logit_grid, positives, 16)
    pieces = lax.all_to_all(sent, (X, Y), 0, 0)
    sent = pl.pallas_call(
        merge_kernel,
        in_specs=[WHOLE],
        out_specs=WHOLE,
        out_shape=jax.ShapeDtypeStruct((8, 32, BLOCK), jnp.float32),
        compiler_params=pltpu.CompilerParams(vmem_limit_bytes=SMALL_LIMIT),
        name="merge_plane",
    )(pieces)
    pieces = lax.all_to_all(sent, Z, 0, 0)
    logs, divergence = pl.pallas_call(
        logs_kernel,
        in_specs=[WHOLE],
        out_specs=[WHOLE] * 2,
        out_shape=[
            jax.ShapeDtypeStruct((16, BLOCK), jnp.float32),
            jax.ShapeDtypeStruct((1, 1), jnp.float32),
        ],
        compiler_params=pltpu.CompilerParams(vmem_limit_bytes=SMALL_LIMIT),
        name="merge_all",
    )(pieces)

    def share(partners, parts=1):
        numbers = jnp.stack([n for k in partners for n in (x ^ k, 4 + (y ^ k))])
        return shares(numbers, parts, logs, queue, logits)

    far = share((2,), 2)
    ways = (X, 1), (X, 3), (Y, 1), (Y, 3)
    came = [exchanged(part, *way) for part, way in zip(far, ways)]
    one = share((1, 3))
    blocks = [one[0], one[2], one[1], one[3]]
    blocks = relayed(blocks, [came[1], came[0], came[3], came[2]])
    got = [exchanged(block, *way) for block, way in zip(blocks, ways)]
    own = share((0,))
    places = y.reshape(1), x.reshape(1)
    first, second = split_sums(places, [own[0], *got[:2]], [own[1], *got[2:]])
    first = [first[0]] + [exchanged(p, Y, k) for p, k in zip(first[1:], ORDER)]
    second = [second[0]] + [exchanged(p, X, k) for p, k in zip(second[1:], ORDER)]
    blocks = column_blocks(first, second)
    pieces = lax.all_to_all(blocks, Z, 0, 0)
    total = pl.pallas_call(
        total_kernel,
        in_specs=[WHOLE],
        out_specs=WHOLE,
        out_shape=jax.ShapeDtypeStruct(pieces.shape, jnp.float32),
        compiler_params=pltpu.CompilerParams(vmem_limit_bytes=SMALL_LIMIT),
        name="total",
    )(pieces)
    blocks = lax.all_to_all(total, Z, 0, 0)
    rows, width = blocks.shape[1] // 2, queries.shape[1]
    first, second = pl.pallas_call(
        rows_kernel,
        in_specs=[WHOLE],
        out_specs=[WHOLE] * 2,
        out_shape=[jax.ShapeDtypeStruct((rows, width), jnp.float32)] * 2,
        compiler_params=pltpu.CompilerParams(vmem_limit_bytes=SMALL_LIMIT),
        name="row_blocks",
    )(blocks)
    from_y, from_x = received(first, Y), received(second, X)
    first, second = stacked(
        [first, *(from_y[k] for k in ORDER)], [second, *(from_x[k] for k in ORDER)]
    )
    blocks = [exchanged(first, X, 1), exchanged(first, X, 3)]
    blocks += [exchanged(second, Y, 1), exchanged(second, Y, 3)]
    upper_x, lower_x, upper_y, lower_y = halves([blocks[1], blocks[0], blocks[3], blocks[2]])
    far = [exchanged(upper_x, X, 1), exchanged(lower_x, X, 3)]
    far += [exchanged(upper_y, Y, 1), exchanged(lower_y, Y, 3)]
    places = x.reshape(1), y.reshape(1)
    kinds = (0, 0, 0), (1, 0, 0), (0, 1, 0), (0, 3, 0), (1, 1, 0), (1, 3, 0)
    query_grad = assembled(kinds, [first, second, *blocks], None, *places)
    kinds = (0, 2, 0), (0, 2, 2), (1, 2, 0), (1, 2, 2)
    query_grad = assembled(kinds, far, query_grad, *places)
    divergence = divergence[0, 0]
    loss_total = divergence + lax.ppermute(divergence, "batch", [(0, 1), (1, 0)])
    loss_value = loss_total / (row_count * lax.axis_size("batch"))
    return (query_grad, loss_value)


def solution(mesh):
    finer = Mesh(
        mesh.devices.reshape(mesh.shape["batch"], 4, 4, 8),
        ("batch", X, Y, Z),
    )
    return jax.shard_map(
        local,
        mesh=finer,
        in_specs=(P("batch", None), P(QUEUE, None), P("batch", QUEUE), P("batch")),
        out_specs=(P("batch", None), P()),
        check_vma=False,
    )
```

time: 219 us -> 166 us (0.76)
  Pallas kernels: 66.5 us -> 37.6 us
  waiting for transfers between devices: 57 us -> 37.3 us
  local copies, waits for them, and re-layouts: 6.5 us -> 0.01 us
  starting transfers between devices: 40.3 us -> 45.7 us
  blocking collectives: 43.9 us -> 40.4 us
    pallas_call x10 -> x14, Pallas kernels: 56.1 us -> 25.5 us  [the longest x3 14.4 us: shares(): pl.pallas_call(share_kernel, in_specs=[pl.BlockSpec(memory_space=pltpu.SM...]
    ppermute x24 -> x28, waiting for transfers between devices: 48.6 us -> 27 us  [exchanged(): return lax.ppermute(part, axis, [(i, i ^ k) for i in range(n)])]
    ppermute x24 -> x28, starting transfers between devices: 31.8 us -> 37.3 us  [exchanged(): return lax.ppermute(part, axis, [(i, i ^ k) for i in range(n)])]
    unnamed x14 -> x4, local copies, waits for them, and re-layouts: 4.68 us -> 0.01 us
  transfers between devices with their start and end apart: 26 -> 30, of which waited for: 17 -> 17; matrix products, arithmetic and copies ran while one was open for 2% -> 0% of each run, Pallas kernels for 5% -> 7%
where the time goes in v3:
time: 166 us; the launch traced here: 165 us
  starting transfers between devices  45.7 us (28%)
  blocking collectives  40.4 us (24%)
  Pallas kernels  37.6 us (23%)
  waiting for transfers between devices  37.3 us (22%)
  between operations  3.2 us (2%)
    ppermute x28, starting transfers between devices, exchanged(): return lax.ppermute(part, axis, [(i, i ^ k) for i in range(n)])  37.3 us
    ppermute x28, waiting for transfers between devices, exchanged(): return lax.ppermute(part, axis, [(i, i ^ k) for i in range(n)])  27 us
    pallas_call x3, Pallas kernels, shares(): pl.pallas_call(share_kernel, in_specs=[pl.BlockSpec(memory_space=pltpu.SM...  14.4 us
    all_to_all x1, blocking collectives, local(): pieces = lax.all_to_all(sent, (X, Y), 0, 0)  14.3 us
    all_to_all x1, blocking collectives, local(): pieces = lax.all_to_all(blocks, Z, 0, 0)  13.2 us
    all_to_all x1, blocking collectives, local(): blocks = lax.all_to_all(total, Z, 0, 0)  12.9 us
    pallas_call x1, Pallas kernels, local_stats(): pl.pallas_call(stats_kernel, grid=(rows // TILE,), in_specs=[pl.BlockSpec...  12.2 us
    all_to_all x1, waiting for transfers between devices, local(): pieces = lax.all_to_all(sent, Z, 0, 0)  9 us
  transfers between devices with their start and end apart: 30, of which 17 were waited for; matrix products, arithmetic and copies ran while one was open for 0% of the time, Pallas kernels for 7%

profile of v3, /device:TPU:2, one launch (start us, length us, event | category | flops | bytes accessed | tf_op | source)
XLA Modules:
  0.0 164.6 jit_solution(8061091983002598285)
XLA Ops:
  0.7 12.2 %local_stats.1 = (f32[2,1024,1536]{2,1,0:T(8,128)}, f32[16,32,128]{2,1,0:T(8,128)}) custom-call(s32[1]{0:T(128)} %bitcast.3.base_ref, bf16[1024,1024]{1,0:T(8,128)(2,1)} %queries_ref.1, bf16[1536,1024]{1,0:T(8,128)(2,1)} %queue_ref.7, bf16[1024,1536]{1,0:T(8,128)(2,1)} %mentor_ref.1, s32[8,128]{1,0:T(8,128)} %bitcast.12), custom_call_target="tpu_custom_call" | custom-call | tf_op jit(solution)/shard_map/local_stats/pallas_call | solution.py:84
  12.8 14.3 %all_to_all.20.pieces_ref = f32[16,32,128]{2,1,0:T(8,128)S(1)} all-to-all(f32[16,32,128]{2,1,0:T(8,128)} %get-tuple-element.36), channel_id=1, replica_groups=mesh['batch'=2,'queue_0'=4,'queue_1'=4,'queue_2'=8] {'queue_0','queue_1'}, dimensions={0} | all-to-all | bytes 524288 | tf_op jit(solution)/shard_map/all_to_all | solution.py:342
  27.1 0.7 merge_plane.1
  27.8 8.5 %all-to-all-start.1 = ((f32[8,32,128]{2,1,0:T(8,128)}), f32[8,32,128]{2,1,0:T(8,128)S(1)}, u32[]{:S(2)}, u32[]{:S(2)}) async-start(f32[8,32,128]{2,1,0:T(8,128)} %merge_plane.1), calls=%async_computation.1 | async-start | bytes 262144 | tf_op jit(solution)/shard_map/all_to_all | solution.py:351
  36.3 0.1 pad_add_fusion.2.numbers_ref
  36.3 9.0 %all-to-all-done.1.pieces_ref = f32[8,32,128]{2,1,0:T(8,128)S(1)} async-done(((f32[8,32,128]{2,1,0:T(8,128)}), f32[8,32,128]{2,1,0:T(8,128)S(1)}, u32[]{:S(2)}, u32[]{:S(2)}) %all-to-all-start.1) | async-done | bytes 131104 | tf_op jit(solution)/shard_map/all_to_all | solution.py:351
  45.4 0.7 merge_all.1
  46.1 4.4 %shares.5 = (f32[64,1024]{1,0:T(8,128)}, f32[64,1024]{1,0:T(8,128)}, f32[64,1024]{1,0:T(8,128)}, f32[64,1024]{1,0:T(8,128)}) custom-call(s32[2]{0:T(128)S(1)} %pad_add_fusion.2.numbers_ref, f32[16,128]{1,0:T(8,128)S(1)} %get-tuple-element.37.logs_ref, bf16[1536,1024]{1,0:T(8,128)(2,1)S(1)} %copy-done, f32[2,1024,1536]{2,1,0:T(8,128)} %get-tuple-element.38.logits_hbm), custom_call_target="tpu_custom_call" | custom-call | tf_op jit(solution)/shard_map/shares/pallas_call | solution.py:159
  50.5 1.1 collective-permute-start
  51.6 1.8 %collective-permute-start.1 = (f32[64,1024]{1,0:T(8,128)}, f32[64,1024]{1,0:T(8,128)}, u32[]{:S(2)}, u32[]{:S(2)}) collective-permute-start(f32[64,1024]{1,0:T(8,128)} %get-tuple-element.45), channel_id=1, source_target_pairs={{0,32},{32,0},{64,96},{96,64},{1,33},{33,1},{65,97},{97,65},{2,34}... | collective-permute-start | bytes 786440 | tf_op jit(solution)/shard_map/ppermute | solution.py:21
  53.4 0.9 collective-permute-start.2
  54.3 0.5 collective-permute-start.3
  54.8 0.1 pad_add_fusion.1.numbers_ref
  54.9 6.6 %shares.4 = (f32[128,1024]{1,0:T(8,128)S(1)}, f32[128,1024]{1,0:T(8,128)S(1)}, f32[128,1024]{1,0:T(8,128)S(1)}, f32[128,1024]{1,0:T(8,128)S(1)}) custom-call(s32[4]{0:T(128)S(1)} %pad_add_fusion.1.numbers_ref, f32[16,128]{1,0:T(8,128)S(1)} %get-tuple-element.37.logs_ref, bf16[1536,1024]{1,0:T(8,128)(2,1)} %queue_ref.7, ...), custom_call_target="tpu_custom_call" | custom-call | tf_op jit(solution)/shard_map/shares/pallas_call | solution.py:159
  61.5 2.7 %relayed.1 = (f32[128,1024]{1,0:T(8,128)}, f32[128,1024]{1,0:T(8,128)}, f32[128,1024]{1,0:T(8,128)}, f32[128,1024]{1,0:T(8,128)}) custom-call(f32[128,1024]{1,0:T(8,128)S(1)} %get-tuple-element.40.refs_0_, f32[128,1024]{1,0:T(8,128)S(1)} %get-tuple-element.41.refs_1_, f32[128,1024]{1,0:T(8,128)S(1)} %get-tuple-element.42.refs_2_, ...), custom_call_target="tpu_custom_call" | custom-call | tf_op jit(solution)/shard_map/relayed/pallas_call | solution.py:188
  64.2 0.3 collective-permute-start.4
  64.5 1.3 collective-permute-start.5
  65.8 1.5 collective-permute-start.6
  67.4 2.3 %collective-permute-start.7 = (f32[128,1024]{1,0:T(8,128)}, f32[128,1024]{1,0:T(8,128)}, u32[]{:S(2)}, u32[]{:S(2)}) collective-permute-start(f32[128,1024]{1,0:T(8,128)} %get-tuple-element.52), channel_id=1, source_target_pairs={{0,24},{8,16},{16,8},{24,0},{1,25},{9,17},{17,9},{25,1},{2,26},{10... | collective-permute-start | bytes 1572872 | tf_op jit(solution)/shard_map/ppermute | solution.py:21
  69.7 0.1 pad_add_fusion.numbers_ref
  69.8 3.5 %shares.3 = (f32[128,1024]{1,0:T(8,128)S(1)}, f32[128,1024]{1,0:T(8,128)S(1)}) custom-call(s32[2]{0:T(128)S(1)} %pad_add_fusion.numbers_ref, f32[16,128]{1,0:T(8,128)S(1)} %get-tuple-element.37.logs_ref, bf16[1536,1024]{1,0:T(8,128)(2,1)S(1)} %copy-done.1, f32[2,1024,1536]{2,1,0:T(8,128)} %get-tuple-element.38.logits_hbm), custom_call_target="tpu_custom_call" | custom-call | tf_op jit(solution)/shard_map/shares/pallas_call | solution.py:159
  73.2 1.4 collective-permute-done.4.refs_3_
  74.6 0.0 collective-permute-done.5.refs_4_
  74.6 1.3 collective-permute-done.6.refs_6_
  76.0 2.4 %collective-permute-done.7.refs_7_ = f32[128,1024]{1,0:T(8,128)} collective-permute-done((f32[128,1024]{1,0:T(8,128)}, f32[128,1024]{1,0:T(8,128)}, u32[]{:S(2)}, u32[]{:S(2)}) %collective-permute-start.7) | collective-permute-done | bytes 524320 | tf_op jit(solution)/shard_map/ppermute | solution.py:21
  78.4 1.7 %split_sums.1 = (f32[32,1024]{1,0:T(8,128)S(1)}, f32[32,1024]{1,0:T(8,128)S(1)}, f32[32,1024]{1,0:T(8,128)S(1)}, f32[32,1024]{1,0:T(8,128)S(1)}, f32[32,1024]{1,...) custom-call(s32[1]{0:T(128)} %bitcast.1.refs_0_.y_ref, ...), custom_call_target="tpu_custom_call" | custom-call | tf_op jit(solution)/shard_map/split_sums/pallas_call | solution.py:210
  80.1 0.8 collective-permute-start.8
  80.9 2.3 %collective-permute-start.9 = (f32[32,1024]{1,0:T(8,128)S(1)}, f32[32,1024]{1,0:T(8,128)S(1)}, u32[]{:S(2)}, u32[]{:S(2)}) collective-permute-start(f32[32,1024]{1,0:T(8,128)S(1)} %get-tuple-element.55), channel_id=1, source_target_pairs={{0,8},{8,0},{16,24},{24,16},{1,9},{9,1},{17,25},{25,17},{2,10},{10... | collective-permute-start | bytes 393224 | tf_op jit(solution)/shard_map/ppermute | solution.py:21
  83.2 1.1 collective-permute-start.10
  84.3 2.2 %collective-permute-start.11 = (f32[32,1024]{1,0:T(8,128)S(1)}, f32[32,1024]{1,0:T(8,128)S(1)}, u32[]{:S(2)}, u32[]{:S(2)}) collective-permute-start(f32[32,1024]{1,0:T(8,128)S(1)} %get-tuple-element.58), channel_id=1, source_target_pairs={{0,64},{32,96},{64,0},{96,32},{1,65},{33,97},{65,1},{97,33},{2,66}... | collective-permute-start | bytes 393224 | tf_op jit(solution)/shard_map/ppermute | solution.py:21
  86.4 0.3 collective-permute-start.12
  86.7 1.6 collective-permute-start.13
  88.4 1.0 collective-permute-done.10.refs_3_
  89.4 1.4 collective-permute-done.11.refs_5_
  90.8 0.6 collective-permute-done.12.refs_6_
  91.4 0.8 collective-permute-done.13.refs_7_
  92.1 0.1 column_blocks.1
  92.2 13.2 %all_to_all.21.pieces_ref = f32[8,64,128]{2,1,0:T(8,128)S(1)} all-to-all(f32[8,64,128]{2,1,0:T(8,128)S(1)} %column_blocks.1), channel_id=1, replica_groups=mesh['batch'=2,'queue_0'=4,'queue_1'=4,'queue_2'=8] {'queue_2'}, dimensions={0} | all-to-all | bytes 524288 | tf_op jit(solution)/shard_map/all_to_all | solution.py:381
  105.5 12.9 %all_to_all.22.blocks_ref = f32[8,64,128]{2,1,0:T(8,128)S(1)} all-to-all(f32[8,64,128]{2,1,0:T(8,128)S(1)} %total.1), channel_id=1, replica_groups=mesh['batch'=2,'queue_0'=4,'queue_1'=4,'queue_2'=8] {'queue_2'}, dimensions={0} | all-to-all | bytes 524288 | tf_op jit(solution)/shard_map/all_to_all | solution.py:390
  118.4 2.3 %collective-permute-start.16 = (f32[32,1024]{1,0:T(8,128)S(1)}, f32[32,1024]{1,0:T(8,128)S(1)}, u32[]{:S(2)}, u32[]{:S(2)}) collective-permute-start(f32[32,1024]{1,0:T(8,128)S(1)} %get-tuple-element.61.refs_0_), channel_id=1, source_target_pairs={{0,24},{8,16},{16,8},{24,0},{1,25},{9,17},{17,9},{25,1},{2,26},{10... | collective-permute-start | bytes 393224 | tf_op jit(solution)/shard_map/ppermute | solution.py:21
  120.7 2.5 %collective-permute-start.14 = (f32[32,1024]{1,0:T(8,128)S(1)}, f32[32,1024]{1,0:T(8,128)S(1)}, u32[]{:S(2)}, u32[]{:S(2)}) collective-permute-start(f32[32,1024]{1,0:T(8,128)S(1)} %get-tuple-element.61.refs_0_), channel_id=1, source_target_pairs={{0,16},{8,24},{16,0},{24,8},{1,17},{9,25},{17,1},{25,9},{2,18},{10... | collective-permute-start | bytes 393224 | tf_op jit(solution)/shard_map/ppermute | solution.py:21
  123.2 1.2 collective-permute-start.19
  124.4 4.0 %collective-permute-start.18 = (f32[32,1024]{1,0:T(8,128)S(1)}, f32[32,1024]{1,0:T(8,128)S(1)}, u32[]{:S(2)}, u32[]{:S(2)}) collective-permute-start(f32[32,1024]{1,0:T(8,128)S(1)} %get-tuple-element.62.refs_4_), channel_id=1, source_target_pairs={{0,32},{32,0},{64,96},{96,64},{1,33},{33,1},{65,97},{97,65},{2,34}... | collective-permute-start | bytes 393224 | tf_op jit(solution)/shard_map/ppermute | solution.py:21
  128.4 0.5 collective-permute-start.17
  128.9 0.7 collective-permute-done.19.refs_7_
  129.6 1.9 %collective-permute-done.18.refs_6_ = f32[32,1024]{1,0:T(8,128)S(1)} collective-permute-done((f32[32,1024]{1,0:T(8,128)S(1)}, f32[32,1024]{1,0:T(8,128)S(1)}, u32[]{:S(2)}, u32[]{:S(2)}) %collective-permute-start.18) | collective-permute-done | bytes 131104 | tf_op jit(solution)/shard_map/ppermute | solution.py:21
  131.5 3.4 %collective-permute-done.17.refs_5_ = f32[32,1024]{1,0:T(8,128)S(1)} collective-permute-done((f32[32,1024]{1,0:T(8,128)S(1)}, f32[32,1024]{1,0:T(8,128)S(1)}, u32[]{:S(2)}, u32[]{:S(2)}) %collective-permute-start.17) | collective-permute-done | bytes 131104 | tf_op jit(solution)/shard_map/ppermute | solution.py:21
  134.8 0.1 stacked.1
  134.9 1.1 collective-permute-start.21
  136.0 1.0 collective-permute-start.20
  137.0 2.2 %collective-permute-start.22 = (f32[128,1024]{1,0:T(8,128)S(1)}, f32[128,1024]{1,0:T(8,128)S(1)}, u32[]{:S(2)}, u32[]{:S(2)}) collective-permute-start(f32[128,1024]{1,0:T(8,128)S(1)} %get-tuple-element.64.refs_1_), channel_id=1, source_target_pairs={{0,24},{8,16},{16,8},{24,0},{1,25},{9,17},{17,9},{25,1},{2,26},{10... | collective-permute-start | bytes 1572872 | tf_op jit(solution)/shard_map/ppermute | solution.py:21
  139.2 7.3 %collective-permute-done.21.b.refs_2_ = f32[128,1024]{1,0:T(8,128)S(1)} collective-permute-done((f32[128,1024]{1,0:T(8,128)S(1)}, f32[128,1024]{1,0:T(8,128)S(1)}, u32[]{:S(2)}, u32[]{:S(2)}) %collective-permute-start.21) | collective-permute-done | bytes 524320 | tf_op jit(solution)/shard_map/ppermute | solution.py:21
  146.5 1.5 collective-permute-done.20.a.refs_3_
  148.0 0.7 collective-permute-done.23.d.refs_4_
  148.7 1.2 collective-permute-done.22.c.refs_5_
  149.9 1.1 halves.1
  150.9 1.1 collective-permute-start.24
  152.0 1.1 collective-permute-start.25
  153.0 0.4 collective-permute-start.26
  153.4 2.0 %collective-permute-start.27 = (f32[64,1024]{1,0:T(8,128)}, f32[64,1024]{1,0:T(8,128)}, u32[]{:S(2)}, u32[]{:S(2)}) collective-permute-start(f32[64,1024]{1,0:T(8,128)} %get-tuple-element.68), channel_id=1, source_target_pairs={{0,24},{8,16},{16,8},{24,0},{1,25},{9,17},{17,9},{25,1},{2,26},{10... | collective-permute-start | bytes 786440 | tf_op jit(solution)/shard_map/ppermute | solution.py:21
  155.4 1.3 collective-permute-done.28
  158.0 1.9 %assembled.2.refs_4_ = f32[1024,1024]{1,0:T(8,128)} custom-call(s32[1]{0:T(128)} %bitcast.refs_1_.x_ref, s32[1]{0:T(128)} %bitcast.1.refs_0_.y_ref, f32[128,1024]{1,0:T(8,128)S(1)} %get-tuple-element.63.refs_0_, f32[128,1024]{1,0:T(8,128)S(1)} %get-tuple-element.64.refs_1_, f32[128,1024]{1,0:T(8,128)S(1)} %collective-permute-done.21.b.refs_2_, ...), custom_call_target="tpu_custom_call" | custom-call | tf_op jit(solution)/shard_map/assembled/pallas_call | solution.py:317
  159.9 1.4 collective-permute-done.27.refs_3_
  161.3 2.1 %assembled.3 = f32[1024,1024]{1,0:T(8,128)} custom-call(s32[1]{0:T(128)} %bitcast.refs_1_.x_ref, s32[1]{0:T(128)} %bitcast.1.refs_0_.y_ref, f32[64,1024]{1,0:T(8,128)S(1)} %collective-permute-done.24.refs_0_, f32[64,1024]{1,0:T(8,128)} %collective-permute-done.25.refs_1_, ...), custom_call_target="tpu_custom_call", output_to_operand_aliasing={{}: (6, {})} | custom-call | tf_op jit(solution)/shard_map/assembled/pallas_call | solution.py:317
  (21 shorter events, 0.1 us)
Async XLA Ops:
  0.6 45.4 %copy-start = (bf16[1536,1024]{1,0:T(8,128)(2,1)S(1)}, bf16[1536,1024]{1,0:T(8,128)(2,1)}, u32[]{:S(2)}) copy-start(bf16[1536,1024]{1,0:T(8,128)(2,1)} %queue_ref.7) | copy-start | bytes 9437188
  27.8 17.5 %all-to-all-start.1 = ((f32[8,32,128]{2,1,0:T(8,128)}), f32[8,32,128]{2,1,0:T(8,128)S(1)}, u32[]{:S(2)}, u32[]{:S(2)}) async-start(f32[8,32,128]{2,1,0:T(8,128)} %merge_plane.1), calls=%async_computation.1 | async-start | bytes 262144 | tf_op jit(solution)/shard_map/all_to_all | solution.py:351
  50.5 11.0 %collective-permute-start = (f32[64,1024]{1,0:T(8,128)}, f32[64,1024]{1,0:T(8,128)S(1)}, u32[]{:S(2)}, u32[]{:S(2)}) collective-permute-start(f32[64,1024]{1,0:T(8,128)} %get-tuple-element.44), channel_id=1, source_target_pairs={{0,96},{32,64},{64,32},{96,0},{1,97},{33,65},{65,33},{97,1},{2,98}... | collective-permute-start | bytes 786440 | tf_op jit(solution)/shard_map/ppermute | solution.py:21
  51.6 9.9 %collective-permute-start.1 = (f32[64,1024]{1,0:T(8,128)}, f32[64,1024]{1,0:T(8,128)}, u32[]{:S(2)}, u32[]{:S(2)}) collective-permute-start(f32[64,1024]{1,0:T(8,128)} %get-tuple-element.45), channel_id=1, source_target_pairs={{0,32},{32,0},{64,96},{96,64},{1,33},{33,1},{65,97},{97,65},{2,34}... | collective-permute-start | bytes 786440 | tf_op jit(solution)/shard_map/ppermute | solution.py:21
  53.4 8.1 %collective-permute-start.2 = (f32[64,1024]{1,0:T(8,128)}, f32[64,1024]{1,0:T(8,128)}, u32[]{:S(2)}, u32[]{:S(2)}) collective-permute-start(f32[64,1024]{1,0:T(8,128)} %get-tuple-element.46), channel_id=1, source_target_pairs={{0,24},{8,16},{16,8},{24,0},{1,25},{9,17},{17,9},{25,1},{2,26},{10... | collective-permute-start | bytes 786440 | tf_op jit(solution)/shard_map/ppermute | solution.py:21
  54.3 7.2 %collective-permute-start.3 = (f32[64,1024]{1,0:T(8,128)}, f32[64,1024]{1,0:T(8,128)}, u32[]{:S(2)}, u32[]{:S(2)}) collective-permute-start(f32[64,1024]{1,0:T(8,128)} %get-tuple-element.47), channel_id=1, source_target_pairs={{0,8},{8,0},{16,24},{24,16},{1,9},{9,1},{17,25},{25,17},{2,10},{10... | collective-permute-start | bytes 786440 | tf_op jit(solution)/shard_map/ppermute | solution.py:21
  61.5 8.3 %copy-start.1 = (bf16[1536,1024]{1,0:T(8,128)(2,1)S(1)}, bf16[1536,1024]{1,0:T(8,128)(2,1)}, u32[]{:S(2)}) copy-start(bf16[1536,1024]{1,0:T(8,128)(2,1)} %queue_ref.7) | copy-start | bytes 9437188
  64.2 10.4 %collective-permute-start.4 = (f32[128,1024]{1,0:T(8,128)}, f32[128,1024]{1,0:T(8,128)}, u32[]{:S(2)}, u32[]{:S(2)}) collective-permute-start(f32[128,1024]{1,0:T(8,128)} %get-tuple-element.48), channel_id=1, source_target_pairs={{0,32},{32,0},{64,96},{96,64},{1,33},{33,1},{65,97},{97,65},{2,34}... | collective-permute-start | bytes 1572872 | tf_op jit(solution)/shard_map/ppermute | solution.py:21
  64.5 10.1 %collective-permute-start.5 = (f32[128,1024]{1,0:T(8,128)}, f32[128,1024]{1,0:T(8,128)}, u32[]{:S(2)}, u32[]{:S(2)}) collective-permute-start(f32[128,1024]{1,0:T(8,128)} %get-tuple-element.49), channel_id=1, source_target_pairs={{0,96},{32,64},{64,32},{96,0},{1,97},{33,65},{65,33},{97,1},{2,98}... | collective-permute-start | bytes 1572872 | tf_op jit(solution)/shard_map/ppermute | solution.py:21
  65.8 10.1 %collective-permute-start.6 = (f32[128,1024]{1,0:T(8,128)}, f32[128,1024]{1,0:T(8,128)}, u32[]{:S(2)}, u32[]{:S(2)}) collective-permute-start(f32[128,1024]{1,0:T(8,128)} %get-tuple-element.51), channel_id=1, source_target_pairs={{0,8},{8,0},{16,24},{24,16},{1,9},{9,1},{17,25},{25,17},{2,10},{10... | collective-permute-start | bytes 1572872 | tf_op jit(solution)/shard_map/ppermute | solution.py:21
  67.4 11.0 %collective-permute-start.7 = (f32[128,1024]{1,0:T(8,128)}, f32[128,1024]{1,0:T(8,128)}, u32[]{:S(2)}, u32[]{:S(2)}) collective-permute-start(f32[128,1024]{1,0:T(8,128)} %get-tuple-element.52), channel_id=1, source_target_pairs={{0,24},{8,16},{16,8},{24,0},{1,25},{9,17},{17,9},{25,1},{2,26},{10... | collective-permute-start | bytes 1572872 | tf_op jit(solution)/shard_map/ppermute | solution.py:21
  80.1 6.6 %collective-permute-start.8 = (f32[32,1024]{1,0:T(8,128)S(1)}, f32[32,1024]{1,0:T(8,128)S(1)}, u32[]{:S(2)}, u32[]{:S(2)}) collective-permute-start(f32[32,1024]{1,0:T(8,128)S(1)} %get-tuple-element.54), channel_id=1, source_target_pairs={{0,16},{8,24},{16,0},{24,8},{1,17},{9,25},{17,1},{25,9},{2,18},{10... | collective-permute-start | bytes 393224 | tf_op jit(solution)/shard_map/ppermute | solution.py:21
  80.9 7.5 %collective-permute-start.9 = (f32[32,1024]{1,0:T(8,128)S(1)}, f32[32,1024]{1,0:T(8,128)S(1)}, u32[]{:S(2)}, u32[]{:S(2)}) collective-permute-start(f32[32,1024]{1,0:T(8,128)S(1)} %get-tuple-element.55), channel_id=1, source_target_pairs={{0,8},{8,0},{16,24},{24,16},{1,9},{9,1},{17,25},{25,17},{2,10},{10... | collective-permute-start | bytes 393224 | tf_op jit(solution)/shard_map/ppermute | solution.py:21
  83.2 6.2 %collective-permute-start.10 = (f32[32,1024]{1,0:T(8,128)S(1)}, f32[32,1024]{1,0:T(8,128)S(1)}, u32[]{:S(2)}, u32[]{:S(2)}) collective-permute-start(f32[32,1024]{1,0:T(8,128)S(1)} %get-tuple-element.56), channel_id=1, source_target_pairs={{0,24},{8,16},{16,8},{24,0},{1,25},{9,17},{17,9},{25,1},{2,26},{10... | collective-permute-start | bytes 393224 | tf_op jit(solution)/shard_map/ppermute | solution.py:21
  84.3 6.5 %collective-permute-start.11 = (f32[32,1024]{1,0:T(8,128)S(1)}, f32[32,1024]{1,0:T(8,128)S(1)}, u32[]{:S(2)}, u32[]{:S(2)}) collective-permute-start(f32[32,1024]{1,0:T(8,128)S(1)} %get-tuple-element.58), channel_id=1, source_target_pairs={{0,64},{32,96},{64,0},{96,32},{1,65},{33,97},{65,1},{97,33},{2,66}... | collective-permute-start | bytes 393224 | tf_op jit(solution)/shard_map/ppermute | solution.py:21
  86.4 5.0 %collective-permute-start.12 = (f32[32,1024]{1,0:T(8,128)S(1)}, f32[32,1024]{1,0:T(8,128)S(1)}, u32[]{:S(2)}, u32[]{:S(2)}) collective-permute-start(f32[32,1024]{1,0:T(8,128)S(1)} %get-tuple-element.59), channel_id=1, source_target_pairs={{0,32},{32,0},{64,96},{96,64},{1,33},{33,1},{65,97},{97,65},{2,34}... | collective-permute-start | bytes 393224 | tf_op jit(solution)/shard_map/ppermute | solution.py:21
  86.7 5.4 %collective-permute-start.13 = (f32[32,1024]{1,0:T(8,128)S(1)}, f32[32,1024]{1,0:T(8,128)S(1)}, u32[]{:S(2)}, u32[]{:S(2)}) collective-permute-start(f32[32,1024]{1,0:T(8,128)S(1)} %get-tuple-element.60), channel_id=1, source_target_pairs={{0,96},{32,64},{64,32},{96,0},{1,97},{33,65},{65,33},{97,1},{2,98}... | collective-permute-start | bytes 393224 | tf_op jit(solution)/shard_map/ppermute | solution.py:21
  118.4 10.0 %collective-permute-start.16 = (f32[32,1024]{1,0:T(8,128)S(1)}, f32[32,1024]{1,0:T(8,128)S(1)}, u32[]{:S(2)}, u32[]{:S(2)}) collective-permute-start(f32[32,1024]{1,0:T(8,128)S(1)} %get-tuple-element.61.refs_0_), channel_id=1, source_target_pairs={{0,24},{8,16},{16,8},{24,0},{1,25},{9,17},{17,9},{25,1},{2,26},{10... | collective-permute-start | bytes 393224 | tf_op jit(solution)/shard_map/ppermute | solution.py:21
  120.7 8.2 %collective-permute-start.15 = (f32[32,1024]{1,0:T(8,128)S(1)}, f32[32,1024]{1,0:T(8,128)S(1)}, u32[]{:S(2)}, u32[]{:S(2)}) collective-permute-start(f32[32,1024]{1,0:T(8,128)S(1)} %get-tuple-element.61.refs_0_), channel_id=1, source_target_pairs={{0,8},{8,0},{16,24},{24,16},{1,9},{9,1},{17,25},{25,17},{2,10},{10... | collective-permute-start | bytes 393224 | tf_op jit(solution)/shard_map/ppermute | solution.py:21
  120.7 8.2 %collective-permute-start.14 = (f32[32,1024]{1,0:T(8,128)S(1)}, f32[32,1024]{1,0:T(8,128)S(1)}, u32[]{:S(2)}, u32[]{:S(2)}) collective-permute-start(f32[32,1024]{1,0:T(8,128)S(1)} %get-tuple-element.61.refs_0_), channel_id=1, source_target_pairs={{0,16},{8,24},{16,0},{24,8},{1,17},{9,25},{17,1},{25,9},{2,18},{10... | collective-permute-start | bytes 393224 | tf_op jit(solution)/shard_map/ppermute | solution.py:21
  123.2 6.4 %collective-permute-start.19 = (f32[32,1024]{1,0:T(8,128)S(1)}, f32[32,1024]{1,0:T(8,128)S(1)}, u32[]{:S(2)}, u32[]{:S(2)}) collective-permute-start(f32[32,1024]{1,0:T(8,128)S(1)} %get-tuple-element.62.refs_4_), channel_id=1, source_target_pairs={{0,96},{32,64},{64,32},{96,0},{1,97},{33,65},{65,33},{97,1},{2,98}... | collective-permute-start | bytes 393224 | tf_op jit(solution)/shard_map/ppermute | solution.py:21
  124.4 7.1 %collective-permute-start.18 = (f32[32,1024]{1,0:T(8,128)S(1)}, f32[32,1024]{1,0:T(8,128)S(1)}, u32[]{:S(2)}, u32[]{:S(2)}) collective-permute-start(f32[32,1024]{1,0:T(8,128)S(1)} %get-tuple-element.62.refs_4_), channel_id=1, source_target_pairs={{0,32},{32,0},{64,96},{96,64},{1,33},{33,1},{65,97},{97,65},{2,34}... | collective-permute-start | bytes 393224 | tf_op jit(solution)/shard_map/ppermute | solution.py:21
  128.4 6.5 %collective-permute-start.17 = (f32[32,1024]{1,0:T(8,128)S(1)}, f32[32,1024]{1,0:T(8,128)S(1)}, u32[]{:S(2)}, u32[]{:S(2)}) collective-permute-start(f32[32,1024]{1,0:T(8,128)S(1)} %get-tuple-element.62.refs_4_), channel_id=1, source_target_pairs={{0,64},{32,96},{64,0},{96,32},{1,65},{33,97},{65,1},{97,33},{2,66}... | collective-permute-start | bytes 393224 | tf_op jit(solution)/shard_map/ppermute | solution.py:21
  134.9 11.6 %collective-permute-start.21 = (f32[128,1024]{1,0:T(8,128)S(1)}, f32[128,1024]{1,0:T(8,128)S(1)}, u32[]{:S(2)}, u32[]{:S(2)}) collective-permute-start(f32[128,1024]{1,0:T(8,128)S(1)} %get-tuple-element.63.refs_0_), channel_id=1, source_target_pairs={{0,32},{32,0},{64,96},{96,64},{1,33},{33,1},{65,97},{97,65},{2,34}... | collective-permute-start | bytes 1572872 | tf_op jit(solution)/shard_map/ppermute | solution.py:21
  136.0 12.0 %collective-permute-start.20 = (f32[128,1024]{1,0:T(8,128)S(1)}, f32[128,1024]{1,0:T(8,128)S(1)}, u32[]{:S(2)}, u32[]{:S(2)}) collective-permute-start(f32[128,1024]{1,0:T(8,128)S(1)} %get-tuple-element.63.refs_0_), channel_id=1, source_target_pairs={{0,96},{32,64},{64,32},{96,0},{1,97},{33,65},{65,33},{97,1},{2,98}... | collective-permute-start | bytes 1572872 | tf_op jit(solution)/shard_map/ppermute | solution.py:21
  137.0 11.7 %collective-permute-start.23 = (f32[128,1024]{1,0:T(8,128)S(1)}, f32[128,1024]{1,0:T(8,128)S(1)}, u32[]{:S(2)}, u32[]{:S(2)}) collective-permute-start(f32[128,1024]{1,0:T(8,128)S(1)} %get-tuple-element.64.refs_1_), channel_id=1, source_target_pairs={{0,8},{8,0},{16,24},{24,16},{1,9},{9,1},{17,25},{25,17},{2,10},{10... | collective-permute-start | bytes 1572872 | tf_op jit(solution)/shard_map/ppermute | solution.py:21
  137.0 12.9 %collective-permute-start.22 = (f32[128,1024]{1,0:T(8,128)S(1)}, f32[128,1024]{1,0:T(8,128)S(1)}, u32[]{:S(2)}, u32[]{:S(2)}) collective-permute-start(f32[128,1024]{1,0:T(8,128)S(1)} %get-tuple-element.64.refs_1_), channel_id=1, source_target_pairs={{0,24},{8,16},{16,8},{24,0},{1,25},{9,17},{17,9},{25,1},{2,26},{10... | collective-permute-start | bytes 1572872 | tf_op jit(solution)/shard_map/ppermute | solution.py:21
  150.9 8.9 %collective-permute-start.24 = (f32[64,1024]{1,0:T(8,128)}, f32[64,1024]{1,0:T(8,128)S(1)}, u32[]{:S(2)}, u32[]{:S(2)}) collective-permute-start(f32[64,1024]{1,0:T(8,128)} %get-tuple-element.65), channel_id=1, source_target_pairs={{0,32},{32,0},{64,96},{96,64},{1,33},{33,1},{65,97},{97,65},{2,34}... | collective-permute-start | bytes 786440 | tf_op jit(solution)/shard_map/ppermute | solution.py:21
  152.0 7.9 %collective-permute-start.25 = (f32[64,1024]{1,0:T(8,128)}, f32[64,1024]{1,0:T(8,128)}, u32[]{:S(2)}, u32[]{:S(2)}) collective-permute-start(f32[64,1024]{1,0:T(8,128)} %get-tuple-element.66), channel_id=1, source_target_pairs={{0,96},{32,64},{64,32},{96,0},{1,97},{33,65},{65,33},{97,1},{2,98}... | collective-permute-start | bytes 786440 | tf_op jit(solution)/shard_map/ppermute | solution.py:21
  153.0 6.8 %collective-permute-start.26 = (f32[64,1024]{1,0:T(8,128)}, f32[64,1024]{1,0:T(8,128)}, u32[]{:S(2)}, u32[]{:S(2)}) collective-permute-start(f32[64,1024]{1,0:T(8,128)} %get-tuple-element.67), channel_id=1, source_target_pairs={{0,8},{8,0},{16,24},{24,16},{1,9},{9,1},{17,25},{25,17},{2,10},{10... | collective-permute-start | bytes 786440 | tf_op jit(solution)/shard_map/ppermute | solution.py:21
  153.4 7.9 %collective-permute-start.27 = (f32[64,1024]{1,0:T(8,128)}, f32[64,1024]{1,0:T(8,128)}, u32[]{:S(2)}, u32[]{:S(2)}) collective-permute-start(f32[64,1024]{1,0:T(8,128)} %get-tuple-element.68), channel_id=1, source_target_pairs={{0,24},{8,16},{16,8},{24,0},{1,25},{9,17},{17,9},{25,1},{2,26},{10... | collective-permute-start | bytes 786440 | tf_op jit(solution)/shard_map/ppermute | solution.py:21
  155.4 1.3 collective-permute-start.28

commit v4 on v3

--- a/solution.py
+++ b/solution.py
@@ -30,6 +30,10 @@
 LIMIT = 60 * 1024 * 1024
 ORDER = (2, 1, 3)
 WHOLE = pl.BlockSpec(memory_space=pltpu.VMEM)
+
+
+def moved(size, flops=0):
+    return pl.CostEstimate(flops=flops, bytes_accessed=size, transcendentals=0)
 
 
 def as_column(row):
@@ -170,29 +174,29 @@
             pltpu.SemaphoreType.DMA((count,)),
         ],
         compiler_params=pltpu.CompilerParams(vmem_limit_bytes=SHARE_LIMIT),
-        cost_estimate=pl.CostEstimate(flops=0, bytes_accessed=0, transcendentals=0),
+        cost_estimate=moved(2 * keys * width + count * BLOCK * (8 * keys + 4 * width), 2 * count * BLOCK * keys * width),
         name="shares",
     )(numbers, logs, queue, logits)
 
 
-def relay_kernel(*refs):
-    for k in range(4):
-        block, half, out = refs[k], refs[4 + k], refs[8 + k]
-        rows = half.shape[0]
-        out[...] = block[...]
-        at = slice(rows, 2 * rows) if k % 2 == 0 else slice(0, rows)
-        out[at, :] = block[at, :] + half[...]
-
-
-def relayed(blocks, halves):
+def relay_kernel(a_ref, b_ref, upper_ref, lower_ref, a_out, b_out):
+    rows = upper_ref.shape[0]
+    a_out[:rows, :] = a_ref[:rows, :]
+    a_out[rows:, :] = a_ref[rows:, :] + lower_ref[...]
+    b_out[:rows, :] = b_ref[:rows, :] + upper_ref[...]
+    b_out[rows:, :] = b_ref[rows:, :]
+
+
+def relayed(a, b, upper, lower):
     return pl.pallas_call(
         relay_kernel,
-        in_specs=[WHOLE] * 8,
-        out_specs=[WHOLE] * 4,
-        out_shape=[jax.ShapeDtypeStruct(b.shape, b.dtype) for b in blocks],
-        compiler_params=pltpu.CompilerParams(vmem_limit_bytes=SMALL_LIMIT),
+        in_specs=[WHOLE] * 4,
+        out_specs=[WHOLE] * 2,
+        out_shape=[jax.ShapeDtypeStruct(a.shape, a.dtype)] * 2,
+        compiler_params=pltpu.CompilerParams(vmem_limit_bytes=SMALL_LIMIT),
+        cost_estimate=moved(20 * a.size),
         name="relayed",
-    )(*blocks, *halves)
+    )(a, b, upper, lower)
 
 
 def split_kernel(*refs):
@@ -213,6 +217,7 @@
         out_specs=[WHOLE] * 8,
         out_shape=[jax.ShapeDtypeStruct((rows // 4, width), jnp.float32)] * 8,
         compiler_params=pltpu.CompilerParams(vmem_limit_bytes=SMALL_LIMIT),
+        cost_estimate=moved(32 * first[0].size),
         name="split_sums",
     )(*places, *first, *second)
     return outs[:4], outs[4:]
@@ -236,6 +241,7 @@
         out_specs=WHOLE,
         out_shape=jax.ShapeDtypeStruct((width // BLOCK, 2 * rows, BLOCK), jnp.float32),
         compiler_params=pltpu.CompilerParams(vmem_limit_bytes=SMALL_LIMIT),
+        cost_estimate=moved(40 * first[0].size),
         name="column_blocks",
     )(*first, *second)
 
@@ -268,26 +274,28 @@
         out_specs=[WHOLE] * 2,
         out_shape=[jax.ShapeDtypeStruct((4 * rows, width), jnp.float32)] * 2,
         compiler_params=pltpu.CompilerParams(vmem_limit_bytes=SMALL_LIMIT),
+        cost_estimate=moved(64 * first[0].size),
         name="stacked",
     )(*first, *second)
 
 
-def halves_kernel(a, b, c, d, *outs):
-    for k, ref in enumerate((a, b, c, d)):
-        rows = ref.shape[0] // 2
-        outs[k][...] = ref[:rows, :] if k % 2 == 0 else ref[rows:, :]
-
-
-def halves(blocks):
-    rows, width = blocks[0].shape
+def halves_kernel(a, b, upper, lower):
+    rows = upper.shape[0]
+    upper[...] = a[:rows, :]
+    lower[...] = b[rows:, :]
+
+
+def halves(a, b):
+    rows, width = a.shape
     return pl.pallas_call(
         halves_kernel,
-        in_specs=[WHOLE] * 4,
-        out_specs=[WHOLE] * 4,
-        out_shape=[jax.ShapeDtypeStruct((rows // 2, width), jnp.float32)] * 4,
-        compiler_params=pltpu.CompilerParams(vmem_limit_bytes=SMALL_LIMIT),
+        in_specs=[WHOLE] * 2,
+        out_specs=[WHOLE] * 2,
+        out_shape=[jax.ShapeDtypeStruct((rows // 2, width), jnp.float32)] * 2,
+        compiler_params=pltpu.CompilerParams(vmem_limit_bytes=SMALL_LIMIT),
+        cost_estimate=moved(8 * a.size),
         name="halves",
-    )(*blocks)
+    )(a, b)
 
 
 def assemble_kernel(kinds, x_ref, y_ref, *refs):
@@ -361,6 +369,8 @@
         name="merge_all",
     )(pieces)
 
+    other = lax.ppermute(divergence, "batch", [(0, 1), (1, 0)])
+
     def share(partners, parts=1):
         numbers = jnp.stack([n for k in partners for n in (x ^ k, 4 + (y ^ k))])
         return shares(numbers, parts, logs, queue, logits)
@@ -368,9 +378,8 @@
     far = share((2,), 2)
     ways = (X, 1), (X, 3), (Y, 1), (Y, 3)
     came = [exchanged(part, *way) for part, way in zip(far, ways)]
-    one = share((1, 3))
-    blocks = [one[0], one[2], one[1], one[3]]
-    blocks = relayed(blocks, [came[1], came[0], came[3], came[2]])
+    near = share((1, 3))
+    blocks = [*relayed(near[0], near[2], *came[:2]), *relayed(near[1], near[3], *came[2:])]
     got = [exchanged(block, *way) for block, way in zip(blocks, ways)]
     own = share((0,))
     places = y.reshape(1), x.reshape(1)
@@ -378,6 +387,8 @@
     first = [first[0]] + [exchanged(p, Y, k) for p, k in zip(first[1:], ORDER)]
     second = [second[0]] + [exchanged(p, X, k) for p, k in zip(second[1:], ORDER)]
     blocks = column_blocks(first, second)
+    loss_value = (divergence + other) / (row_count * lax.axis_size("batch"))
+    blocks, loss_value = lax.optimization_barrier((blocks, loss_value))
     pieces = lax.all_to_all(blocks, Z, 0, 0)
     total = pl.pallas_call(
         total_kernel,
@@ -403,7 +414,8 @@
     )
     blocks = [exchanged(first, X, 1), exchanged(first, X, 3)]
     blocks += [exchanged(second, Y, 1), exchanged(second, Y, 3)]
-    upper_x, lower_x, upper_y, lower_y = halves([blocks[1], blocks[0], blocks[3], blocks[2]])
+    upper_x, lower_x = halves(blocks[1], blocks[0])
+    upper_y, lower_y = halves(blocks[3], blocks[2])
     far = [exchanged(upper_x, X, 1), exchanged(lower_x, X, 3)]
     far += [exchanged(upper_y, Y, 1), exchanged(lower_y, Y, 3)]
     places = x.reshape(1), y.reshape(1)
@@ -411,10 +423,7 @@
     query_grad = assembled(kinds, [first, second, *blocks], None, *places)
     kinds = (0, 2, 0), (0, 2, 2), (1, 2, 0), (1, 2, 2)
     query_grad = assembled(kinds, far, query_grad, *places)
-    divergence = divergence[0, 0]
-    loss_total = divergence + lax.ppermute(divergence, "batch", [(0, 1), (1, 0)])
-    loss_value = loss_total / (row_count * lax.axis_size("batch"))
-    return (query_grad, loss_value)
+    return (query_grad, loss_value.reshape(()))
 
 
 def solution(mesh):

time: 166 us -> 160 us (0.964)
  Pallas kernels: 37.6 us -> 34.1 us
    pallas_call x2 -> x4, Pallas kernels: 3.76 us -> 2.26 us  [the longest x2 2.19 us: relayed(): pl.pallas_call(relay_kernel, in_specs=[WHOLE] * 4, out_specs=[WHOLE] * 2,...]
  transfers between devices with their start and end apart: 30 -> 30, of which waited for: 17 -> 16; matrix products, arithmetic and copies ran while one was open for 0% -> 0% of each run, Pallas kernels for 7% -> 9%
where the time goes in v4:
time: 160 us; the launch traced here: 159 us
  starting transfers between devices  44.4 us (28%)
  blocking collectives  40.7 us (25%)
  waiting for transfers between devices  36.7 us (23%)
  Pallas kernels  34.1 us (21%)
  between operations  3.11 us (2%)
    ppermute x28, starting transfers between devices, exchanged(): return lax.ppermute(part, axis, [(i, i ^ k) for i in range(n)])  35.9 us
    ppermute x28, waiting for transfers between devices, exchanged(): return lax.ppermute(part, axis, [(i, i ^ k) for i in range(n)])  27.7 us
    all_to_all x1, blocking collectives, local(): pieces = lax.all_to_all(sent, (X, Y), 0, 0)  14.3 us
    pallas_call x3, Pallas kernels, shares(): pl.pallas_call(share_kernel, in_specs=[pl.BlockSpec(memory_space=pltpu.SM...  13.5 us
    all_to_all x1, blocking collectives, local(): pieces = lax.all_to_all(blocks, Z, 0, 0)  13.5 us
    all_to_all x1, blocking collectives, local(): blocks = lax.all_to_all(total, Z, 0, 0)  12.9 us
    pallas_call x1, Pallas kernels, local_stats(): pl.pallas_call(stats_kernel, grid=(rows // TILE,), in_specs=[pl.BlockSpec...  12.2 us
    all_to_all x1, waiting for transfers between devices, local(): pieces = lax.all_to_all(sent, Z, 0, 0)  9 us
  transfers between devices with their start and end apart: 30, of which 16 were waited for; matrix products, arithmetic and copies ran while one was open for 0% of the time, Pallas kernels for 9%

profile of v4, /device:TPU:2, one launch (start us, length us, event | category | flops | bytes accessed | tf_op | source)
XLA Modules:
  0.0 159.2 jit_solution(7595643152080854307)
XLA Ops:
  0.6 0.0 copy-start
  0.7 12.2 %local_stats.1 = (f32[2,1024,1536]{2,1,0:T(8,128)}, f32[16,32,128]{2,1,0:T(8,128)}) custom-call(s32[1]{0:T(128)} %bitcast.3.base_ref, bf16[1024,1024]{1,0:T(8,128)(2,1)} %queries_ref.1, bf16[1536,1024]{1,0:T(8,128)(2,1)} %queue_ref.7, bf16[1024,1536]{1,0:T(8,128)(2,1)} %mentor_ref.1, s32[8,128]{1,0:T(8,128)} %bitcast.12), custom_call_target="tpu_custom_call" | custom-call | tf_op jit(solution)/shard_map/local_stats/pallas_call | solution.py:88
  12.8 14.3 %all_to_all.20.pieces_ref = f32[16,32,128]{2,1,0:T(8,128)S(1)} all-to-all(f32[16,32,128]{2,1,0:T(8,128)} %get-tuple-element.38), channel_id=1, replica_groups=mesh['batch'=2,'queue_0'=4,'queue_1'=4,'queue_2'=8] {'queue_0','queue_1'}, dimensions={0} | all-to-all | bytes 524288 | tf_op jit(solution)/shard_map/all_to_all | solution.py:350
  27.1 0.7 merge_plane.1
  27.8 8.5 %all-to-all-start.1 = ((f32[8,32,128]{2,1,0:T(8,128)}), f32[8,32,128]{2,1,0:T(8,128)S(1)}, u32[]{:S(2)}, u32[]{:S(2)}) async-start(f32[8,32,128]{2,1,0:T(8,128)} %merge_plane.1), calls=%async_computation.1 | async-start | bytes 262144 | tf_op jit(solution)/shard_map/all_to_all | solution.py:359
  36.3 0.1 pad_add_fusion.2.numbers_ref
  36.3 9.0 %all-to-all-done.1.pieces_ref = f32[8,32,128]{2,1,0:T(8,128)S(1)} async-done(((f32[8,32,128]{2,1,0:T(8,128)}), f32[8,32,128]{2,1,0:T(8,128)S(1)}, u32[]{:S(2)}, u32[]{:S(2)}) %all-to-all-start.1) | async-done | bytes 131104 | tf_op jit(solution)/shard_map/all_to_all | solution.py:359
  45.4 0.7 merge_all.1
  46.0 3.5 %shares.5 = (f32[64,1024]{1,0:T(8,128)S(1)}, f32[64,1024]{1,0:T(8,128)S(1)}, f32[64,1024]{1,0:T(8,128)S(1)}, f32[64,1024]{1,0:T(8,128)S(1)}) custom-call(s32[2]{0:T(128)S(1)} %pad_add_fusion.2.numbers_ref, f32[16,128]{1,0:T(8,128)S(1)} %get-tuple-element.39.logs_ref, bf16[1536,1024]{1,0:T(8,128)(2,1)S(1)} %copy-done, ...), custom_call_target="tpu_custom_call" | custom-call | flops 805306368 | bytes 7340032 | tf_op jit(solution)/shard_map/shares/pallas_call | solution.py:163
  49.5 0.6 collective-permute-start.4
  50.1 1.7 %collective-permute-start.5 = (f32[64,1024]{1,0:T(8,128)S(1)}, f32[64,1024]{1,0:T(8,128)S(1)}, u32[]{:S(2)}, u32[]{:S(2)}) collective-permute-start(f32[64,1024]{1,0:T(8,128)S(1)} %get-tuple-element.52), channel_id=1, source_target_pairs={{0,24},{8,16},{16,8},{24,0},{1,25},{9,17},{17,9},{25,1},{2,26},{10... | collective-permute-start | bytes 786440 | tf_op jit(solution)/shard_map/ppermute | solution.py:21
  51.8 1.6 %collective-permute-start = (f32[64,1024]{1,0:T(8,128)S(1)}, f32[64,1024]{1,0:T(8,128)S(1)}, u32[]{:S(2)}, u32[]{:S(2)}) collective-permute-start(f32[64,1024]{1,0:T(8,128)S(1)} %get-tuple-element.44), channel_id=1, source_target_pairs={{0,32},{32,0},{64,96},{96,64},{1,33},{33,1},{65,97},{97,65},{2,34}... | collective-permute-start | bytes 786440 | tf_op jit(solution)/shard_map/ppermute | solution.py:21
  53.4 0.4 collective-permute-start.1
  53.8 0.1 pad_add_fusion.1.numbers_ref
  53.9 6.6 %shares.4 = (f32[128,1024]{1,0:T(8,128)S(1)}, f32[128,1024]{1,0:T(8,128)S(1)}, f32[128,1024]{1,0:T(8,128)S(1)}, f32[128,1024]{1,0:T(8,128)S(1)}) custom-call(s32[4]{0:T(128)S(1)} %pad_add_fusion.1.numbers_ref, f32[16,128]{1,0:T(8,128)S(1)} %get-tuple-element.39.logs_ref, bf16[1536,1024]{1,0:T(8,128)(2,1)} %queue_ref.7, ...), custom_call_target="tpu_custom_call" | custom-call | flops 1610612736 | bytes 11534336 | tf_op jit(solution)/shard_map/shares/pallas_call | solution.py:163
  60.5 1.1 relayed.3
  61.6 0.3 collective-permute-start.6
  61.9 2.4 %collective-permute-start.7 = (f32[128,1024]{1,0:T(8,128)}, f32[128,1024]{1,0:T(8,128)}, u32[]{:S(2)}, u32[]{:S(2)}) collective-permute-start(f32[128,1024]{1,0:T(8,128)} %get-tuple-element.54), channel_id=1, source_target_pairs={{0,24},{8,16},{16,8},{24,0},{1,25},{9,17},{17,9},{25,1},{2,26},{10... | collective-permute-start | bytes 1572872 | tf_op jit(solution)/shard_map/ppermute | solution.py:21
  64.3 1.1 relayed.2
  65.4 1.4 collective-permute-start.2
  66.8 1.0 collective-permute-start.3
  67.8 0.1 pad_add_fusion.numbers_ref
  67.9 3.5 %shares.3 = (f32[128,1024]{1,0:T(8,128)S(1)}, f32[128,1024]{1,0:T(8,128)S(1)}) custom-call(s32[2]{0:T(128)S(1)} %pad_add_fusion.numbers_ref, f32[16,128]{1,0:T(8,128)S(1)} %get-tuple-element.39.logs_ref, bf16[1536,1024]{1,0:T(8,128)(2,1)S(1)} %copy-done.1, f32[2,1024,1536]{2,1,0:T(8,128)} %get-tuple-element.40.logits_hbm), custom_call_target="tpu_custom_call" | custom-call | flops 805306368 | bytes 7340032 | tf_op jit(solution)/shard_map/shares/pallas_call | solution.py:163
  71.3 0.7 collective-permute-done.6.refs_6_
  72.0 1.3 collective-permute-done.7.refs_7_
  73.3 1.9 %collective-permute-done.2.refs_3_ = f32[128,1024]{1,0:T(8,128)} collective-permute-done((f32[128,1024]{1,0:T(8,128)}, f32[128,1024]{1,0:T(8,128)}, u32[]{:S(2)}, u32[]{:S(2)}) %collective-permute-start.2) | collective-permute-done | bytes 524320 | tf_op jit(solution)/shard_map/ppermute | solution.py:21
  75.2 1.1 collective-permute-done.3.refs_4_
  76.3 1.7 %split_sums.1 = (f32[32,1024]{1,0:T(8,128)S(1)}, f32[32,1024]{1,0:T(8,128)S(1)}, f32[32,1024]{1,0:T(8,128)S(1)}, f32[32,1024]{1,0:T(8,128)S(1)}, f32[32,1024]{1,...) custom-call(s32[1]{0:T(128)} %bitcast.1.refs_0_.y_ref, ...), custom_call_target="tpu_custom_call" | custom-call | bytes 4194304 | tf_op jit(solution)/shard_map/split_sums/pallas_call | solution.py:214
  78.0 1.1 collective-permute-start.10
  79.1 2.8 %collective-permute-start.11 = (f32[32,1024]{1,0:T(8,128)S(1)}, f32[32,1024]{1,0:T(8,128)S(1)}, u32[]{:S(2)}, u32[]{:S(2)}) collective-permute-start(f32[32,1024]{1,0:T(8,128)S(1)} %get-tuple-element.60), channel_id=1, source_target_pairs={{0,64},{32,96},{64,0},{96,32},{1,65},{33,97},{65,1},{97,33},{2,66}... | collective-permute-start | bytes 393224 | tf_op jit(solution)/shard_map/ppermute | solution.py:21
  81.9 0.4 collective-permute-start.12
  82.3 0.9 collective-permute-start.13
  83.2 1.4 collective-permute-start.8
  84.6 1.6 %collective-permute-start.9 = (f32[32,1024]{1,0:T(8,128)S(1)}, f32[32,1024]{1,0:T(8,128)S(1)}, u32[]{:S(2)}, u32[]{:S(2)}) collective-permute-start(f32[32,1024]{1,0:T(8,128)S(1)} %get-tuple-element.57), channel_id=1, source_target_pairs={{0,8},{8,0},{16,24},{24,16},{1,9},{9,1},{17,25},{25,17},{2,10},{10... | collective-permute-start | bytes 393224 | tf_op jit(solution)/shard_map/ppermute | solution.py:21
  87.5 1.5 collective-permute-done.12.refs_6_
  89.0 0.4 collective-permute-done.13.refs_7_
  89.3 1.8 %collective-permute-done.8.refs_1_ = f32[32,1024]{1,0:T(8,128)S(1)} collective-permute-done((f32[32,1024]{1,0:T(8,128)S(1)}, f32[32,1024]{1,0:T(8,128)S(1)}, u32[]{:S(2)}, u32[]{:S(2)}) %collective-permute-start.8) | collective-permute-done | bytes 131104 | tf_op jit(solution)/shard_map/ppermute | solution.py:21
  91.1 1.0 collective-permute-done.9.refs_2_
  92.1 0.1 column_blocks.1
  92.2 13.5 %all_to_all.21.pieces_ref = f32[8,64,128]{2,1,0:T(8,128)S(1)} all-to-all(f32[8,64,128]{2,1,0:T(8,128)S(1)} %column_blocks.1), channel_id=1, replica_groups=mesh['batch'=2,'queue_0'=4,'queue_1'=4,'queue_2'=8] {'queue_2'}, dimensions={0} | all-to-all | bytes 524288 | tf_op jit(solution)/shard_map/all_to_all | solution.py:392
  105.7 12.9 %all_to_all.22.blocks_ref = f32[8,64,128]{2,1,0:T(8,128)S(1)} all-to-all(f32[8,64,128]{2,1,0:T(8,128)S(1)} %total.1), channel_id=1, replica_groups=mesh['batch'=2,'queue_0'=4,'queue_1'=4,'queue_2'=8] {'queue_2'}, dimensions={0} | all-to-all | bytes 524288 | tf_op jit(solution)/shard_map/all_to_all | solution.py:401
  118.6 1.7 %collective-permute-start.15 = (f32[32,1024]{1,0:T(8,128)S(1)}, f32[32,1024]{1,0:T(8,128)S(1)}, u32[]{:S(2)}, u32[]{:S(2)}) collective-permute-start(f32[32,1024]{1,0:T(8,128)S(1)} %get-tuple-element.65.refs_0_), channel_id=1, source_target_pairs={{0,16},{8,24},{16,0},{24,8},{1,17},{9,25},{17,1},{25,9},{2,18},{10... | collective-permute-start | bytes 393224 | tf_op jit(solution)/shard_map/ppermute | solution.py:21
  120.3 0.3 collective-permute-start.16
  120.6 2.2 %collective-permute-start.17 = (f32[32,1024]{1,0:T(8,128)S(1)}, f32[32,1024]{1,0:T(8,128)S(1)}, u32[]{:S(2)}, u32[]{:S(2)}) collective-permute-start(f32[32,1024]{1,0:T(8,128)S(1)} %get-tuple-element.65.refs_0_), channel_id=1, source_target_pairs={{0,24},{8,16},{16,8},{24,0},{1,25},{9,17},{17,9},{25,1},{2,26},{10... | collective-permute-start | bytes 393224 | tf_op jit(solution)/shard_map/ppermute | solution.py:21
  122.8 2.8 %collective-permute-start.18 = (f32[32,1024]{1,0:T(8,128)S(1)}, f32[32,1024]{1,0:T(8,128)S(1)}, u32[]{:S(2)}, u32[]{:S(2)}) collective-permute-start(f32[32,1024]{1,0:T(8,128)S(1)} %get-tuple-element.66.refs_4_), channel_id=1, source_target_pairs={{0,64},{32,96},{64,0},{96,32},{1,65},{33,97},{65,1},{97,33},{2,66}... | collective-permute-start | bytes 393224 | tf_op jit(solution)/shard_map/ppermute | solution.py:21
  125.7 0.4 collective-permute-start.19
  126.0 0.9 collective-permute-start.20
  126.9 2.4 %collective-permute-done.18.refs_5_ = f32[32,1024]{1,0:T(8,128)S(1)} collective-permute-done((f32[32,1024]{1,0:T(8,128)S(1)}, f32[32,1024]{1,0:T(8,128)S(1)}, u32[]{:S(2)}, u32[]{:S(2)}) %collective-permute-start.18) | collective-permute-done | bytes 131104 | tf_op jit(solution)/shard_map/ppermute | solution.py:21
  129.3 1.3 collective-permute-done.19.refs_6_
  130.6 1.8 %collective-permute-done.20.refs_7_ = f32[32,1024]{1,0:T(8,128)S(1)} collective-permute-done((f32[32,1024]{1,0:T(8,128)S(1)}, f32[32,1024]{1,0:T(8,128)S(1)}, u32[]{:S(2)}, u32[]{:S(2)}) %collective-permute-start.20) | collective-permute-done | bytes 131104 | tf_op jit(solution)/shard_map/ppermute | solution.py:21
  132.4 0.1 stacked.1
  132.5 0.3 collective-permute-start.25
  132.8 0.8 collective-permute-start.21
  133.6 3.4 %collective-permute-start.22 = (f32[128,1024]{1,0:T(8,128)S(1)}, f32[128,1024]{1,0:T(8,128)S(1)}, u32[]{:S(2)}, u32[]{:S(2)}) collective-permute-start(f32[128,1024]{1,0:T(8,128)S(1)} %get-tuple-element.67.refs_0_), channel_id=1, source_target_pairs={{0,32},{32,0},{64,96},{96,64},{1,33},{33,1},{65,97},{97,65},{2,34}... | collective-permute-start | bytes 1572872 | tf_op jit(solution)/shard_map/ppermute | solution.py:21
  137.0 8.7 %collective-permute-done.25.a.refs_5_ = f32[128,1024]{1,0:T(8,128)S(1)} collective-permute-done((f32[128,1024]{1,0:T(8,128)S(1)}, f32[128,1024]{1,0:T(8,128)S(1)}, u32[]{:S(2)}, u32[]{:S(2)}) %collective-permute-start.25) | collective-permute-done | bytes 524320 | tf_op jit(solution)/shard_map/ppermute | solution.py:21
  145.8 0.1 collective-permute-start.27
  145.9 2.1 %collective-permute-start.28 = (f32[64,1024]{1,0:T(8,128)S(1)}, f32[64,1024]{1,0:T(8,128)S(1)}, u32[]{:S(2)}, u32[]{:S(2)}) collective-permute-start(f32[64,1024]{1,0:T(8,128)S(1)} %get-tuple-element.72), channel_id=1, source_target_pairs={{0,24},{8,16},{16,8},{24,0},{1,25},{9,17},{17,9},{25,1},{2,26},{10... | collective-permute-start | bytes 786440 | tf_op jit(solution)/shard_map/ppermute | solution.py:21
  148.1 2.6 %collective-permute-start.23 = (f32[64,1024]{1,0:T(8,128)S(1)}, f32[64,1024]{1,0:T(8,128)S(1)}, u32[]{:S(2)}, u32[]{:S(2)}) collective-permute-start(f32[64,1024]{1,0:T(8,128)S(1)} %get-tuple-element.68), channel_id=1, source_target_pairs={{0,32},{32,0},{64,96},{96,64},{1,33},{33,1},{65,97},{97,65},{2,34}... | collective-permute-start | bytes 786440 | tf_op jit(solution)/shard_map/ppermute | solution.py:21
  150.7 0.6 collective-permute-start.24
  151.3 1.8 %assembled.2.refs_4_ = f32[1024,1024]{1,0:T(8,128)} custom-call(s32[1]{0:T(128)} %bitcast.refs_1_.x_ref, s32[1]{0:T(128)} %bitcast.1.refs_0_.y_ref, f32[128,1024]{1,0:T(8,128)S(1)} %get-tuple-element.67.refs_0_, f32[128,1024]{1,0:T(8,128)S(1)} %get-tuple-element.70.refs_1_, f32[128,1024]{1,0:T(8,128)S(1)} %collective-permute-done.22.b.refs_2_, ...), custom_call_target="tpu_custom_call" | custom-call | tf_op jit(solution)/shard_map/assembled/pallas_call | solution.py:325
  153.1 0.4 collective-permute-done.28.refs_3_
  153.6 1.5 collective-permute-done.23.refs_0_
  155.0 2.0 %collective-permute-done.24.refs_1_ = f32[64,1024]{1,0:T(8,128)S(1)} collective-permute-done((f32[64,1024]{1,0:T(8,128)S(1)}, f32[64,1024]{1,0:T(8,128)S(1)}, u32[]{:S(2)}, u32[]{:S(2)}) %collective-permute-start.24) | collective-permute-done | bytes 262176 | tf_op jit(solution)/shard_map/ppermute | solution.py:21
  157.1 1.0 assembled.3
  (23 shorter events, 0.2 us)
Async XLA Ops:
  0.6 45.4 %copy-start = (bf16[1536,1024]{1,0:T(8,128)(2,1)S(1)}, bf16[1536,1024]{1,0:T(8,128)(2,1)}, u32[]{:S(2)}) copy-start(bf16[1536,1024]{1,0:T(8,128)(2,1)} %queue_ref.7) | copy-start | bytes 9437188
  27.8 17.5 %all-to-all-start.1 = ((f32[8,32,128]{2,1,0:T(8,128)}), f32[8,32,128]{2,1,0:T(8,128)S(1)}, u32[]{:S(2)}, u32[]{:S(2)}) async-start(f32[8,32,128]{2,1,0:T(8,128)} %merge_plane.1), calls=%async_computation.1 | async-start | bytes 262144 | tf_op jit(solution)/shard_map/all_to_all | solution.py:359
  49.5 11.0 %collective-permute-start.4 = (f32[64,1024]{1,0:T(8,128)S(1)}, f32[64,1024]{1,0:T(8,128)S(1)}, u32[]{:S(2)}, u32[]{:S(2)}) collective-permute-start(f32[64,1024]{1,0:T(8,128)S(1)} %get-tuple-element.51), channel_id=1, source_target_pairs={{0,8},{8,0},{16,24},{24,16},{1,9},{9,1},{17,25},{25,17},{2,10},{10... | collective-permute-start | bytes 786440 | tf_op jit(solution)/shard_map/ppermute | solution.py:21
  50.1 10.4 %collective-permute-start.5 = (f32[64,1024]{1,0:T(8,128)S(1)}, f32[64,1024]{1,0:T(8,128)S(1)}, u32[]{:S(2)}, u32[]{:S(2)}) collective-permute-start(f32[64,1024]{1,0:T(8,128)S(1)} %get-tuple-element.52), channel_id=1, source_target_pairs={{0,24},{8,16},{16,8},{24,0},{1,25},{9,17},{17,9},{25,1},{2,26},{10... | collective-permute-start | bytes 786440 | tf_op jit(solution)/shard_map/ppermute | solution.py:21
  51.8 12.5 %collective-permute-start = (f32[64,1024]{1,0:T(8,128)S(1)}, f32[64,1024]{1,0:T(8,128)S(1)}, u32[]{:S(2)}, u32[]{:S(2)}) collective-permute-start(f32[64,1024]{1,0:T(8,128)S(1)} %get-tuple-element.44), channel_id=1, source_target_pairs={{0,32},{32,0},{64,96},{96,64},{1,33},{33,1},{65,97},{97,65},{2,34}... | collective-permute-start | bytes 786440 | tf_op jit(solution)/shard_map/ppermute | solution.py:21
  53.4 10.9 %collective-permute-start.1 = (f32[64,1024]{1,0:T(8,128)S(1)}, f32[64,1024]{1,0:T(8,128)S(1)}, u32[]{:S(2)}, u32[]{:S(2)}) collective-permute-start(f32[64,1024]{1,0:T(8,128)S(1)} %get-tuple-element.45), channel_id=1, source_target_pairs={{0,96},{32,64},{64,32},{96,0},{1,97},{33,65},{65,33},{97,1},{2,98}... | collective-permute-start | bytes 786440 | tf_op jit(solution)/shard_map/ppermute | solution.py:21
  60.5 7.4 %copy-start.1 = (bf16[1536,1024]{1,0:T(8,128)(2,1)S(1)}, bf16[1536,1024]{1,0:T(8,128)(2,1)}, u32[]{:S(2)}) copy-start(bf16[1536,1024]{1,0:T(8,128)(2,1)} %queue_ref.7) | copy-start | bytes 9437188
  61.6 10.4 %collective-permute-start.6 = (f32[128,1024]{1,0:T(8,128)}, f32[128,1024]{1,0:T(8,128)}, u32[]{:S(2)}, u32[]{:S(2)}) collective-permute-start(f32[128,1024]{1,0:T(8,128)} %get-tuple-element.53), channel_id=1, source_target_pairs={{0,8},{8,0},{16,24},{24,16},{1,9},{9,1},{17,25},{25,17},{2,10},{10... | collective-permute-start | bytes 1572872 | tf_op jit(solution)/shard_map/ppermute | solution.py:21
  61.9 11.4 %collective-permute-start.7 = (f32[128,1024]{1,0:T(8,128)}, f32[128,1024]{1,0:T(8,128)}, u32[]{:S(2)}, u32[]{:S(2)}) collective-permute-start(f32[128,1024]{1,0:T(8,128)} %get-tuple-element.54), channel_id=1, source_target_pairs={{0,24},{8,16},{16,8},{24,0},{1,25},{9,17},{17,9},{25,1},{2,26},{10... | collective-permute-start | bytes 1572872 | tf_op jit(solution)/shard_map/ppermute | solution.py:21
  65.4 9.8 %collective-permute-start.2 = (f32[128,1024]{1,0:T(8,128)}, f32[128,1024]{1,0:T(8,128)}, u32[]{:S(2)}, u32[]{:S(2)}) collective-permute-start(f32[128,1024]{1,0:T(8,128)} %get-tuple-element.46), channel_id=1, source_target_pairs={{0,32},{32,0},{64,96},{96,64},{1,33},{33,1},{65,97},{97,65},{2,34}... | collective-permute-start | bytes 1572872 | tf_op jit(solution)/shard_map/ppermute | solution.py:21
  66.8 9.5 %collective-permute-start.3 = (f32[128,1024]{1,0:T(8,128)}, f32[128,1024]{1,0:T(8,128)}, u32[]{:S(2)}, u32[]{:S(2)}) collective-permute-start(f32[128,1024]{1,0:T(8,128)} %get-tuple-element.47), channel_id=1, source_target_pairs={{0,96},{32,64},{64,32},{96,0},{1,97},{33,65},{65,33},{97,1},{2,98}... | collective-permute-start | bytes 1572872 | tf_op jit(solution)/shard_map/ppermute | solution.py:21
  78.0 6.6 %collective-permute-start.10 = (f32[32,1024]{1,0:T(8,128)S(1)}, f32[32,1024]{1,0:T(8,128)S(1)}, u32[]{:S(2)}, u32[]{:S(2)}) collective-permute-start(f32[32,1024]{1,0:T(8,128)S(1)} %get-tuple-element.58), channel_id=1, source_target_pairs={{0,24},{8,16},{16,8},{24,0},{1,25},{9,17},{17,9},{25,1},{2,26},{10... | collective-permute-start | bytes 393224 | tf_op jit(solution)/shard_map/ppermute | solution.py:21
  79.1 4.1 %collective-permute-start.14 = (f32[1,1]{1,0:T(1,128)}, f32[1,1]{1,0:T(1,128)}, u32[]{:S(2)}, u32[]{:S(2)}) collective-permute-start(f32[1,1]{1,0:T(1,128)} %get-tuple-element.63), channel_id=1, source_target_pairs={{0,128},{128,0},{1,129},{129,1},{2,130},{130,2},{3,131},{131,3},{4... | collective-permute-start | bytes 20 | tf_op jit(solution)/shard_map/ppermute | solution.py:372
  79.1 8.4 %collective-permute-start.11 = (f32[32,1024]{1,0:T(8,128)S(1)}, f32[32,1024]{1,0:T(8,128)S(1)}, u32[]{:S(2)}, u32[]{:S(2)}) collective-permute-start(f32[32,1024]{1,0:T(8,128)S(1)} %get-tuple-element.60), channel_id=1, source_target_pairs={{0,64},{32,96},{64,0},{96,32},{1,65},{33,97},{65,1},{97,33},{2,66}... | collective-permute-start | bytes 393224 | tf_op jit(solution)/shard_map/ppermute | solution.py:21
  81.9 7.1 %collective-permute-start.12 = (f32[32,1024]{1,0:T(8,128)S(1)}, f32[32,1024]{1,0:T(8,128)S(1)}, u32[]{:S(2)}, u32[]{:S(2)}) collective-permute-start(f32[32,1024]{1,0:T(8,128)S(1)} %get-tuple-element.61), channel_id=1, source_target_pairs={{0,32},{32,0},{64,96},{96,64},{1,33},{33,1},{65,97},{97,65},{2,34}... | collective-permute-start | bytes 393224 | tf_op jit(solution)/shard_map/ppermute | solution.py:21
  82.3 7.0 %collective-permute-start.13 = (f32[32,1024]{1,0:T(8,128)S(1)}, f32[32,1024]{1,0:T(8,128)S(1)}, u32[]{:S(2)}, u32[]{:S(2)}) collective-permute-start(f32[32,1024]{1,0:T(8,128)S(1)} %get-tuple-element.62), channel_id=1, source_target_pairs={{0,96},{32,64},{64,32},{96,0},{1,97},{33,65},{65,33},{97,1},{2,98}... | collective-permute-start | bytes 393224 | tf_op jit(solution)/shard_map/ppermute | solution.py:21
  83.2 7.9 %collective-permute-start.8 = (f32[32,1024]{1,0:T(8,128)S(1)}, f32[32,1024]{1,0:T(8,128)S(1)}, u32[]{:S(2)}, u32[]{:S(2)}) collective-permute-start(f32[32,1024]{1,0:T(8,128)S(1)} %get-tuple-element.56), channel_id=1, source_target_pairs={{0,16},{8,24},{16,0},{24,8},{1,17},{9,25},{17,1},{25,9},{2,18},{10... | collective-permute-start | bytes 393224 | tf_op jit(solution)/shard_map/ppermute | solution.py:21
  84.6 7.5 %collective-permute-start.9 = (f32[32,1024]{1,0:T(8,128)S(1)}, f32[32,1024]{1,0:T(8,128)S(1)}, u32[]{:S(2)}, u32[]{:S(2)}) collective-permute-start(f32[32,1024]{1,0:T(8,128)S(1)} %get-tuple-element.57), channel_id=1, source_target_pairs={{0,8},{8,0},{16,24},{24,16},{1,9},{9,1},{17,25},{25,17},{2,10},{10... | collective-permute-start | bytes 393224 | tf_op jit(solution)/shard_map/ppermute | solution.py:21
  118.6 7.4 %collective-permute-start.15 = (f32[32,1024]{1,0:T(8,128)S(1)}, f32[32,1024]{1,0:T(8,128)S(1)}, u32[]{:S(2)}, u32[]{:S(2)}) collective-permute-start(f32[32,1024]{1,0:T(8,128)S(1)} %get-tuple-element.65.refs_0_), channel_id=1, source_target_pairs={{0,16},{8,24},{16,0},{24,8},{1,17},{9,25},{17,1},{25,9},{2,18},{10... | collective-permute-start | bytes 393224 | tf_op jit(solution)/shard_map/ppermute | solution.py:21
  120.3 6.6 %collective-permute-start.16 = (f32[32,1024]{1,0:T(8,128)S(1)}, f32[32,1024]{1,0:T(8,128)S(1)}, u32[]{:S(2)}, u32[]{:S(2)}) collective-permute-start(f32[32,1024]{1,0:T(8,128)S(1)} %get-tuple-element.65.refs_0_), channel_id=1, source_target_pairs={{0,8},{8,0},{16,24},{24,16},{1,9},{9,1},{17,25},{25,17},{2,10},{10... | collective-permute-start | bytes 393224 | tf_op jit(solution)/shard_map/ppermute | solution.py:21
  120.6 6.3 %collective-permute-start.17 = (f32[32,1024]{1,0:T(8,128)S(1)}, f32[32,1024]{1,0:T(8,128)S(1)}, u32[]{:S(2)}, u32[]{:S(2)}) collective-permute-start(f32[32,1024]{1,0:T(8,128)S(1)} %get-tuple-element.65.refs_0_), channel_id=1, source_target_pairs={{0,24},{8,16},{16,8},{24,0},{1,25},{9,17},{17,9},{25,1},{2,26},{10... | collective-permute-start | bytes 393224 | tf_op jit(solution)/shard_map/ppermute | solution.py:21
  122.8 6.5 %collective-permute-start.18 = (f32[32,1024]{1,0:T(8,128)S(1)}, f32[32,1024]{1,0:T(8,128)S(1)}, u32[]{:S(2)}, u32[]{:S(2)}) collective-permute-start(f32[32,1024]{1,0:T(8,128)S(1)} %get-tuple-element.66.refs_4_), channel_id=1, source_target_pairs={{0,64},{32,96},{64,0},{96,32},{1,65},{33,97},{65,1},{97,33},{2,66}... | collective-permute-start | bytes 393224 | tf_op jit(solution)/shard_map/ppermute | solution.py:21
  125.7 5.0 %collective-permute-start.19 = (f32[32,1024]{1,0:T(8,128)S(1)}, f32[32,1024]{1,0:T(8,128)S(1)}, u32[]{:S(2)}, u32[]{:S(2)}) collective-permute-start(f32[32,1024]{1,0:T(8,128)S(1)} %get-tuple-element.66.refs_4_), channel_id=1, source_target_pairs={{0,32},{32,0},{64,96},{96,64},{1,33},{33,1},{65,97},{97,65},{2,34}... | collective-permute-start | bytes 393224 | tf_op jit(solution)/shard_map/ppermute | solution.py:21
  126.0 6.4 %collective-permute-start.20 = (f32[32,1024]{1,0:T(8,128)S(1)}, f32[32,1024]{1,0:T(8,128)S(1)}, u32[]{:S(2)}, u32[]{:S(2)}) collective-permute-start(f32[32,1024]{1,0:T(8,128)S(1)} %get-tuple-element.66.refs_4_), channel_id=1, source_target_pairs={{0,96},{32,64},{64,32},{96,0},{1,97},{33,65},{65,33},{97,1},{2,98}... | collective-permute-start | bytes 393224 | tf_op jit(solution)/shard_map/ppermute | solution.py:21
  132.5 13.3 %collective-permute-start.25 = (f32[128,1024]{1,0:T(8,128)S(1)}, f32[128,1024]{1,0:T(8,128)S(1)}, u32[]{:S(2)}, u32[]{:S(2)}) collective-permute-start(f32[128,1024]{1,0:T(8,128)S(1)} %get-tuple-element.70.refs_1_), channel_id=1, source_target_pairs={{0,24},{8,16},{16,8},{24,0},{1,25},{9,17},{17,9},{25,1},{2,26},{10... | collective-permute-start | bytes 1572872 | tf_op jit(solution)/shard_map/ppermute | solution.py:21
  132.8 13.0 %collective-permute-start.26 = (f32[128,1024]{1,0:T(8,128)S(1)}, f32[128,1024]{1,0:T(8,128)S(1)}, u32[]{:S(2)}, u32[]{:S(2)}) collective-permute-start(f32[128,1024]{1,0:T(8,128)S(1)} %get-tuple-element.70.refs_1_), channel_id=1, source_target_pairs={{0,8},{8,0},{16,24},{24,16},{1,9},{9,1},{17,25},{25,17},{2,10},{10... | collective-permute-start | bytes 1572872 | tf_op jit(solution)/shard_map/ppermute | solution.py:21
  132.8 15.2 %collective-permute-start.21 = (f32[128,1024]{1,0:T(8,128)S(1)}, f32[128,1024]{1,0:T(8,128)S(1)}, u32[]{:S(2)}, u32[]{:S(2)}) collective-permute-start(f32[128,1024]{1,0:T(8,128)S(1)} %get-tuple-element.67.refs_0_), channel_id=1, source_target_pairs={{0,96},{32,64},{64,32},{96,0},{1,97},{33,65},{65,33},{97,1},{2,98}... | collective-permute-start | bytes 1572872 | tf_op jit(solution)/shard_map/ppermute | solution.py:21
  133.6 14.4 %collective-permute-start.22 = (f32[128,1024]{1,0:T(8,128)S(1)}, f32[128,1024]{1,0:T(8,128)S(1)}, u32[]{:S(2)}, u32[]{:S(2)}) collective-permute-start(f32[128,1024]{1,0:T(8,128)S(1)} %get-tuple-element.67.refs_0_), channel_id=1, source_target_pairs={{0,32},{32,0},{64,96},{96,64},{1,33},{33,1},{65,97},{97,65},{2,34}... | collective-permute-start | bytes 1572872 | tf_op jit(solution)/shard_map/ppermute | solution.py:21
  145.8 7.3 %collective-permute-start.27 = (f32[64,1024]{1,0:T(8,128)S(1)}, f32[64,1024]{1,0:T(8,128)S(1)}, u32[]{:S(2)}, u32[]{:S(2)}) collective-permute-start(f32[64,1024]{1,0:T(8,128)S(1)} %get-tuple-element.71), channel_id=1, source_target_pairs={{0,8},{8,0},{16,24},{24,16},{1,9},{9,1},{17,25},{25,17},{2,10},{10... | collective-permute-start | bytes 786440 | tf_op jit(solution)/shard_map/ppermute | solution.py:21
  145.9 7.7 %collective-permute-start.28 = (f32[64,1024]{1,0:T(8,128)S(1)}, f32[64,1024]{1,0:T(8,128)S(1)}, u32[]{:S(2)}, u32[]{:S(2)}) collective-permute-start(f32[64,1024]{1,0:T(8,128)S(1)} %get-tuple-element.72), channel_id=1, source_target_pairs={{0,24},{8,16},{16,8},{24,0},{1,25},{9,17},{17,9},{25,1},{2,26},{10... | collective-permute-start | bytes 786440 | tf_op jit(solution)/shard_map/ppermute | solution.py:21
  148.1 7.0 %collective-permute-start.23 = (f32[64,1024]{1,0:T(8,128)S(1)}, f32[64,1024]{1,0:T(8,128)S(1)}, u32[]{:S(2)}, u32[]{:S(2)}) collective-permute-start(f32[64,1024]{1,0:T(8,128)S(1)} %get-tuple-element.68), channel_id=1, source_target_pairs={{0,32},{32,0},{64,96},{96,64},{1,33},{33,1},{65,97},{97,65},{2,34}... | collective-permute-start | bytes 786440 | tf_op jit(solution)/shard_map/ppermute | solution.py:21
  150.7 6.4 %collective-permute-start.24 = (f32[64,1024]{1,0:T(8,128)S(1)}, f32[64,1024]{1,0:T(8,128)S(1)}, u32[]{:S(2)}, u32[]{:S(2)}) collective-permute-start(f32[64,1024]{1,0:T(8,128)S(1)} %get-tuple-element.69), channel_id=1, source_target_pairs={{0,96},{32,64},{64,32},{96,0},{1,97},{33,65},{65,33},{97,1},{2,98}... | collective-permute-start | bytes 786440 | tf_op jit(solution)/shard_map/ppermute | solution.py:21

commit v5 on v4

--- a/solution.py
+++ b/solution.py
@@ -382,13 +382,13 @@
     blocks = [*relayed(near[0], near[2], *came[:2]), *relayed(near[1], near[3], *came[2:])]
     got = [exchanged(block, *way) for block, way in zip(blocks, ways)]
     own = share((0,))
+    loss_value = (divergence + other) / (row_count * lax.axis_size("batch"))
+    own, loss_value = lax.optimization_barrier((own, loss_value))
     places = y.reshape(1), x.reshape(1)
     first, second = split_sums(places, [own[0], *got[:2]], [own[1], *got[2:]])
     first = [first[0]] + [exchanged(p, Y, k) for p, k in zip(first[1:], ORDER)]
     second = [second[0]] + [exchanged(p, X, k) for p, k in zip(second[1:], ORDER)]
     blocks = column_blocks(first, second)
-    loss_value = (divergence + other) / (row_count * lax.axis_size("batch"))
-    blocks, loss_value = lax.optimization_barrier((blocks, loss_value))
     pieces = lax.all_to_all(blocks, Z, 0, 0)
     total = pl.pallas_call(
         total_kernel,

time: 160 us -> 157 us (0.981)
  waiting for transfers between devices: 36.7 us -> 32 us
  starting transfers between devices: 44.4 us -> 47.2 us
    ppermute x28, waiting for transfers between devices: 27.7 us -> 23 us  [exchanged(): return lax.ppermute(part, axis, [(i, i ^ k) for i in range(n)])]
    ppermute x28, starting transfers between devices: 35.9 us -> 38.6 us  [exchanged(): return lax.ppermute(part, axis, [(i, i ^ k) for i in range(n)])]
  transfers between devices with their start and end apart: 30 -> 30, of which waited for: 16 -> 14; matrix products, arithmetic and copies ran while one was open for 0% -> 0% of each run, Pallas kernels for 9% -> 9%
where the time goes in v5:
time: 157 us
  starting transfers between devices  47.2 us (30%)
  blocking collectives  40.1 us (26%)
  Pallas kernels  34.1 us (22%)
  waiting for transfers between devices  32 us (20%)
  between operations  3.14 us (2%)
    ppermute x28, starting transfers between devices, exchanged(): return lax.ppermute(part, axis, [(i, i ^ k) for i in range(n)])  38.6 us
    ppermute x28, waiting for transfers between devices, exchanged(): return lax.ppermute(part, axis, [(i, i ^ k) for i in range(n)])  23 us
    all_to_all x1, blocking collectives, local(): pieces = lax.all_to_all(sent, (X, Y), 0, 0)  14.3 us
    pallas_call x3, Pallas kernels, shares(): pl.pallas_call(share_kernel, in_specs=[pl.BlockSpec(memory_space=pltpu.SM...  13.5 us
    all_to_all x1, blocking collectives, local(): pieces = lax.all_to_all(blocks, Z, 0, 0)  12.9 us
    all_to_all x1, blocking collectives, local(): blocks = lax.all_to_all(total, Z, 0, 0)  12.9 us
    pallas_call x1, Pallas kernels, local_stats(): pl.pallas_call(stats_kernel, grid=(rows // TILE,), in_specs=[pl.BlockSpec...  12.2 us
    all_to_all x1, waiting for transfers between devices, local(): pieces = lax.all_to_all(sent, Z, 0, 0)  9 us
  transfers between devices with their start and end apart: 30, of which 14 were waited for; matrix products, arithmetic and copies ran while one was open for 0% of the time, Pallas kernels for 9%

profile of v5, /device:TPU:2, one launch (start us, length us, event | category | flops | bytes accessed | tf_op | source)
XLA Modules:
  0.0 156.7 jit_solution(12135324185174593497)
XLA Ops:
  0.7 12.2 %local_stats.1 = (f32[2,1024,1536]{2,1,0:T(8,128)}, f32[16,32,128]{2,1,0:T(8,128)}) custom-call(s32[1]{0:T(128)} %bitcast.3.base_ref, bf16[1024,1024]{1,0:T(8,128)(2,1)} %queries_ref.1, bf16[1536,1024]{1,0:T(8,128)(2,1)} %queue_ref.7, bf16[1024,1536]{1,0:T(8,128)(2,1)} %mentor_ref.1, s32[8,128]{1,0:T(8,128)} %bitcast.12), custom_call_target="tpu_custom_call" | custom-call | tf_op jit(solution)/shard_map/local_stats/pallas_call | solution.py:88
  12.8 14.3 %all_to_all.20.pieces_ref = f32[16,32,128]{2,1,0:T(8,128)S(1)} all-to-all(f32[16,32,128]{2,1,0:T(8,128)} %get-tuple-element.39), channel_id=1, replica_groups=mesh['batch'=2,'queue_0'=4,'queue_1'=4,'queue_2'=8] {'queue_0','queue_1'}, dimensions={0} | all-to-all | bytes 524288 | tf_op jit(solution)/shard_map/all_to_all | solution.py:350
  27.1 0.7 merge_plane.1
  27.8 8.5 %all-to-all-start.1 = ((f32[8,32,128]{2,1,0:T(8,128)}), f32[8,32,128]{2,1,0:T(8,128)S(1)}, u32[]{:S(2)}, u32[]{:S(2)}) async-start(f32[8,32,128]{2,1,0:T(8,128)} %merge_plane.1), calls=%async_computation.1 | async-start | bytes 262144 | tf_op jit(solution)/shard_map/all_to_all | solution.py:359
  36.3 0.1 pad_add_fusion.2.numbers_ref
  36.3 9.0 %all-to-all-done.1.pieces_ref = f32[8,32,128]{2,1,0:T(8,128)S(1)} async-done(((f32[8,32,128]{2,1,0:T(8,128)}), f32[8,32,128]{2,1,0:T(8,128)S(1)}, u32[]{:S(2)}, u32[]{:S(2)}) %all-to-all-start.1) | async-done | bytes 131104 | tf_op jit(solution)/shard_map/all_to_all | solution.py:359
  45.4 0.7 merge_all.1
  46.0 3.5 %shares.5 = (f32[64,1024]{1,0:T(8,128)S(1)}, f32[64,1024]{1,0:T(8,128)S(1)}, f32[64,1024]{1,0:T(8,128)S(1)}, f32[64,1024]{1,0:T(8,128)S(1)}) custom-call(s32[2]{0:T(128)S(1)} %pad_add_fusion.2.numbers_ref, f32[16,128]{1,0:T(8,128)S(1)} %get-tuple-element.40.logs_ref, bf16[1536,1024]{1,0:T(8,128)(2,1)S(1)} %copy-done, ...), custom_call_target="tpu_custom_call" | custom-call | flops 805306368 | bytes 7340032 | tf_op jit(solution)/shard_map/shares/pallas_call | solution.py:163
  49.5 0.6 collective-permute-start.5
  50.1 1.7 %collective-permute-start.6 = (f32[64,1024]{1,0:T(8,128)S(1)}, f32[64,1024]{1,0:T(8,128)S(1)}, u32[]{:S(2)}, u32[]{:S(2)}) collective-permute-start(f32[64,1024]{1,0:T(8,128)S(1)} %get-tuple-element.56), channel_id=1, source_target_pairs={{0,24},{8,16},{16,8},{24,0},{1,25},{9,17},{17,9},{25,1},{2,26},{10... | collective-permute-start | bytes 786440 | tf_op jit(solution)/shard_map/ppermute | solution.py:21
  51.8 1.6 %collective-permute-start.1 = (f32[64,1024]{1,0:T(8,128)S(1)}, f32[64,1024]{1,0:T(8,128)S(1)}, u32[]{:S(2)}, u32[]{:S(2)}) collective-permute-start(f32[64,1024]{1,0:T(8,128)S(1)} %get-tuple-element.48), channel_id=1, source_target_pairs={{0,32},{32,0},{64,96},{96,64},{1,33},{33,1},{65,97},{97,65},{2,34}... | collective-permute-start | bytes 786440 | tf_op jit(solution)/shard_map/ppermute | solution.py:21
  53.4 0.4 collective-permute-start.2
  53.8 0.1 pad_add_fusion.1.numbers_ref
  53.9 6.6 %shares.4 = (f32[128,1024]{1,0:T(8,128)S(1)}, f32[128,1024]{1,0:T(8,128)S(1)}, f32[128,1024]{1,0:T(8,128)S(1)}, f32[128,1024]{1,0:T(8,128)S(1)}) custom-call(s32[4]{0:T(128)S(1)} %pad_add_fusion.1.numbers_ref, f32[16,128]{1,0:T(8,128)S(1)} %get-tuple-element.40.logs_ref, bf16[1536,1024]{1,0:T(8,128)(2,1)} %queue_ref.7, ...), custom_call_target="tpu_custom_call" | custom-call | flops 1610612736 | bytes 11534336 | tf_op jit(solution)/shard_map/shares/pallas_call | solution.py:163
  60.5 0.0 copy-start.1
  60.5 1.1 relayed.3
  61.6 0.3 collective-permute-start.7
  61.9 2.4 %collective-permute-start.8 = (f32[128,1024]{1,0:T(8,128)}, f32[128,1024]{1,0:T(8,128)}, u32[]{:S(2)}, u32[]{:S(2)}) collective-permute-start(f32[128,1024]{1,0:T(8,128)} %get-tuple-element.58), channel_id=1, source_target_pairs={{0,24},{8,16},{16,8},{24,0},{1,25},{9,17},{17,9},{25,1},{2,26},{10... | collective-permute-start | bytes 1572872 | tf_op jit(solution)/shard_map/ppermute | solution.py:21
  64.3 1.1 relayed.2
  65.4 1.4 collective-permute-start.3
  66.8 1.0 collective-permute-start.4
  67.8 0.1 pad_add_fusion.numbers_ref
  67.9 0.2 collective-permute-start
  68.1 3.5 %shares.3 = (f32[128,1024]{1,0:T(8,128)S(1)}, f32[128,1024]{1,0:T(8,128)S(1)}) custom-call(s32[2]{0:T(128)S(1)} %pad_add_fusion.numbers_ref, f32[16,128]{1,0:T(8,128)S(1)} %get-tuple-element.40.logs_ref, bf16[1536,1024]{1,0:T(8,128)(2,1)S(1)} %copy-done.1, f32[2,1024,1536]{2,1,0:T(8,128)} %get-tuple-element.41.logits_hbm), custom_call_target="tpu_custom_call" | custom-call | flops 805306368 | bytes 7340032 | tf_op jit(solution)/shard_map/shares/pallas_call | solution.py:163
  72.8 0.5 collective-permute-done.8.refs_7_
  73.3 1.9 %collective-permute-done.3.refs_3_ = f32[128,1024]{1,0:T(8,128)} collective-permute-done((f32[128,1024]{1,0:T(8,128)}, f32[128,1024]{1,0:T(8,128)}, u32[]{:S(2)}, u32[]{:S(2)}) %collective-permute-start.3) | collective-permute-done | bytes 524320 | tf_op jit(solution)/shard_map/ppermute | solution.py:21
  75.2 1.1 collective-permute-done.4.refs_4_
  76.3 1.7 %split_sums.1 = (f32[32,1024]{1,0:T(8,128)S(1)}, f32[32,1024]{1,0:T(8,128)S(1)}, f32[32,1024]{1,0:T(8,128)S(1)}, f32[32,1024]{1,0:T(8,128)S(1)}, f32[32,1024]{1,...) custom-call(s32[1]{0:T(128)} %bitcast.1.refs_0_.y_ref, ...), custom_call_target="tpu_custom_call" | custom-call | bytes 4194304 | tf_op jit(solution)/shard_map/split_sums/pallas_call | solution.py:214
  78.0 0.5 collective-permute-start.10
  78.5 1.8 %collective-permute-start.11 = (f32[32,1024]{1,0:T(8,128)S(1)}, f32[32,1024]{1,0:T(8,128)S(1)}, u32[]{:S(2)}, u32[]{:S(2)}) collective-permute-start(f32[32,1024]{1,0:T(8,128)S(1)} %get-tuple-element.62), channel_id=1, source_target_pairs={{0,24},{8,16},{16,8},{24,0},{1,25},{9,17},{17,9},{25,1},{2,26},{10... | collective-permute-start | bytes 393224 | tf_op jit(solution)/shard_map/ppermute | solution.py:21
  80.2 2.8 %collective-permute-start.12 = (f32[32,1024]{1,0:T(8,128)S(1)}, f32[32,1024]{1,0:T(8,128)S(1)}, u32[]{:S(2)}, u32[]{:S(2)}) collective-permute-start(f32[32,1024]{1,0:T(8,128)S(1)} %get-tuple-element.64), channel_id=1, source_target_pairs={{0,64},{32,96},{64,0},{96,32},{1,65},{33,97},{65,1},{97,33},{2,66}... | collective-permute-start | bytes 393224 | tf_op jit(solution)/shard_map/ppermute | solution.py:21
  83.0 0.4 collective-permute-start.13
  83.4 0.9 collective-permute-start.14
  84.3 1.9 %collective-permute-start.9 = (f32[32,1024]{1,0:T(8,128)S(1)}, f32[32,1024]{1,0:T(8,128)S(1)}, u32[]{:S(2)}, u32[]{:S(2)}) collective-permute-start(f32[32,1024]{1,0:T(8,128)S(1)} %get-tuple-element.60), channel_id=1, source_target_pairs={{0,16},{8,24},{16,0},{24,8},{1,17},{9,25},{17,1},{25,9},{2,18},{10... | collective-permute-start | bytes 393224 | tf_op jit(solution)/shard_map/ppermute | solution.py:21
  86.3 0.4 collective-permute-done.12.refs_5_
  86.7 1.3 collective-permute-done.13.refs_6_
  88.0 0.4 collective-permute-done.14.refs_7_
  88.4 2.4 %collective-permute-done.9.refs_1_ = f32[32,1024]{1,0:T(8,128)S(1)} collective-permute-done((f32[32,1024]{1,0:T(8,128)S(1)}, f32[32,1024]{1,0:T(8,128)S(1)}, u32[]{:S(2)}, u32[]{:S(2)}) %collective-permute-start.9) | collective-permute-done | bytes 131104 | tf_op jit(solution)/shard_map/ppermute | solution.py:21
  90.8 0.1 column_blocks.1
  90.9 12.9 %all_to_all.21.pieces_ref = f32[8,64,128]{2,1,0:T(8,128)S(1)} all-to-all(f32[8,64,128]{2,1,0:T(8,128)S(1)} %column_blocks.1), channel_id=1, replica_groups=mesh['batch'=2,'queue_0'=4,'queue_1'=4,'queue_2'=8] {'queue_2'}, dimensions={0} | all-to-all | bytes 524288 | tf_op jit(solution)/shard_map/all_to_all | solution.py:392
  103.8 12.9 %all_to_all.22.blocks_ref = f32[8,64,128]{2,1,0:T(8,128)S(1)} all-to-all(f32[8,64,128]{2,1,0:T(8,128)S(1)} %total.1), channel_id=1, replica_groups=mesh['batch'=2,'queue_0'=4,'queue_1'=4,'queue_2'=8] {'queue_2'}, dimensions={0} | all-to-all | bytes 524288 | tf_op jit(solution)/shard_map/all_to_all | solution.py:401
  116.7 2.0 %collective-permute-start.15 = (f32[32,1024]{1,0:T(8,128)S(1)}, f32[32,1024]{1,0:T(8,128)S(1)}, u32[]{:S(2)}, u32[]{:S(2)}) collective-permute-start(f32[32,1024]{1,0:T(8,128)S(1)} %get-tuple-element.67.refs_0_), channel_id=1, source_target_pairs={{0,16},{8,24},{16,0},{24,8},{1,17},{9,25},{17,1},{25,9},{2,18},{10... | collective-permute-start | bytes 393224 | tf_op jit(solution)/shard_map/ppermute | solution.py:21
  118.7 0.4 collective-permute-start.16
  119.1 1.8 %collective-permute-start.17 = (f32[32,1024]{1,0:T(8,128)S(1)}, f32[32,1024]{1,0:T(8,128)S(1)}, u32[]{:S(2)}, u32[]{:S(2)}) collective-permute-start(f32[32,1024]{1,0:T(8,128)S(1)} %get-tuple-element.67.refs_0_), channel_id=1, source_target_pairs={{0,24},{8,16},{16,8},{24,0},{1,25},{9,17},{17,9},{25,1},{2,26},{10... | collective-permute-start | bytes 393224 | tf_op jit(solution)/shard_map/ppermute | solution.py:21
  120.9 2.9 %collective-permute-start.18 = (f32[32,1024]{1,0:T(8,128)S(1)}, f32[32,1024]{1,0:T(8,128)S(1)}, u32[]{:S(2)}, u32[]{:S(2)}) collective-permute-start(f32[32,1024]{1,0:T(8,128)S(1)} %get-tuple-element.68.refs_4_), channel_id=1, source_target_pairs={{0,64},{32,96},{64,0},{96,32},{1,65},{33,97},{65,1},{97,33},{2,66}... | collective-permute-start | bytes 393224 | tf_op jit(solution)/shard_map/ppermute | solution.py:21
  123.7 0.3 collective-permute-start.19
  124.1 0.9 collective-permute-start.20
  125.0 1.7 %collective-permute-done.17.refs_3_ = f32[32,1024]{1,0:T(8,128)S(1)} collective-permute-done((f32[32,1024]{1,0:T(8,128)S(1)}, f32[32,1024]{1,0:T(8,128)S(1)}, u32[]{:S(2)}, u32[]{:S(2)}) %collective-permute-start.17) | collective-permute-done | bytes 131104 | tf_op jit(solution)/shard_map/ppermute | solution.py:21
  126.7 2.0 %collective-permute-done.18.refs_5_ = f32[32,1024]{1,0:T(8,128)S(1)} collective-permute-done((f32[32,1024]{1,0:T(8,128)S(1)}, f32[32,1024]{1,0:T(8,128)S(1)}, u32[]{:S(2)}, u32[]{:S(2)}) %collective-permute-start.18) | collective-permute-done | bytes 131104 | tf_op jit(solution)/shard_map/ppermute | solution.py:21
  128.6 2.4 %collective-permute-done.19.refs_6_ = f32[32,1024]{1,0:T(8,128)S(1)} collective-permute-done((f32[32,1024]{1,0:T(8,128)S(1)}, f32[32,1024]{1,0:T(8,128)S(1)}, u32[]{:S(2)}, u32[]{:S(2)}) %collective-permute-start.19) | collective-permute-done | bytes 131104 | tf_op jit(solution)/shard_map/ppermute | solution.py:21
  131.0 0.1 stacked.1
  131.1 1.8 %collective-permute-start.25 = (f32[128,1024]{1,0:T(8,128)S(1)}, f32[128,1024]{1,0:T(8,128)S(1)}, u32[]{:S(2)}, u32[]{:S(2)}) collective-permute-start(f32[128,1024]{1,0:T(8,128)S(1)} %get-tuple-element.72.refs_1_), channel_id=1, source_target_pairs={{0,24},{8,16},{16,8},{24,0},{1,25},{9,17},{17,9},{25,1},{2,26},{10... | collective-permute-start | bytes 1572872 | tf_op jit(solution)/shard_map/ppermute | solution.py:21
  132.9 0.0 collective-permute-start.26
  132.9 1.0 collective-permute-start.21
  133.9 3.5 %collective-permute-start.22 = (f32[128,1024]{1,0:T(8,128)S(1)}, f32[128,1024]{1,0:T(8,128)S(1)}, u32[]{:S(2)}, u32[]{:S(2)}) collective-permute-start(f32[128,1024]{1,0:T(8,128)S(1)} %get-tuple-element.69.refs_0_), channel_id=1, source_target_pairs={{0,32},{32,0},{64,96},{96,64},{1,33},{33,1},{65,97},{97,65},{2,34}... | collective-permute-start | bytes 1572872 | tf_op jit(solution)/shard_map/ppermute | solution.py:21
  137.4 5.5 %collective-permute-done.25.a.refs_5_ = f32[128,1024]{1,0:T(8,128)S(1)} collective-permute-done((f32[128,1024]{1,0:T(8,128)S(1)}, f32[128,1024]{1,0:T(8,128)S(1)}, u32[]{:S(2)}, u32[]{:S(2)}) %collective-permute-start.25) | collective-permute-done | bytes 524320 | tf_op jit(solution)/shard_map/ppermute | solution.py:21
  142.9 0.1 collective-permute-start.27
  143.0 2.1 %collective-permute-start.28 = (f32[64,1024]{1,0:T(8,128)S(1)}, f32[64,1024]{1,0:T(8,128)S(1)}, u32[]{:S(2)}, u32[]{:S(2)}) collective-permute-start(f32[64,1024]{1,0:T(8,128)S(1)} %get-tuple-element.74), channel_id=1, source_target_pairs={{0,24},{8,16},{16,8},{24,0},{1,25},{9,17},{17,9},{25,1},{2,26},{10... | collective-permute-start | bytes 786440 | tf_op jit(solution)/shard_map/ppermute | solution.py:21
  145.2 2.9 %collective-permute-start.23 = (f32[64,1024]{1,0:T(8,128)S(1)}, f32[64,1024]{1,0:T(8,128)S(1)}, u32[]{:S(2)}, u32[]{:S(2)}) collective-permute-start(f32[64,1024]{1,0:T(8,128)S(1)} %get-tuple-element.70), channel_id=1, source_target_pairs={{0,32},{32,0},{64,96},{96,64},{1,33},{33,1},{65,97},{97,65},{2,34}... | collective-permute-start | bytes 786440 | tf_op jit(solution)/shard_map/ppermute | solution.py:21
  148.1 1.1 collective-permute-start.24
  149.3 1.8 %assembled.2.refs_4_ = f32[1024,1024]{1,0:T(8,128)} custom-call(s32[1]{0:T(128)} %bitcast.refs_1_.x_ref, s32[1]{0:T(128)} %bitcast.1.refs_0_.y_ref, f32[128,1024]{1,0:T(8,128)S(1)} %get-tuple-element.69.refs_0_, f32[128,1024]{1,0:T(8,128)S(1)} %get-tuple-element.72.refs_1_, f32[128,1024]{1,0:T(8,128)S(1)} %collective-permute-done.22.b.refs_2_, ...), custom_call_target="tpu_custom_call" | custom-call | tf_op jit(solution)/shard_map/assembled/pallas_call | solution.py:325
  151.1 1.4 collective-permute-done.23.refs_0_
  152.5 2.0 %collective-permute-done.24.refs_1_ = f32[64,1024]{1,0:T(8,128)S(1)} collective-permute-done((f32[64,1024]{1,0:T(8,128)S(1)}, f32[64,1024]{1,0:T(8,128)S(1)}, u32[]{:S(2)}, u32[]{:S(2)}) %collective-permute-start.24) | collective-permute-done | bytes 262176 | tf_op jit(solution)/shard_map/ppermute | solution.py:21
  154.5 1.0 assembled.3
  (23 shorter events, 0.2 us)
Async XLA Ops:
  0.6 45.4 %copy-start = (bf16[1536,1024]{1,0:T(8,128)(2,1)S(1)}, bf16[1536,1024]{1,0:T(8,128)(2,1)}, u32[]{:S(2)}) copy-start(bf16[1536,1024]{1,0:T(8,128)(2,1)} %queue_ref.7) | copy-start | bytes 9437188
  27.8 17.5 %all-to-all-start.1 = ((f32[8,32,128]{2,1,0:T(8,128)}), f32[8,32,128]{2,1,0:T(8,128)S(1)}, u32[]{:S(2)}, u32[]{:S(2)}) async-start(f32[8,32,128]{2,1,0:T(8,128)} %merge_plane.1), calls=%async_computation.1 | async-start | bytes 262144 | tf_op jit(solution)/shard_map/all_to_all | solution.py:359
  49.5 11.0 %collective-permute-start.5 = (f32[64,1024]{1,0:T(8,128)S(1)}, f32[64,1024]{1,0:T(8,128)S(1)}, u32[]{:S(2)}, u32[]{:S(2)}) collective-permute-start(f32[64,1024]{1,0:T(8,128)S(1)} %get-tuple-element.55), channel_id=1, source_target_pairs={{0,8},{8,0},{16,24},{24,16},{1,9},{9,1},{17,25},{25,17},{2,10},{10... | collective-permute-start | bytes 786440 | tf_op jit(solution)/shard_map/ppermute | solution.py:21
  50.1 10.4 %collective-permute-start.6 = (f32[64,1024]{1,0:T(8,128)S(1)}, f32[64,1024]{1,0:T(8,128)S(1)}, u32[]{:S(2)}, u32[]{:S(2)}) collective-permute-start(f32[64,1024]{1,0:T(8,128)S(1)} %get-tuple-element.56), channel_id=1, source_target_pairs={{0,24},{8,16},{16,8},{24,0},{1,25},{9,17},{17,9},{25,1},{2,26},{10... | collective-permute-start | bytes 786440 | tf_op jit(solution)/shard_map/ppermute | solution.py:21
  51.8 12.5 %collective-permute-start.1 = (f32[64,1024]{1,0:T(8,128)S(1)}, f32[64,1024]{1,0:T(8,128)S(1)}, u32[]{:S(2)}, u32[]{:S(2)}) collective-permute-start(f32[64,1024]{1,0:T(8,128)S(1)} %get-tuple-element.48), channel_id=1, source_target_pairs={{0,32},{32,0},{64,96},{96,64},{1,33},{33,1},{65,97},{97,65},{2,34}... | collective-permute-start | bytes 786440 | tf_op jit(solution)/shard_map/ppermute | solution.py:21
  53.4 10.9 %collective-permute-start.2 = (f32[64,1024]{1,0:T(8,128)S(1)}, f32[64,1024]{1,0:T(8,128)S(1)}, u32[]{:S(2)}, u32[]{:S(2)}) collective-permute-start(f32[64,1024]{1,0:T(8,128)S(1)} %get-tuple-element.49), channel_id=1, source_target_pairs={{0,96},{32,64},{64,32},{96,0},{1,97},{33,65},{65,33},{97,1},{2,98}... | collective-permute-start | bytes 786440 | tf_op jit(solution)/shard_map/ppermute | solution.py:21
  60.5 7.6 %copy-start.1 = (bf16[1536,1024]{1,0:T(8,128)(2,1)S(1)}, bf16[1536,1024]{1,0:T(8,128)(2,1)}, u32[]{:S(2)}) copy-start(bf16[1536,1024]{1,0:T(8,128)(2,1)} %queue_ref.7) | copy-start | bytes 9437188
  61.6 11.2 %collective-permute-start.7 = (f32[128,1024]{1,0:T(8,128)}, f32[128,1024]{1,0:T(8,128)}, u32[]{:S(2)}, u32[]{:S(2)}) collective-permute-start(f32[128,1024]{1,0:T(8,128)} %get-tuple-element.57), channel_id=1, source_target_pairs={{0,8},{8,0},{16,24},{24,16},{1,9},{9,1},{17,25},{25,17},{2,10},{10... | collective-permute-start | bytes 1572872 | tf_op jit(solution)/shard_map/ppermute | solution.py:21
  61.9 11.4 %collective-permute-start.8 = (f32[128,1024]{1,0:T(8,128)}, f32[128,1024]{1,0:T(8,128)}, u32[]{:S(2)}, u32[]{:S(2)}) collective-permute-start(f32[128,1024]{1,0:T(8,128)} %get-tuple-element.58), channel_id=1, source_target_pairs={{0,24},{8,16},{16,8},{24,0},{1,25},{9,17},{17,9},{25,1},{2,26},{10... | collective-permute-start | bytes 1572872 | tf_op jit(solution)/shard_map/ppermute | solution.py:21
  65.4 9.8 %collective-permute-start.3 = (f32[128,1024]{1,0:T(8,128)}, f32[128,1024]{1,0:T(8,128)}, u32[]{:S(2)}, u32[]{:S(2)}) collective-permute-start(f32[128,1024]{1,0:T(8,128)} %get-tuple-element.50), channel_id=1, source_target_pairs={{0,32},{32,0},{64,96},{96,64},{1,33},{33,1},{65,97},{97,65},{2,34}... | collective-permute-start | bytes 1572872 | tf_op jit(solution)/shard_map/ppermute | solution.py:21
  66.8 9.5 %collective-permute-start.4 = (f32[128,1024]{1,0:T(8,128)}, f32[128,1024]{1,0:T(8,128)}, u32[]{:S(2)}, u32[]{:S(2)}) collective-permute-start(f32[128,1024]{1,0:T(8,128)} %get-tuple-element.51), channel_id=1, source_target_pairs={{0,96},{32,64},{64,32},{96,0},{1,97},{33,65},{65,33},{97,1},{2,98}... | collective-permute-start | bytes 1572872 | tf_op jit(solution)/shard_map/ppermute | solution.py:21
  67.9 3.7 %collective-permute-start = (f32[1,1]{1,0:T(1,128)}, f32[1,1]{1,0:T(1,128)}, u32[]{:S(2)}, u32[]{:S(2)}) collective-permute-start(f32[1,1]{1,0:T(1,128)} %get-tuple-element.44), channel_id=1, source_target_pairs={{0,128},{128,0},{1,129},{129,1},{2,130},{130,2},{3,131},{131,3},{4... | collective-permute-start | bytes 20 | tf_op jit(solution)/shard_map/ppermute | solution.py:372
  78.0 6.3 %collective-permute-start.10 = (f32[32,1024]{1,0:T(8,128)S(1)}, f32[32,1024]{1,0:T(8,128)S(1)}, u32[]{:S(2)}, u32[]{:S(2)}) collective-permute-start(f32[32,1024]{1,0:T(8,128)S(1)} %get-tuple-element.61), channel_id=1, source_target_pairs={{0,8},{8,0},{16,24},{24,16},{1,9},{9,1},{17,25},{25,17},{2,10},{10... | collective-permute-start | bytes 393224 | tf_op jit(solution)/shard_map/ppermute | solution.py:21
  78.5 7.8 %collective-permute-start.11 = (f32[32,1024]{1,0:T(8,128)S(1)}, f32[32,1024]{1,0:T(8,128)S(1)}, u32[]{:S(2)}, u32[]{:S(2)}) collective-permute-start(f32[32,1024]{1,0:T(8,128)S(1)} %get-tuple-element.62), channel_id=1, source_target_pairs={{0,24},{8,16},{16,8},{24,0},{1,25},{9,17},{17,9},{25,1},{2,26},{10... | collective-permute-start | bytes 393224 | tf_op jit(solution)/shard_map/ppermute | solution.py:21
  80.2 6.5 %collective-permute-start.12 = (f32[32,1024]{1,0:T(8,128)S(1)}, f32[32,1024]{1,0:T(8,128)S(1)}, u32[]{:S(2)}, u32[]{:S(2)}) collective-permute-start(f32[32,1024]{1,0:T(8,128)S(1)} %get-tuple-element.64), channel_id=1, source_target_pairs={{0,64},{32,96},{64,0},{96,32},{1,65},{33,97},{65,1},{97,33},{2,66}... | collective-permute-start | bytes 393224 | tf_op jit(solution)/shard_map/ppermute | solution.py:21
  83.0 5.0 %collective-permute-start.13 = (f32[32,1024]{1,0:T(8,128)S(1)}, f32[32,1024]{1,0:T(8,128)S(1)}, u32[]{:S(2)}, u32[]{:S(2)}) collective-permute-start(f32[32,1024]{1,0:T(8,128)S(1)} %get-tuple-element.65), channel_id=1, source_target_pairs={{0,32},{32,0},{64,96},{96,64},{1,33},{33,1},{65,97},{97,65},{2,34}... | collective-permute-start | bytes 393224 | tf_op jit(solution)/shard_map/ppermute | solution.py:21
  83.4 5.0 %collective-permute-start.14 = (f32[32,1024]{1,0:T(8,128)S(1)}, f32[32,1024]{1,0:T(8,128)S(1)}, u32[]{:S(2)}, u32[]{:S(2)}) collective-permute-start(f32[32,1024]{1,0:T(8,128)S(1)} %get-tuple-element.66), channel_id=1, source_target_pairs={{0,96},{32,64},{64,32},{96,0},{1,97},{33,65},{65,33},{97,1},{2,98}... | collective-permute-start | bytes 393224 | tf_op jit(solution)/shard_map/ppermute | solution.py:21
  84.3 6.5 %collective-permute-start.9 = (f32[32,1024]{1,0:T(8,128)S(1)}, f32[32,1024]{1,0:T(8,128)S(1)}, u32[]{:S(2)}, u32[]{:S(2)}) collective-permute-start(f32[32,1024]{1,0:T(8,128)S(1)} %get-tuple-element.60), channel_id=1, source_target_pairs={{0,16},{8,24},{16,0},{24,8},{1,17},{9,25},{17,1},{25,9},{2,18},{10... | collective-permute-start | bytes 393224 | tf_op jit(solution)/shard_map/ppermute | solution.py:21
  116.7 7.4 %collective-permute-start.15 = (f32[32,1024]{1,0:T(8,128)S(1)}, f32[32,1024]{1,0:T(8,128)S(1)}, u32[]{:S(2)}, u32[]{:S(2)}) collective-permute-start(f32[32,1024]{1,0:T(8,128)S(1)} %get-tuple-element.67.refs_0_), channel_id=1, source_target_pairs={{0,16},{8,24},{16,0},{24,8},{1,17},{9,25},{17,1},{25,9},{2,18},{10... | collective-permute-start | bytes 393224 | tf_op jit(solution)/shard_map/ppermute | solution.py:21
  118.7 6.3 %collective-permute-start.16 = (f32[32,1024]{1,0:T(8,128)S(1)}, f32[32,1024]{1,0:T(8,128)S(1)}, u32[]{:S(2)}, u32[]{:S(2)}) collective-permute-start(f32[32,1024]{1,0:T(8,128)S(1)} %get-tuple-element.67.refs_0_), channel_id=1, source_target_pairs={{0,8},{8,0},{16,24},{24,16},{1,9},{9,1},{17,25},{25,17},{2,10},{10... | collective-permute-start | bytes 393224 | tf_op jit(solution)/shard_map/ppermute | solution.py:21
  119.1 7.6 %collective-permute-start.17 = (f32[32,1024]{1,0:T(8,128)S(1)}, f32[32,1024]{1,0:T(8,128)S(1)}, u32[]{:S(2)}, u32[]{:S(2)}) collective-permute-start(f32[32,1024]{1,0:T(8,128)S(1)} %get-tuple-element.67.refs_0_), channel_id=1, source_target_pairs={{0,24},{8,16},{16,8},{24,0},{1,25},{9,17},{17,9},{25,1},{2,26},{10... | collective-permute-start | bytes 393224 | tf_op jit(solution)/shard_map/ppermute | solution.py:21
  120.9 7.8 %collective-permute-start.18 = (f32[32,1024]{1,0:T(8,128)S(1)}, f32[32,1024]{1,0:T(8,128)S(1)}, u32[]{:S(2)}, u32[]{:S(2)}) collective-permute-start(f32[32,1024]{1,0:T(8,128)S(1)} %get-tuple-element.68.refs_4_), channel_id=1, source_target_pairs={{0,64},{32,96},{64,0},{96,32},{1,65},{33,97},{65,1},{97,33},{2,66}... | collective-permute-start | bytes 393224 | tf_op jit(solution)/shard_map/ppermute | solution.py:21
  123.7 7.3 %collective-permute-start.19 = (f32[32,1024]{1,0:T(8,128)S(1)}, f32[32,1024]{1,0:T(8,128)S(1)}, u32[]{:S(2)}, u32[]{:S(2)}) collective-permute-start(f32[32,1024]{1,0:T(8,128)S(1)} %get-tuple-element.68.refs_4_), channel_id=1, source_target_pairs={{0,32},{32,0},{64,96},{96,64},{1,33},{33,1},{65,97},{97,65},{2,34}... | collective-permute-start | bytes 393224 | tf_op jit(solution)/shard_map/ppermute | solution.py:21
  124.1 7.0 %collective-permute-start.20 = (f32[32,1024]{1,0:T(8,128)S(1)}, f32[32,1024]{1,0:T(8,128)S(1)}, u32[]{:S(2)}, u32[]{:S(2)}) collective-permute-start(f32[32,1024]{1,0:T(8,128)S(1)} %get-tuple-element.68.refs_4_), channel_id=1, source_target_pairs={{0,96},{32,64},{64,32},{96,0},{1,97},{33,65},{65,33},{97,1},{2,98}... | collective-permute-start | bytes 393224 | tf_op jit(solution)/shard_map/ppermute | solution.py:21
  131.1 11.8 %collective-permute-start.25 = (f32[128,1024]{1,0:T(8,128)S(1)}, f32[128,1024]{1,0:T(8,128)S(1)}, u32[]{:S(2)}, u32[]{:S(2)}) collective-permute-start(f32[128,1024]{1,0:T(8,128)S(1)} %get-tuple-element.72.refs_1_), channel_id=1, source_target_pairs={{0,24},{8,16},{16,8},{24,0},{1,25},{9,17},{17,9},{25,1},{2,26},{10... | collective-permute-start | bytes 1572872 | tf_op jit(solution)/shard_map/ppermute | solution.py:21
  132.9 10.0 %collective-permute-start.26 = (f32[128,1024]{1,0:T(8,128)S(1)}, f32[128,1024]{1,0:T(8,128)S(1)}, u32[]{:S(2)}, u32[]{:S(2)}) collective-permute-start(f32[128,1024]{1,0:T(8,128)S(1)} %get-tuple-element.72.refs_1_), channel_id=1, source_target_pairs={{0,8},{8,0},{16,24},{24,16},{1,9},{9,1},{17,25},{25,17},{2,10},{10... | collective-permute-start | bytes 1572872 | tf_op jit(solution)/shard_map/ppermute | solution.py:21
  132.9 12.3 %collective-permute-start.21 = (f32[128,1024]{1,0:T(8,128)S(1)}, f32[128,1024]{1,0:T(8,128)S(1)}, u32[]{:S(2)}, u32[]{:S(2)}) collective-permute-start(f32[128,1024]{1,0:T(8,128)S(1)} %get-tuple-element.69.refs_0_), channel_id=1, source_target_pairs={{0,96},{32,64},{64,32},{96,0},{1,97},{33,65},{65,33},{97,1},{2,98}... | collective-permute-start | bytes 1572872 | tf_op jit(solution)/shard_map/ppermute | solution.py:21
  133.9 11.3 %collective-permute-start.22 = (f32[128,1024]{1,0:T(8,128)S(1)}, f32[128,1024]{1,0:T(8,128)S(1)}, u32[]{:S(2)}, u32[]{:S(2)}) collective-permute-start(f32[128,1024]{1,0:T(8,128)S(1)} %get-tuple-element.69.refs_0_), channel_id=1, source_target_pairs={{0,32},{32,0},{64,96},{96,64},{1,33},{33,1},{65,97},{97,65},{2,34}... | collective-permute-start | bytes 1572872 | tf_op jit(solution)/shard_map/ppermute | solution.py:21
  142.9 8.2 %collective-permute-start.27 = (f32[64,1024]{1,0:T(8,128)S(1)}, f32[64,1024]{1,0:T(8,128)S(1)}, u32[]{:S(2)}, u32[]{:S(2)}) collective-permute-start(f32[64,1024]{1,0:T(8,128)S(1)} %get-tuple-element.73), channel_id=1, source_target_pairs={{0,8},{8,0},{16,24},{24,16},{1,9},{9,1},{17,25},{25,17},{2,10},{10... | collective-permute-start | bytes 786440 | tf_op jit(solution)/shard_map/ppermute | solution.py:21
  143.0 8.1 %collective-permute-start.28 = (f32[64,1024]{1,0:T(8,128)S(1)}, f32[64,1024]{1,0:T(8,128)S(1)}, u32[]{:S(2)}, u32[]{:S(2)}) collective-permute-start(f32[64,1024]{1,0:T(8,128)S(1)} %get-tuple-element.74), channel_id=1, source_target_pairs={{0,24},{8,16},{16,8},{24,0},{1,25},{9,17},{17,9},{25,1},{2,26},{10... | collective-permute-start | bytes 786440 | tf_op jit(solution)/shard_map/ppermute | solution.py:21
  145.2 7.3 %collective-permute-start.23 = (f32[64,1024]{1,0:T(8,128)S(1)}, f32[64,1024]{1,0:T(8,128)S(1)}, u32[]{:S(2)}, u32[]{:S(2)}) collective-permute-start(f32[64,1024]{1,0:T(8,128)S(1)} %get-tuple-element.70), channel_id=1, source_target_pairs={{0,32},{32,0},{64,96},{96,64},{1,33},{33,1},{65,97},{97,65},{2,34}... | collective-permute-start | bytes 786440 | tf_op jit(solution)/shard_map/ppermute | solution.py:21
  148.1 6.4 %collective-permute-start.24 = (f32[64,1024]{1,0:T(8,128)S(1)}, f32[64,1024]{1,0:T(8,128)S(1)}, u32[]{:S(2)}, u32[]{:S(2)}) collective-permute-start(f32[64,1024]{1,0:T(8,128)S(1)} %get-tuple-element.71), channel_id=1, source_target_pairs={{0,96},{32,64},{64,32},{96,0},{1,97},{33,65},{65,33},{97,1},{2,98}... | collective-permute-start | bytes 786440 | tf_op jit(solution)/shard_map/ppermute | solution.py:21

commit v6 on v5

--- a/solution.py
+++ b/solution.py
@@ -21,7 +21,7 @@
     return lax.ppermute(part, axis, [(i, i ^ k) for i in range(n)])
 
 
-SHARE_LIMIT = 49 * 1024 * 1024
+SHARE_LIMIT = 44 * 1024 * 1024
 SMALL_LIMIT = 8 * 1024 * 1024
 
 BLOCK = 128
@@ -46,7 +46,7 @@
 
 
 def stats_kernel(
-    base_ref, queries_ref, queue_ref, mentor_ref, positives_ref, logits_ref, sent_ref
+    base_ref, queries_ref, queue_ref, mentor_ref, positives_ref, scores_ref, kept_ref, sent_ref
 ):
     step = pl.program_id(0)
     scale = score_factor / math.sqrt(queries_ref.shape[1])
@@ -54,7 +54,8 @@
         queries_ref[...], queue_ref[...], (((1,), (1,)), ((), ())),
         preferred_element_type=jnp.float32,
     )
-    logits_ref[0] = tile
+    scores_ref[0] = tile
+    kept_ref[0] = mentor_ref[...]
     for part in range(TILE // BLOCK):
         at = slice(part * BLOCK, (part + 1) * BLOCK)
         number = step * (TILE // BLOCK) + part
@@ -63,7 +64,6 @@
         stud_sum = jnp.sum(jnp.exp(scores - stud_max), axis=1, keepdims=True)
         wanted = as_column(positives_ref[pl.ds(number, 1), :]) - base_ref[0]
         teacher = teacher_logits(mentor_ref[at, :], wanted)
-        logits_ref[1, at, :] = teacher
         teach_max = jnp.max(teacher, axis=1, keepdims=True)
         teach_exp = jnp.exp(teacher - teach_max)
         teach_sum = jnp.sum(teach_exp, axis=1, keepdims=True)
@@ -96,11 +96,13 @@
             pl.BlockSpec((8, BLOCK), lambda i: (0, 0)),
         ],
         out_specs=[
-            pl.BlockSpec((2, TILE, keys), lambda i: (0, i, 0)),
+            pl.BlockSpec((1, TILE, keys), lambda i: (0, i, 0)),
+            pl.BlockSpec((1, TILE, keys), lambda i: (0, i, 0)),
             pl.BlockSpec((copies, 32, BLOCK), lambda i: (0, 0, 0)),
         ],
         out_shape=[
-            jax.ShapeDtypeStruct((2, rows, keys), jnp.float32),
+            jax.ShapeDtypeStruct((3, rows, keys), jnp.float32),
+            jax.ShapeDtypeStruct((6, rows, keys), mentor.dtype),
             jax.ShapeDtypeStruct((copies, 32, BLOCK), jnp.float32),
         ],
         compiler_params=pltpu.CompilerParams(vmem_limit_bytes=LIMIT),
@@ -134,49 +136,71 @@
     total_ref[...] = jnp.broadcast_to(total, total_ref.shape)
 
 
-def share_kernel(numbers_ref, logs_ref, queue_ref, logits_hbm, *refs):
-    outs, (logits_ref, weights_ref, sem) = refs[:-3], refs[-3:]
+def share_kernel(
+    numbers_ref, base_ref, logs_ref, positives_ref, queue_ref, scores_hbm, mentor_hbm, *refs
+):
+    outs, (scores_ref, mentor_ref, weights_ref, sem) = refs[:-4], refs[-4:]
     copies = []
     for k in range(numbers_ref.shape[0]):
         at = pl.ds(pl.multiple_of(numbers_ref[k] * BLOCK, BLOCK), BLOCK)
         copies.append(
-            pltpu.make_async_copy(logits_hbm.at[:, at, :], logits_ref.at[k], sem.at[k])
+            [
+                pltpu.make_async_copy(mentor_hbm.at[0, at, :], mentor_ref.at[k], sem.at[2 * k]),
+                pltpu.make_async_copy(scores_hbm.at[0, at, :], scores_ref.at[k], sem.at[2 * k + 1]),
+            ]
         )
-        copies[k].start()
-    for k, copy in enumerate(copies):
+        for copy in copies[k]:
+            copy.start()
+
+    def weigh(k):
         number = numbers_ref[k]
         stud_log = as_column(logs_ref[pl.ds(number, 1), :])
         teach_log = as_column(logs_ref[pl.ds(8 + number, 1), :])
-        copy.wait()
-        weights = jnp.exp(logits_ref[k, 0] - stud_log) - jnp.exp(logits_ref[k, 1] - teach_log)
+        wanted = as_column(positives_ref[pl.ds(number, 1), :]) - base_ref[0]
+        for copy in copies[k]:
+            copy.wait()
+        weights = jnp.exp(scores_ref[k] - stud_log) - jnp.exp(
+            teacher_logits(mentor_ref[k], wanted) - teach_log
+        )
         weights_ref[k * BLOCK : (k + 1) * BLOCK, :] = weights.astype(jnp.bfloat16)
-    total = jnp.dot(weights_ref[...], queue_ref[...], preferred_element_type=jnp.float32)
+
     rows = outs[0].shape[0]
-    for k, out in enumerate(outs):
-        out[...] = total[k * rows : (k + 1) * rows, :]
-
-
-def shares(numbers, parts, logs, queue, logits):
+    for first in range(0, len(copies), 2):
+        for k in (first, first + 1):
+            weigh(k)
+        total = jnp.dot(
+            weights_ref[first * BLOCK : (first + 2) * BLOCK, :], queue_ref[...],
+            preferred_element_type=jnp.float32,
+        )
+        each = 2 * BLOCK // rows
+        for k in range(each):
+            outs[first // 2 * each + k][...] = total[k * rows : (k + 1) * rows, :]
+
+
+def shares(numbers, parts, base, logs, positives, scores, mentor, queue):
     count = numbers.shape[0]
     keys, width = queue.shape
     out = jax.ShapeDtypeStruct((BLOCK // parts, width), jnp.float32)
     return pl.pallas_call(
         share_kernel,
-        in_specs=[
-            pl.BlockSpec(memory_space=pltpu.SMEM), WHOLE, WHOLE,
-            pl.BlockSpec(memory_space=pl.ANY),
-        ],
+        in_specs=[pl.BlockSpec(memory_space=pltpu.SMEM)] * 2
+        + [WHOLE] * 3
+        + [pl.BlockSpec(memory_space=pl.ANY)] * 2,
         out_specs=[WHOLE] * (count * parts),
         out_shape=[out] * (count * parts),
         scratch_shapes=[
-            pltpu.VMEM((count, 2, BLOCK, keys), jnp.float32),
+            pltpu.VMEM((count, BLOCK, keys), jnp.float32),
+            pltpu.VMEM((count, BLOCK, keys), jnp.bfloat16),
             pltpu.VMEM((count * BLOCK, keys), jnp.bfloat16),
-            pltpu.SemaphoreType.DMA((count,)),
+            pltpu.SemaphoreType.DMA((2 * count,)),
         ],
         compiler_params=pltpu.CompilerParams(vmem_limit_bytes=SHARE_LIMIT),
-        cost_estimate=moved(2 * keys * width + count * BLOCK * (8 * keys + 4 * width), 2 * count * BLOCK * keys * width),
+        cost_estimate=moved(
+            2 * keys * width + count * BLOCK * (6 * keys + 4 * width),
+            2 * count * BLOCK * keys * width,
+        ),
         name="shares",
-    )(numbers, logs, queue, logits)
+    )(numbers, base, logs, positives, queue, scores, mentor)
 
 
 def relay_kernel(a_ref, b_ref, upper_ref, lower_ref, a_out, b_out):
@@ -346,7 +370,7 @@
     x, y = (lax.axis_index(axis).astype(jnp.int32) for axis in (X, Y))
     base = (lax.axis_index(QUEUE) * key_count).astype(jnp.int32).reshape(1)
     positives = positives.reshape(8, BLOCK)
-    logits, sent = local_stats(base, queries, queue, mentor_logit_grid, positives, 16)
+    scores, mentor, sent = local_stats(base, queries, queue, mentor_logit_grid, positives, 16)
     pieces = lax.all_to_all(sent, (X, Y), 0, 0)
     sent = pl.pallas_call(
         merge_kernel,
@@ -373,7 +397,7 @@
 
     def share(partners, parts=1):
         numbers = jnp.stack([n for k in partners for n in (x ^ k, 4 + (y ^ k))])
-        return shares(numbers, parts, logs, queue, logits)
+        return shares(numbers, parts, base, logs, positives, scores, mentor, queue)
 
     far = share((2,), 2)
     ways = (X, 1), (X, 3), (Y, 1), (Y, 3)

time: 157 us -> 154 us (0.981)
  Pallas kernels: 34.1 us -> 30.8 us
    pallas_call x3, Pallas kernels: 13.5 us -> 11.4 us  [shares(): pl.pallas_call(share_kernel, in_specs=[pl.BlockSpec(memory_space=pltpu.SM...]
  transfers between devices with their start and end apart: 30 -> 30, of which waited for: 14 -> 15; matrix products, arithmetic and copies ran while one was open for 0% -> 0% of each run, Pallas kernels for 9% -> 8%
where the time goes in v6:
time: 154 us
  starting transfers between devices  46.1 us (30%)
  blocking collectives  40.1 us (26%)
  waiting for transfers between devices  33.2 us (22%)
  Pallas kernels  30.8 us (20%)
  between operations  3.21 us (2%)
    ppermute x28, starting transfers between devices, exchanged(): return lax.ppermute(part, axis, [(i, i ^ k) for i in range(n)])  37.6 us
    ppermute x28, waiting for transfers between devices, exchanged(): return lax.ppermute(part, axis, [(i, i ^ k) for i in range(n)])  24.2 us
    all_to_all x1, blocking collectives, local(): pieces = lax.all_to_all(sent, (X, Y), 0, 0)  14.3 us
    all_to_all x1, blocking collectives, local(): pieces = lax.all_to_all(blocks, Z, 0, 0)  13 us
    all_to_all x1, blocking collectives, local(): blocks = lax.all_to_all(total, Z, 0, 0)  12.9 us
    pallas_call x3, Pallas kernels, shares(): pl.pallas_call(share_kernel, in_specs=[pl.BlockSpec(memory_space=pltpu.SM...  11.4 us
    pallas_call x1, Pallas kernels, local_stats(): pl.pallas_call(stats_kernel, grid=(rows // TILE,), in_specs=[pl.BlockSpec...  11.1 us
    all_to_all x1, waiting for transfers between devices, local(): pieces = lax.all_to_all(sent, Z, 0, 0)  9 us
  transfers between devices with their start and end apart: 30, of which 15 were waited for; matrix products, arithmetic and copies ran while one was open for 0% of the time, Pallas kernels for 8%

profile of v6, /device:TPU:2, one launch (start us, length us, event | category | flops | bytes accessed | tf_op | source)
XLA Modules:
  0.0 153.7 jit_solution(5441322869064022519)
XLA Ops:
  0.7 11.1 %local_stats.1 = (f32[3,1024,1536]{2,1,0:T(8,128)}, bf16[6,1024,1536]{2,1,0:T(8,128)(2,1)}, f32[16,32,128]{2,1,0:T(8,128)}) custom-call(s32[1]{0:T(128)} %bitcast.3.base_ref, bf16[1024,1024]{1,0:T(8,128)(2,1)} %queries_ref.1, bf16[1536,1024]{1,0:T(8,128)(2,1)} %queue_ref.7, bf16[1024,1536]{1,0:T(8,128)(2,1)} %mentor_ref.1, s32[8,128]{1,0:T(8,128)} %bitcast.12), custom_call_target="tpu_custom_call" | custom-call | tf_op jit(solution)/shard_map/local_stats/pallas_call | solution.py:88
  11.7 14.3 %all_to_all.20.pieces_ref = f32[16,32,128]{2,1,0:T(8,128)S(1)} all-to-all(f32[16,32,128]{2,1,0:T(8,128)} %get-tuple-element.40), channel_id=1, replica_groups=mesh['batch'=2,'queue_0'=4,'queue_1'=4,'queue_2'=8] {'queue_0','queue_1'}, dimensions={0} | all-to-all | bytes 524288 | tf_op jit(solution)/shard_map/all_to_all | solution.py:374
  26.0 0.7 merge_plane.1
  26.7 8.5 %all-to-all-start.1 = ((f32[8,32,128]{2,1,0:T(8,128)}), f32[8,32,128]{2,1,0:T(8,128)S(1)}, u32[]{:S(2)}, u32[]{:S(2)}) async-start(f32[8,32,128]{2,1,0:T(8,128)} %merge_plane.1), calls=%async_computation.1 | async-start | bytes 262144 | tf_op jit(solution)/shard_map/all_to_all | solution.py:383
  35.2 0.1 pad_add_fusion.2.numbers_ref
  35.3 9.0 %all-to-all-done.1.pieces_ref = f32[8,32,128]{2,1,0:T(8,128)S(1)} async-done(((f32[8,32,128]{2,1,0:T(8,128)}), f32[8,32,128]{2,1,0:T(8,128)S(1)}, u32[]{:S(2)}, u32[]{:S(2)}) %all-to-all-start.1) | async-done | bytes 131104 | tf_op jit(solution)/shard_map/all_to_all | solution.py:383
  44.3 0.7 merge_all.1
  45.0 3.3 %shares.5 = (f32[64,1024]{1,0:T(8,128)S(1)}, f32[64,1024]{1,0:T(8,128)S(1)}, f32[64,1024]{1,0:T(8,128)S(1)}, f32[64,1024]{1,0:T(8,128)S(1)}) custom-call(s32[2]{0:T(128)S(1)} %pad_add_fusion.2.numbers_ref, s32[1]{0:T(128)} %bitcast.3.base_ref, f32[16,128]{1,0:T(8,128)S(1)} %get-tuple-element.41.logs_ref, s32[8,128]{1,0:T(8,128)S(1)} %bitcast.13, ...), custom_call_target="tpu_custom_call" | custom-call | flops 805306368 | bytes 6553600 | tf_op jit(solution)/shard_map/shares/pallas_call | solution.py:184
  48.3 0.5 collective-permute-start.5
  48.8 1.7 %collective-permute-start.6 = (f32[64,1024]{1,0:T(8,128)S(1)}, f32[64,1024]{1,0:T(8,128)S(1)}, u32[]{:S(2)}, u32[]{:S(2)}) collective-permute-start(f32[64,1024]{1,0:T(8,128)S(1)} %get-tuple-element.58), channel_id=1, source_target_pairs={{0,24},{8,16},{16,8},{24,0},{1,25},{9,17},{17,9},{25,1},{2,26},{10... | collective-permute-start | bytes 786440 | tf_op jit(solution)/shard_map/ppermute | solution.py:21
  50.6 1.6 %collective-permute-start.1 = (f32[64,1024]{1,0:T(8,128)S(1)}, f32[64,1024]{1,0:T(8,128)S(1)}, u32[]{:S(2)}, u32[]{:S(2)}) collective-permute-start(f32[64,1024]{1,0:T(8,128)S(1)} %get-tuple-element.50), channel_id=1, source_target_pairs={{0,32},{32,0},{64,96},{96,64},{1,33},{33,1},{65,97},{97,65},{2,34}... | collective-permute-start | bytes 786440 | tf_op jit(solution)/shard_map/ppermute | solution.py:21
  52.2 0.4 collective-permute-start.2
  52.6 0.1 pad_add_fusion.1.numbers_ref
  52.7 4.8 %shares.4 = (f32[128,1024]{1,0:T(8,128)S(1)}, f32[128,1024]{1,0:T(8,128)S(1)}, f32[128,1024]{1,0:T(8,128)S(1)}, f32[128,1024]{1,0:T(8,128)S(1)}) custom-call(s32[4]{0:T(128)S(1)} %pad_add_fusion.1.numbers_ref, s32[1]{0:T(128)} %bitcast.3.base_ref, f32[16,128]{1,0:T(8,128)S(1)} %get-tuple-element.41.logs_ref, s32[8,128]{1,0:T(8,128)S(1)} %bitcast.14, ...), custom_call_target="tpu_custom_call" | custom-call | flops 1610612736 | bytes 9961472 | tf_op jit(solution)/shard_map/shares/pallas_call | solution.py:184
  57.5 1.1 relayed.3
  58.6 0.3 collective-permute-start.7
  58.9 2.4 %collective-permute-start.8 = (f32[128,1024]{1,0:T(8,128)}, f32[128,1024]{1,0:T(8,128)}, u32[]{:S(2)}, u32[]{:S(2)}) collective-permute-start(f32[128,1024]{1,0:T(8,128)} %get-tuple-element.60), channel_id=1, source_target_pairs={{0,24},{8,16},{16,8},{24,0},{1,25},{9,17},{17,9},{25,1},{2,26},{10... | collective-permute-start | bytes 1572872 | tf_op jit(solution)/shard_map/ppermute | solution.py:21
  61.3 1.1 relayed.2
  62.3 1.4 collective-permute-start.3
  63.8 1.0 collective-permute-start.4
  64.7 0.1 pad_add_fusion.numbers_ref
  64.8 0.0 collective-permute-start
  64.8 3.3 %shares.3 = (f32[128,1024]{1,0:T(8,128)S(1)}, f32[128,1024]{1,0:T(8,128)S(1)}) custom-call(s32[2]{0:T(128)S(1)} %pad_add_fusion.numbers_ref, s32[1]{0:T(128)} %bitcast.3.base_ref, f32[16,128]{1,0:T(8,128)S(1)} %get-tuple-element.41.logs_ref, s32[8,128]{1,0:T(8,128)S(1)} %bitcast.15, bf16[1536,1024]{1,0:T(8,128)(2,1)S(1)} %copy-done, ...), custom_call_target="tpu_custom_call" | custom-call | flops 805306368 | bytes 6553600 | tf_op jit(solution)/shard_map/shares/pallas_call | solution.py:184
  69.4 0.8 collective-permute-done.8.refs_7_
  70.2 1.9 %collective-permute-done.3.refs_3_ = f32[128,1024]{1,0:T(8,128)} collective-permute-done((f32[128,1024]{1,0:T(8,128)}, f32[128,1024]{1,0:T(8,128)}, u32[]{:S(2)}, u32[]{:S(2)}) %collective-permute-start.3) | collective-permute-done | bytes 524320 | tf_op jit(solution)/shard_map/ppermute | solution.py:21
  72.1 1.1 collective-permute-done.4.refs_4_
  73.3 1.7 %split_sums.1 = (f32[32,1024]{1,0:T(8,128)S(1)}, f32[32,1024]{1,0:T(8,128)S(1)}, f32[32,1024]{1,0:T(8,128)S(1)}, f32[32,1024]{1,0:T(8,128)S(1)}, f32[32,1024]{1,...) custom-call(s32[1]{0:T(128)} %bitcast.1.refs_0_.y_ref, ...), custom_call_target="tpu_custom_call" | custom-call | bytes 4194304 | tf_op jit(solution)/shard_map/split_sums/pallas_call | solution.py:238
  74.9 0.5 collective-permute-start.10
  75.4 1.7 %collective-permute-start.11 = (f32[32,1024]{1,0:T(8,128)S(1)}, f32[32,1024]{1,0:T(8,128)S(1)}, u32[]{:S(2)}, u32[]{:S(2)}) collective-permute-start(f32[32,1024]{1,0:T(8,128)S(1)} %get-tuple-element.64), channel_id=1, source_target_pairs={{0,24},{8,16},{16,8},{24,0},{1,25},{9,17},{17,9},{25,1},{2,26},{10... | collective-permute-start | bytes 393224 | tf_op jit(solution)/shard_map/ppermute | solution.py:21
  77.1 2.8 %collective-permute-start.12 = (f32[32,1024]{1,0:T(8,128)S(1)}, f32[32,1024]{1,0:T(8,128)S(1)}, u32[]{:S(2)}, u32[]{:S(2)}) collective-permute-start(f32[32,1024]{1,0:T(8,128)S(1)} %get-tuple-element.66), channel_id=1, source_target_pairs={{0,64},{32,96},{64,0},{96,32},{1,65},{33,97},{65,1},{97,33},{2,66}... | collective-permute-start | bytes 393224 | tf_op jit(solution)/shard_map/ppermute | solution.py:21
  79.9 0.4 collective-permute-start.13
  80.3 0.9 collective-permute-start.14
  81.2 2.0 %collective-permute-start.9 = (f32[32,1024]{1,0:T(8,128)S(1)}, f32[32,1024]{1,0:T(8,128)S(1)}, u32[]{:S(2)}, u32[]{:S(2)}) collective-permute-start(f32[32,1024]{1,0:T(8,128)S(1)} %get-tuple-element.62), channel_id=1, source_target_pairs={{0,16},{8,24},{16,0},{24,8},{1,17},{9,25},{17,1},{25,9},{2,18},{10... | collective-permute-start | bytes 393224 | tf_op jit(solution)/shard_map/ppermute | solution.py:21
  83.2 0.4 collective-permute-done.12.refs_5_
  83.6 1.3 collective-permute-done.13.refs_6_
  84.9 0.4 collective-permute-done.14.refs_7_
  85.3 2.4 %collective-permute-done.9.refs_1_ = f32[32,1024]{1,0:T(8,128)S(1)} collective-permute-done((f32[32,1024]{1,0:T(8,128)S(1)}, f32[32,1024]{1,0:T(8,128)S(1)}, u32[]{:S(2)}, u32[]{:S(2)}) %collective-permute-start.9) | collective-permute-done | bytes 131104 | tf_op jit(solution)/shard_map/ppermute | solution.py:21
  87.7 0.1 column_blocks.1
  87.8 13.0 %all_to_all.21.pieces_ref = f32[8,64,128]{2,1,0:T(8,128)S(1)} all-to-all(f32[8,64,128]{2,1,0:T(8,128)S(1)} %column_blocks.1), channel_id=1, replica_groups=mesh['batch'=2,'queue_0'=4,'queue_1'=4,'queue_2'=8] {'queue_2'}, dimensions={0} | all-to-all | bytes 524288 | tf_op jit(solution)/shard_map/all_to_all | solution.py:416
  100.8 12.9 %all_to_all.22.blocks_ref = f32[8,64,128]{2,1,0:T(8,128)S(1)} all-to-all(f32[8,64,128]{2,1,0:T(8,128)S(1)} %total.1), channel_id=1, replica_groups=mesh['batch'=2,'queue_0'=4,'queue_1'=4,'queue_2'=8] {'queue_2'}, dimensions={0} | all-to-all | bytes 524288 | tf_op jit(solution)/shard_map/all_to_all | solution.py:425
  113.7 2.1 %collective-permute-start.15 = (f32[32,1024]{1,0:T(8,128)S(1)}, f32[32,1024]{1,0:T(8,128)S(1)}, u32[]{:S(2)}, u32[]{:S(2)}) collective-permute-start(f32[32,1024]{1,0:T(8,128)S(1)} %get-tuple-element.69.refs_0_), channel_id=1, source_target_pairs={{0,16},{8,24},{16,0},{24,8},{1,17},{9,25},{17,1},{25,9},{2,18},{10... | collective-permute-start | bytes 393224 | tf_op jit(solution)/shard_map/ppermute | solution.py:21
  115.7 0.3 collective-permute-start.16
  116.0 1.8 %collective-permute-start.17 = (f32[32,1024]{1,0:T(8,128)S(1)}, f32[32,1024]{1,0:T(8,128)S(1)}, u32[]{:S(2)}, u32[]{:S(2)}) collective-permute-start(f32[32,1024]{1,0:T(8,128)S(1)} %get-tuple-element.69.refs_0_), channel_id=1, source_target_pairs={{0,24},{8,16},{16,8},{24,0},{1,25},{9,17},{17,9},{25,1},{2,26},{10... | collective-permute-start | bytes 393224 | tf_op jit(solution)/shard_map/ppermute | solution.py:21
  117.9 2.9 %collective-permute-start.18 = (f32[32,1024]{1,0:T(8,128)S(1)}, f32[32,1024]{1,0:T(8,128)S(1)}, u32[]{:S(2)}, u32[]{:S(2)}) collective-permute-start(f32[32,1024]{1,0:T(8,128)S(1)} %get-tuple-element.70.refs_4_), channel_id=1, source_target_pairs={{0,64},{32,96},{64,0},{96,32},{1,65},{33,97},{65,1},{97,33},{2,66}... | collective-permute-start | bytes 393224 | tf_op jit(solution)/shard_map/ppermute | solution.py:21
  120.8 0.3 collective-permute-start.19
  121.0 0.9 collective-permute-start.20
  122.0 1.7 %collective-permute-done.17.refs_3_ = f32[32,1024]{1,0:T(8,128)S(1)} collective-permute-done((f32[32,1024]{1,0:T(8,128)S(1)}, f32[32,1024]{1,0:T(8,128)S(1)}, u32[]{:S(2)}, u32[]{:S(2)}) %collective-permute-start.17) | collective-permute-done | bytes 131104 | tf_op jit(solution)/shard_map/ppermute | solution.py:21
  123.6 2.1 %collective-permute-done.18.refs_5_ = f32[32,1024]{1,0:T(8,128)S(1)} collective-permute-done((f32[32,1024]{1,0:T(8,128)S(1)}, f32[32,1024]{1,0:T(8,128)S(1)}, u32[]{:S(2)}, u32[]{:S(2)}) %collective-permute-start.18) | collective-permute-done | bytes 131104 | tf_op jit(solution)/shard_map/ppermute | solution.py:21
  125.7 2.5 %collective-permute-done.19.refs_6_ = f32[32,1024]{1,0:T(8,128)S(1)} collective-permute-done((f32[32,1024]{1,0:T(8,128)S(1)}, f32[32,1024]{1,0:T(8,128)S(1)}, u32[]{:S(2)}, u32[]{:S(2)}) %collective-permute-start.19) | collective-permute-done | bytes 131104 | tf_op jit(solution)/shard_map/ppermute | solution.py:21
  128.2 0.1 stacked.1
  128.3 1.5 collective-permute-start.25
  129.8 0.3 collective-permute-start.26
  130.1 1.1 collective-permute-start.21
  131.2 3.2 %collective-permute-start.22 = (f32[128,1024]{1,0:T(8,128)S(1)}, f32[128,1024]{1,0:T(8,128)S(1)}, u32[]{:S(2)}, u32[]{:S(2)}) collective-permute-start(f32[128,1024]{1,0:T(8,128)S(1)} %get-tuple-element.71.refs_0_), channel_id=1, source_target_pairs={{0,32},{32,0},{64,96},{96,64},{1,33},{33,1},{65,97},{97,65},{2,34}... | collective-permute-start | bytes 1572872 | tf_op jit(solution)/shard_map/ppermute | solution.py:21
  134.4 5.6 %collective-permute-done.25.a.refs_5_ = f32[128,1024]{1,0:T(8,128)S(1)} collective-permute-done((f32[128,1024]{1,0:T(8,128)S(1)}, f32[128,1024]{1,0:T(8,128)S(1)}, u32[]{:S(2)}, u32[]{:S(2)}) %collective-permute-start.25) | collective-permute-done | bytes 524320 | tf_op jit(solution)/shard_map/ppermute | solution.py:21
  140.0 0.1 collective-permute-start.27
  140.1 1.6 %collective-permute-start.28 = (f32[64,1024]{1,0:T(8,128)S(1)}, f32[64,1024]{1,0:T(8,128)S(1)}, u32[]{:S(2)}, u32[]{:S(2)}) collective-permute-start(f32[64,1024]{1,0:T(8,128)S(1)} %get-tuple-element.76), channel_id=1, source_target_pairs={{0,24},{8,16},{16,8},{24,0},{1,25},{9,17},{17,9},{25,1},{2,26},{10... | collective-permute-start | bytes 786440 | tf_op jit(solution)/shard_map/ppermute | solution.py:21
  141.7 0.4 collective-permute-done.21.a.refs_3_
  142.1 3.0 %collective-permute-start.23 = (f32[64,1024]{1,0:T(8,128)S(1)}, f32[64,1024]{1,0:T(8,128)S(1)}, u32[]{:S(2)}, u32[]{:S(2)}) collective-permute-start(f32[64,1024]{1,0:T(8,128)S(1)} %get-tuple-element.72), channel_id=1, source_target_pairs={{0,32},{32,0},{64,96},{96,64},{1,33},{33,1},{65,97},{97,65},{2,34}... | collective-permute-start | bytes 786440 | tf_op jit(solution)/shard_map/ppermute | solution.py:21
  145.1 0.9 collective-permute-start.24
  146.0 1.8 %assembled.2.refs_4_ = f32[1024,1024]{1,0:T(8,128)} custom-call(s32[1]{0:T(128)} %bitcast.refs_1_.x_ref, s32[1]{0:T(128)} %bitcast.1.refs_0_.y_ref, f32[128,1024]{1,0:T(8,128)S(1)} %get-tuple-element.71.refs_0_, f32[128,1024]{1,0:T(8,128)S(1)} %get-tuple-element.74.refs_1_, f32[128,1024]{1,0:T(8,128)S(1)} %collective-permute-done.22.b.refs_2_, ...), custom_call_target="tpu_custom_call" | custom-call | tf_op jit(solution)/shard_map/assembled/pallas_call | solution.py:349
  147.9 1.6 %collective-permute-done.23.refs_0_ = f32[64,1024]{1,0:T(8,128)S(1)} collective-permute-done((f32[64,1024]{1,0:T(8,128)S(1)}, f32[64,1024]{1,0:T(8,128)S(1)}, u32[]{:S(2)}, u32[]{:S(2)}) %collective-permute-start.23) | collective-permute-done | bytes 262176 | tf_op jit(solution)/shard_map/ppermute | solution.py:21
  149.5 2.0 %collective-permute-done.24.refs_1_ = f32[64,1024]{1,0:T(8,128)S(1)} collective-permute-done((f32[64,1024]{1,0:T(8,128)S(1)}, f32[64,1024]{1,0:T(8,128)S(1)}, u32[]{:S(2)}, u32[]{:S(2)}) %collective-permute-start.24) | collective-permute-done | bytes 262176 | tf_op jit(solution)/shard_map/ppermute | solution.py:21
  151.5 1.0 assembled.3
  (23 shorter events, 0.2 us)
Async XLA Ops:
  0.6 44.3 %copy-start = (bf16[1536,1024]{1,0:T(8,128)(2,1)S(1)}, bf16[1536,1024]{1,0:T(8,128)(2,1)}, u32[]{:S(2)}) copy-start(bf16[1536,1024]{1,0:T(8,128)(2,1)} %queue_ref.7) | copy-start | bytes 9437188
  0.7 44.3 %copy-start.1 = (s32[1024]{0:T(1024)S(1)}, s32[1024]{0:T(1024)}, u32[]{:S(2)}) copy-start(s32[1024]{0:T(1024)} %param.7) | copy-start | bytes 12292
  26.7 17.6 %all-to-all-start.1 = ((f32[8,32,128]{2,1,0:T(8,128)}), f32[8,32,128]{2,1,0:T(8,128)S(1)}, u32[]{:S(2)}, u32[]{:S(2)}) async-start(f32[8,32,128]{2,1,0:T(8,128)} %merge_plane.1), calls=%async_computation.1 | async-start | bytes 262144 | tf_op jit(solution)/shard_map/all_to_all | solution.py:383
  48.3 9.2 %collective-permute-start.5 = (f32[64,1024]{1,0:T(8,128)S(1)}, f32[64,1024]{1,0:T(8,128)S(1)}, u32[]{:S(2)}, u32[]{:S(2)}) collective-permute-start(f32[64,1024]{1,0:T(8,128)S(1)} %get-tuple-element.57), channel_id=1, source_target_pairs={{0,8},{8,0},{16,24},{24,16},{1,9},{9,1},{17,25},{25,17},{2,10},{10... | collective-permute-start | bytes 786440 | tf_op jit(solution)/shard_map/ppermute | solution.py:21
  48.8 8.7 %collective-permute-start.6 = (f32[64,1024]{1,0:T(8,128)S(1)}, f32[64,1024]{1,0:T(8,128)S(1)}, u32[]{:S(2)}, u32[]{:S(2)}) collective-permute-start(f32[64,1024]{1,0:T(8,128)S(1)} %get-tuple-element.58), channel_id=1, source_target_pairs={{0,24},{8,16},{16,8},{24,0},{1,25},{9,17},{17,9},{25,1},{2,26},{10... | collective-permute-start | bytes 786440 | tf_op jit(solution)/shard_map/ppermute | solution.py:21
  50.6 10.7 %collective-permute-start.1 = (f32[64,1024]{1,0:T(8,128)S(1)}, f32[64,1024]{1,0:T(8,128)S(1)}, u32[]{:S(2)}, u32[]{:S(2)}) collective-permute-start(f32[64,1024]{1,0:T(8,128)S(1)} %get-tuple-element.50), channel_id=1, source_target_pairs={{0,32},{32,0},{64,96},{96,64},{1,33},{33,1},{65,97},{97,65},{2,34}... | collective-permute-start | bytes 786440 | tf_op jit(solution)/shard_map/ppermute | solution.py:21
  52.2 9.0 %collective-permute-start.2 = (f32[64,1024]{1,0:T(8,128)S(1)}, f32[64,1024]{1,0:T(8,128)S(1)}, u32[]{:S(2)}, u32[]{:S(2)}) collective-permute-start(f32[64,1024]{1,0:T(8,128)S(1)} %get-tuple-element.51), channel_id=1, source_target_pairs={{0,96},{32,64},{64,32},{96,0},{1,97},{33,65},{65,33},{97,1},{2,98}... | collective-permute-start | bytes 786440 | tf_op jit(solution)/shard_map/ppermute | solution.py:21
  58.6 10.9 %collective-permute-start.7 = (f32[128,1024]{1,0:T(8,128)}, f32[128,1024]{1,0:T(8,128)}, u32[]{:S(2)}, u32[]{:S(2)}) collective-permute-start(f32[128,1024]{1,0:T(8,128)} %get-tuple-element.59), channel_id=1, source_target_pairs={{0,8},{8,0},{16,24},{24,16},{1,9},{9,1},{17,25},{25,17},{2,10},{10... | collective-permute-start | bytes 1572872 | tf_op jit(solution)/shard_map/ppermute | solution.py:21
  58.9 11.3 %collective-permute-start.8 = (f32[128,1024]{1,0:T(8,128)}, f32[128,1024]{1,0:T(8,128)}, u32[]{:S(2)}, u32[]{:S(2)}) collective-permute-start(f32[128,1024]{1,0:T(8,128)} %get-tuple-element.60), channel_id=1, source_target_pairs={{0,24},{8,16},{16,8},{24,0},{1,25},{9,17},{17,9},{25,1},{2,26},{10... | collective-permute-start | bytes 1572872 | tf_op jit(solution)/shard_map/ppermute | solution.py:21
  62.3 9.8 %collective-permute-start.3 = (f32[128,1024]{1,0:T(8,128)}, f32[128,1024]{1,0:T(8,128)}, u32[]{:S(2)}, u32[]{:S(2)}) collective-permute-start(f32[128,1024]{1,0:T(8,128)} %get-tuple-element.52), channel_id=1, source_target_pairs={{0,32},{32,0},{64,96},{96,64},{1,33},{33,1},{65,97},{97,65},{2,34}... | collective-permute-start | bytes 1572872 | tf_op jit(solution)/shard_map/ppermute | solution.py:21
  63.8 9.5 %collective-permute-start.4 = (f32[128,1024]{1,0:T(8,128)}, f32[128,1024]{1,0:T(8,128)}, u32[]{:S(2)}, u32[]{:S(2)}) collective-permute-start(f32[128,1024]{1,0:T(8,128)} %get-tuple-element.53), channel_id=1, source_target_pairs={{0,96},{32,64},{64,32},{96,0},{1,97},{33,65},{65,33},{97,1},{2,98}... | collective-permute-start | bytes 1572872 | tf_op jit(solution)/shard_map/ppermute | solution.py:21
  64.8 3.3 %collective-permute-start = (f32[1,1]{1,0:T(1,128)}, f32[1,1]{1,0:T(1,128)}, u32[]{:S(2)}, u32[]{:S(2)}) collective-permute-start(f32[1,1]{1,0:T(1,128)} %get-tuple-element.46), channel_id=1, source_target_pairs={{0,128},{128,0},{1,129},{129,1},{2,130},{130,2},{3,131},{131,3},{4... | collective-permute-start | bytes 20 | tf_op jit(solution)/shard_map/ppermute | solution.py:396
  74.9 6.3 %collective-permute-start.10 = (f32[32,1024]{1,0:T(8,128)S(1)}, f32[32,1024]{1,0:T(8,128)S(1)}, u32[]{:S(2)}, u32[]{:S(2)}) collective-permute-start(f32[32,1024]{1,0:T(8,128)S(1)} %get-tuple-element.63), channel_id=1, source_target_pairs={{0,8},{8,0},{16,24},{24,16},{1,9},{9,1},{17,25},{25,17},{2,10},{10... | collective-permute-start | bytes 393224 | tf_op jit(solution)/shard_map/ppermute | solution.py:21
  75.4 7.8 %collective-permute-start.11 = (f32[32,1024]{1,0:T(8,128)S(1)}, f32[32,1024]{1,0:T(8,128)S(1)}, u32[]{:S(2)}, u32[]{:S(2)}) collective-permute-start(f32[32,1024]{1,0:T(8,128)S(1)} %get-tuple-element.64), channel_id=1, source_target_pairs={{0,24},{8,16},{16,8},{24,0},{1,25},{9,17},{17,9},{25,1},{2,26},{10... | collective-permute-start | bytes 393224 | tf_op jit(solution)/shard_map/ppermute | solution.py:21
  77.1 6.5 %collective-permute-start.12 = (f32[32,1024]{1,0:T(8,128)S(1)}, f32[32,1024]{1,0:T(8,128)S(1)}, u32[]{:S(2)}, u32[]{:S(2)}) collective-permute-start(f32[32,1024]{1,0:T(8,128)S(1)} %get-tuple-element.66), channel_id=1, source_target_pairs={{0,64},{32,96},{64,0},{96,32},{1,65},{33,97},{65,1},{97,33},{2,66}... | collective-permute-start | bytes 393224 | tf_op jit(solution)/shard_map/ppermute | solution.py:21
  79.9 5.0 %collective-permute-start.13 = (f32[32,1024]{1,0:T(8,128)S(1)}, f32[32,1024]{1,0:T(8,128)S(1)}, u32[]{:S(2)}, u32[]{:S(2)}) collective-permute-start(f32[32,1024]{1,0:T(8,128)S(1)} %get-tuple-element.67), channel_id=1, source_target_pairs={{0,32},{32,0},{64,96},{96,64},{1,33},{33,1},{65,97},{97,65},{2,34}... | collective-permute-start | bytes 393224 | tf_op jit(solution)/shard_map/ppermute | solution.py:21
  80.3 5.0 %collective-permute-start.14 = (f32[32,1024]{1,0:T(8,128)S(1)}, f32[32,1024]{1,0:T(8,128)S(1)}, u32[]{:S(2)}, u32[]{:S(2)}) collective-permute-start(f32[32,1024]{1,0:T(8,128)S(1)} %get-tuple-element.68), channel_id=1, source_target_pairs={{0,96},{32,64},{64,32},{96,0},{1,97},{33,65},{65,33},{97,1},{2,98}... | collective-permute-start | bytes 393224 | tf_op jit(solution)/shard_map/ppermute | solution.py:21
  81.2 6.5 %collective-permute-start.9 = (f32[32,1024]{1,0:T(8,128)S(1)}, f32[32,1024]{1,0:T(8,128)S(1)}, u32[]{:S(2)}, u32[]{:S(2)}) collective-permute-start(f32[32,1024]{1,0:T(8,128)S(1)} %get-tuple-element.62), channel_id=1, source_target_pairs={{0,16},{8,24},{16,0},{24,8},{1,17},{9,25},{17,1},{25,9},{2,18},{10... | collective-permute-start | bytes 393224 | tf_op jit(solution)/shard_map/ppermute | solution.py:21
  113.7 7.4 %collective-permute-start.15 = (f32[32,1024]{1,0:T(8,128)S(1)}, f32[32,1024]{1,0:T(8,128)S(1)}, u32[]{:S(2)}, u32[]{:S(2)}) collective-permute-start(f32[32,1024]{1,0:T(8,128)S(1)} %get-tuple-element.69.refs_0_), channel_id=1, source_target_pairs={{0,16},{8,24},{16,0},{24,8},{1,17},{9,25},{17,1},{25,9},{2,18},{10... | collective-permute-start | bytes 393224 | tf_op jit(solution)/shard_map/ppermute | solution.py:21
  115.7 6.2 %collective-permute-start.16 = (f32[32,1024]{1,0:T(8,128)S(1)}, f32[32,1024]{1,0:T(8,128)S(1)}, u32[]{:S(2)}, u32[]{:S(2)}) collective-permute-start(f32[32,1024]{1,0:T(8,128)S(1)} %get-tuple-element.69.refs_0_), channel_id=1, source_target_pairs={{0,8},{8,0},{16,24},{24,16},{1,9},{9,1},{17,25},{25,17},{2,10},{10... | collective-permute-start | bytes 393224 | tf_op jit(solution)/shard_map/ppermute | solution.py:21
  116.0 7.6 %collective-permute-start.17 = (f32[32,1024]{1,0:T(8,128)S(1)}, f32[32,1024]{1,0:T(8,128)S(1)}, u32[]{:S(2)}, u32[]{:S(2)}) collective-permute-start(f32[32,1024]{1,0:T(8,128)S(1)} %get-tuple-element.69.refs_0_), channel_id=1, source_target_pairs={{0,24},{8,16},{16,8},{24,0},{1,25},{9,17},{17,9},{25,1},{2,26},{10... | collective-permute-start | bytes 393224 | tf_op jit(solution)/shard_map/ppermute | solution.py:21
  117.9 7.9 %collective-permute-start.18 = (f32[32,1024]{1,0:T(8,128)S(1)}, f32[32,1024]{1,0:T(8,128)S(1)}, u32[]{:S(2)}, u32[]{:S(2)}) collective-permute-start(f32[32,1024]{1,0:T(8,128)S(1)} %get-tuple-element.70.refs_4_), channel_id=1, source_target_pairs={{0,64},{32,96},{64,0},{96,32},{1,65},{33,97},{65,1},{97,33},{2,66}... | collective-permute-start | bytes 393224 | tf_op jit(solution)/shard_map/ppermute | solution.py:21
  120.8 7.4 %collective-permute-start.19 = (f32[32,1024]{1,0:T(8,128)S(1)}, f32[32,1024]{1,0:T(8,128)S(1)}, u32[]{:S(2)}, u32[]{:S(2)}) collective-permute-start(f32[32,1024]{1,0:T(8,128)S(1)} %get-tuple-element.70.refs_4_), channel_id=1, source_target_pairs={{0,32},{32,0},{64,96},{96,64},{1,33},{33,1},{65,97},{97,65},{2,34}... | collective-permute-start | bytes 393224 | tf_op jit(solution)/shard_map/ppermute | solution.py:21
  121.0 7.2 %collective-permute-start.20 = (f32[32,1024]{1,0:T(8,128)S(1)}, f32[32,1024]{1,0:T(8,128)S(1)}, u32[]{:S(2)}, u32[]{:S(2)}) collective-permute-start(f32[32,1024]{1,0:T(8,128)S(1)} %get-tuple-element.70.refs_4_), channel_id=1, source_target_pairs={{0,96},{32,64},{64,32},{96,0},{1,97},{33,65},{65,33},{97,1},{2,98}... | collective-permute-start | bytes 393224 | tf_op jit(solution)/shard_map/ppermute | solution.py:21
  128.3 11.7 %collective-permute-start.25 = (f32[128,1024]{1,0:T(8,128)S(1)}, f32[128,1024]{1,0:T(8,128)S(1)}, u32[]{:S(2)}, u32[]{:S(2)}) collective-permute-start(f32[128,1024]{1,0:T(8,128)S(1)} %get-tuple-element.74.refs_1_), channel_id=1, source_target_pairs={{0,24},{8,16},{16,8},{24,0},{1,25},{9,17},{17,9},{25,1},{2,26},{10... | collective-permute-start | bytes 1572872 | tf_op jit(solution)/shard_map/ppermute | solution.py:21
  129.8 10.2 %collective-permute-start.26 = (f32[128,1024]{1,0:T(8,128)S(1)}, f32[128,1024]{1,0:T(8,128)S(1)}, u32[]{:S(2)}, u32[]{:S(2)}) collective-permute-start(f32[128,1024]{1,0:T(8,128)S(1)} %get-tuple-element.74.refs_1_), channel_id=1, source_target_pairs={{0,8},{8,0},{16,24},{24,16},{1,9},{9,1},{17,25},{25,17},{2,10},{10... | collective-permute-start | bytes 1572872 | tf_op jit(solution)/shard_map/ppermute | solution.py:21
  130.1 12.0 %collective-permute-start.21 = (f32[128,1024]{1,0:T(8,128)S(1)}, f32[128,1024]{1,0:T(8,128)S(1)}, u32[]{:S(2)}, u32[]{:S(2)}) collective-permute-start(f32[128,1024]{1,0:T(8,128)S(1)} %get-tuple-element.71.refs_0_), channel_id=1, source_target_pairs={{0,96},{32,64},{64,32},{96,0},{1,97},{33,65},{65,33},{97,1},{2,98}... | collective-permute-start | bytes 1572872 | tf_op jit(solution)/shard_map/ppermute | solution.py:21
  131.2 10.9 %collective-permute-start.22 = (f32[128,1024]{1,0:T(8,128)S(1)}, f32[128,1024]{1,0:T(8,128)S(1)}, u32[]{:S(2)}, u32[]{:S(2)}) collective-permute-start(f32[128,1024]{1,0:T(8,128)S(1)} %get-tuple-element.71.refs_0_), channel_id=1, source_target_pairs={{0,32},{32,0},{64,96},{96,64},{1,33},{33,1},{65,97},{97,65},{2,34}... | collective-permute-start | bytes 1572872 | tf_op jit(solution)/shard_map/ppermute | solution.py:21
  140.0 7.9 %collective-permute-start.27 = (f32[64,1024]{1,0:T(8,128)S(1)}, f32[64,1024]{1,0:T(8,128)S(1)}, u32[]{:S(2)}, u32[]{:S(2)}) collective-permute-start(f32[64,1024]{1,0:T(8,128)S(1)} %get-tuple-element.75), channel_id=1, source_target_pairs={{0,8},{8,0},{16,24},{24,16},{1,9},{9,1},{17,25},{25,17},{2,10},{10... | collective-permute-start | bytes 786440 | tf_op jit(solution)/shard_map/ppermute | solution.py:21
  140.1 7.8 %collective-permute-start.28 = (f32[64,1024]{1,0:T(8,128)S(1)}, f32[64,1024]{1,0:T(8,128)S(1)}, u32[]{:S(2)}, u32[]{:S(2)}) collective-permute-start(f32[64,1024]{1,0:T(8,128)S(1)} %get-tuple-element.76), channel_id=1, source_target_pairs={{0,24},{8,16},{16,8},{24,0},{1,25},{9,17},{17,9},{25,1},{2,26},{10... | collective-permute-start | bytes 786440 | tf_op jit(solution)/shard_map/ppermute | solution.py:21
  142.1 7.4 %collective-permute-start.23 = (f32[64,1024]{1,0:T(8,128)S(1)}, f32[64,1024]{1,0:T(8,128)S(1)}, u32[]{:S(2)}, u32[]{:S(2)}) collective-permute-start(f32[64,1024]{1,0:T(8,128)S(1)} %get-tuple-element.72), channel_id=1, source_target_pairs={{0,32},{32,0},{64,96},{96,64},{1,33},{33,1},{65,97},{97,65},{2,34}... | collective-permute-start | bytes 786440 | tf_op jit(solution)/shard_map/ppermute | solution.py:21
  145.1 6.4 %collective-permute-start.24 = (f32[64,1024]{1,0:T(8,128)S(1)}, f32[64,1024]{1,0:T(8,128)S(1)}, u32[]{:S(2)}, u32[]{:S(2)}) collective-permute-start(f32[64,1024]{1,0:T(8,128)S(1)} %get-tuple-element.73), channel_id=1, source_target_pairs={{0,96},{32,64},{64,32},{96,0},{1,97},{33,65},{65,33},{97,1},{2,98}... | collective-permute-start | bytes 786440 | tf_op jit(solution)/shard_map/ppermute | solution.py:21

commit v7 on v6

--- a/solution.py
+++ b/solution.py
@@ -410,8 +410,8 @@
     own, loss_value = lax.optimization_barrier((own, loss_value))
     places = y.reshape(1), x.reshape(1)
     first, second = split_sums(places, [own[0], *got[:2]], [own[1], *got[2:]])
-    first = [first[0]] + [exchanged(p, Y, k) for p, k in zip(first[1:], ORDER)]
-    second = [second[0]] + [exchanged(p, X, k) for p, k in zip(second[1:], ORDER)]
+    first = [first[0]] + [exchanged(first[i], Y, ORDER[i - 1]) for i in (2, 1, 3)]
+    second = [second[0]] + [exchanged(second[i], X, ORDER[i - 1]) for i in (1, 2, 3)]
     blocks = column_blocks(first, second)
     pieces = lax.all_to_all(blocks, Z, 0, 0)
     total = pl.pallas_call(

time: 154 us -> 154 us (level)
  no operation moved by 1% of the time
where the time goes in v7:
time: 154 us; the launch traced here: 153 us
  starting transfers between devices  45.9 us (30%)
  blocking collectives  40 us (26%)
  waiting for transfers between devices  32.9 us (21%)
  Pallas kernels  30.8 us (20%)
  between operations  3.21 us (2%)
    ppermute x28, starting transfers between devices, exchanged(): return lax.ppermute(part, axis, [(i, i ^ k) for i in range(n)])  37.4 us
    ppermute x28, waiting for transfers between devices, exchanged(): return lax.ppermute(part, axis, [(i, i ^ k) for i in range(n)])  23.9 us
    all_to_all x1, blocking collectives, local(): pieces = lax.all_to_all(sent, (X, Y), 0, 0)  14.3 us
    all_to_all x1, blocking collectives, local(): pieces = lax.all_to_all(blocks, Z, 0, 0)  12.9 us
    all_to_all x1, blocking collectives, local(): blocks = lax.all_to_all(total, Z, 0, 0)  12.9 us
    pallas_call x3, Pallas kernels, shares(): pl.pallas_call(share_kernel, in_specs=[pl.BlockSpec(memory_space=pltpu.SM...  11.4 us
    pallas_call x1, Pallas kernels, local_stats(): pl.pallas_call(stats_kernel, grid=(rows // TILE,), in_specs=[pl.BlockSpec...  11.1 us
    all_to_all x1, waiting for transfers between devices, local(): pieces = lax.all_to_all(sent, Z, 0, 0)  9 us
  transfers between devices with their start and end apart: 30, of which 15 were waited for; matrix products, arithmetic and copies ran while one was open for 0% of the time, Pallas kernels for 8%

profile of v7, /device:TPU:2, one launch (start us, length us, event | category | flops | bytes accessed | tf_op | source)
XLA Modules:
  0.0 153.1 jit_solution(3268303719740820041)
XLA Ops:
  0.7 11.1 %local_stats.1 = (f32[3,1024,1536]{2,1,0:T(8,128)}, bf16[6,1024,1536]{2,1,0:T(8,128)(2,1)}, f32[16,32,128]{2,1,0:T(8,128)}) custom-call(s32[1]{0:T(128)} %bitcast.3.base_ref, bf16[1024,1024]{1,0:T(8,128)(2,1)} %queries_ref.1, bf16[1536,1024]{1,0:T(8,128)(2,1)} %queue_ref.7, bf16[1024,1536]{1,0:T(8,128)(2,1)} %mentor_ref.1, s32[8,128]{1,0:T(8,128)} %bitcast.12), custom_call_target="tpu_custom_call" | custom-call | tf_op jit(solution)/shard_map/local_stats/pallas_call | solution.py:88
  11.7 14.3 %all_to_all.20.pieces_ref = f32[16,32,128]{2,1,0:T(8,128)S(1)} all-to-all(f32[16,32,128]{2,1,0:T(8,128)} %get-tuple-element.40), channel_id=1, replica_groups=mesh['batch'=2,'queue_0'=4,'queue_1'=4,'queue_2'=8] {'queue_0','queue_1'}, dimensions={0} | all-to-all | bytes 524288 | tf_op jit(solution)/shard_map/all_to_all | solution.py:374
  26.0 0.7 merge_plane.1
  26.7 8.5 %all-to-all-start.1 = ((f32[8,32,128]{2,1,0:T(8,128)}), f32[8,32,128]{2,1,0:T(8,128)S(1)}, u32[]{:S(2)}, u32[]{:S(2)}) async-start(f32[8,32,128]{2,1,0:T(8,128)} %merge_plane.1), calls=%async_computation.1 | async-start | bytes 262144 | tf_op jit(solution)/shard_map/all_to_all | solution.py:383
  35.2 0.1 pad_add_fusion.2.numbers_ref
  35.3 9.0 %all-to-all-done.1.pieces_ref = f32[8,32,128]{2,1,0:T(8,128)S(1)} async-done(((f32[8,32,128]{2,1,0:T(8,128)}), f32[8,32,128]{2,1,0:T(8,128)S(1)}, u32[]{:S(2)}, u32[]{:S(2)}) %all-to-all-start.1) | async-done | bytes 131104 | tf_op jit(solution)/shard_map/all_to_all | solution.py:383
  44.3 0.7 merge_all.1
  45.0 3.3 %shares.5 = (f32[64,1024]{1,0:T(8,128)S(1)}, f32[64,1024]{1,0:T(8,128)S(1)}, f32[64,1024]{1,0:T(8,128)S(1)}, f32[64,1024]{1,0:T(8,128)S(1)}) custom-call(s32[2]{0:T(128)S(1)} %pad_add_fusion.2.numbers_ref, s32[1]{0:T(128)} %bitcast.3.base_ref, f32[16,128]{1,0:T(8,128)S(1)} %get-tuple-element.41.logs_ref, s32[8,128]{1,0:T(8,128)S(1)} %bitcast.13, ...), custom_call_target="tpu_custom_call" | custom-call | flops 805306368 | bytes 6553600 | tf_op jit(solution)/shard_map/shares/pallas_call | solution.py:184
  48.3 0.5 collective-permute-start.5
  48.8 1.7 %collective-permute-start.6 = (f32[64,1024]{1,0:T(8,128)S(1)}, f32[64,1024]{1,0:T(8,128)S(1)}, u32[]{:S(2)}, u32[]{:S(2)}) collective-permute-start(f32[64,1024]{1,0:T(8,128)S(1)} %get-tuple-element.58), channel_id=1, source_target_pairs={{0,24},{8,16},{16,8},{24,0},{1,25},{9,17},{17,9},{25,1},{2,26},{10... | collective-permute-start | bytes 786440 | tf_op jit(solution)/shard_map/ppermute | solution.py:21
  50.6 1.6 %collective-permute-start.1 = (f32[64,1024]{1,0:T(8,128)S(1)}, f32[64,1024]{1,0:T(8,128)S(1)}, u32[]{:S(2)}, u32[]{:S(2)}) collective-permute-start(f32[64,1024]{1,0:T(8,128)S(1)} %get-tuple-element.50), channel_id=1, source_target_pairs={{0,32},{32,0},{64,96},{96,64},{1,33},{33,1},{65,97},{97,65},{2,34}... | collective-permute-start | bytes 786440 | tf_op jit(solution)/shard_map/ppermute | solution.py:21
  52.2 0.4 collective-permute-start.2
  52.6 0.1 pad_add_fusion.1.numbers_ref
  52.7 4.8 %shares.4 = (f32[128,1024]{1,0:T(8,128)S(1)}, f32[128,1024]{1,0:T(8,128)S(1)}, f32[128,1024]{1,0:T(8,128)S(1)}, f32[128,1024]{1,0:T(8,128)S(1)}) custom-call(s32[4]{0:T(128)S(1)} %pad_add_fusion.1.numbers_ref, s32[1]{0:T(128)} %bitcast.3.base_ref, f32[16,128]{1,0:T(8,128)S(1)} %get-tuple-element.41.logs_ref, s32[8,128]{1,0:T(8,128)S(1)} %bitcast.14, ...), custom_call_target="tpu_custom_call" | custom-call | flops 1610612736 | bytes 9961472 | tf_op jit(solution)/shard_map/shares/pallas_call | solution.py:184
  57.5 1.1 relayed.3
  58.6 0.3 collective-permute-start.7
  58.9 2.4 %collective-permute-start.8 = (f32[128,1024]{1,0:T(8,128)}, f32[128,1024]{1,0:T(8,128)}, u32[]{:S(2)}, u32[]{:S(2)}) collective-permute-start(f32[128,1024]{1,0:T(8,128)} %get-tuple-element.60), channel_id=1, source_target_pairs={{0,24},{8,16},{16,8},{24,0},{1,25},{9,17},{17,9},{25,1},{2,26},{10... | collective-permute-start | bytes 1572872 | tf_op jit(solution)/shard_map/ppermute | solution.py:21
  61.3 1.1 relayed.2
  62.3 1.4 collective-permute-start.3
  63.8 1.0 collective-permute-start.4
  64.7 0.1 pad_add_fusion.numbers_ref
  64.8 0.0 collective-permute-start
  64.8 3.3 %shares.3 = (f32[128,1024]{1,0:T(8,128)S(1)}, f32[128,1024]{1,0:T(8,128)S(1)}) custom-call(s32[2]{0:T(128)S(1)} %pad_add_fusion.numbers_ref, s32[1]{0:T(128)} %bitcast.3.base_ref, f32[16,128]{1,0:T(8,128)S(1)} %get-tuple-element.41.logs_ref, s32[8,128]{1,0:T(8,128)S(1)} %bitcast.15, bf16[1536,1024]{1,0:T(8,128)(2,1)S(1)} %copy-done, ...), custom_call_target="tpu_custom_call" | custom-call | flops 805306368 | bytes 6553600 | tf_op jit(solution)/shard_map/shares/pallas_call | solution.py:184
  69.4 0.8 collective-permute-done.8.refs_7_
  70.2 1.9 %collective-permute-done.3.refs_3_ = f32[128,1024]{1,0:T(8,128)} collective-permute-done((f32[128,1024]{1,0:T(8,128)}, f32[128,1024]{1,0:T(8,128)}, u32[]{:S(2)}, u32[]{:S(2)}) %collective-permute-start.3) | collective-permute-done | bytes 524320 | tf_op jit(solution)/shard_map/ppermute | solution.py:21
  72.1 1.1 collective-permute-done.4.refs_4_
  73.3 1.7 %split_sums.1 = (f32[32,1024]{1,0:T(8,128)S(1)}, f32[32,1024]{1,0:T(8,128)S(1)}, f32[32,1024]{1,0:T(8,128)S(1)}, f32[32,1024]{1,0:T(8,128)S(1)}, f32[32,1024]{1,...) custom-call(s32[1]{0:T(128)} %bitcast.1.refs_0_.y_ref, ...), custom_call_target="tpu_custom_call" | custom-call | bytes 4194304 | tf_op jit(solution)/shard_map/split_sums/pallas_call | solution.py:238
  74.9 1.6 %collective-permute-start.10 = (f32[32,1024]{1,0:T(8,128)S(1)}, f32[32,1024]{1,0:T(8,128)S(1)}, u32[]{:S(2)}, u32[]{:S(2)}) collective-permute-start(f32[32,1024]{1,0:T(8,128)S(1)} %get-tuple-element.63), channel_id=1, source_target_pairs={{0,16},{8,24},{16,0},{24,8},{1,17},{9,25},{17,1},{25,9},{2,18},{10... | collective-permute-start | bytes 393224 | tf_op jit(solution)/shard_map/ppermute | solution.py:21
  76.6 1.5 collective-permute-start.11
  78.1 2.9 %collective-permute-start.12 = (f32[32,1024]{1,0:T(8,128)S(1)}, f32[32,1024]{1,0:T(8,128)S(1)}, u32[]{:S(2)}, u32[]{:S(2)}) collective-permute-start(f32[32,1024]{1,0:T(8,128)S(1)} %get-tuple-element.66), channel_id=1, source_target_pairs={{0,64},{32,96},{64,0},{96,32},{1,65},{33,97},{65,1},{97,33},{2,66}... | collective-permute-start | bytes 393224 | tf_op jit(solution)/shard_map/ppermute | solution.py:21
  81.0 0.3 collective-permute-start.13
  81.3 0.9 collective-permute-start.14
  82.2 0.6 collective-permute-start.9
  82.8 0.1 collective-permute-done.11.refs_3_
  82.9 1.7 %collective-permute-done.12.refs_5_ = f32[32,1024]{1,0:T(8,128)S(1)} collective-permute-done((f32[32,1024]{1,0:T(8,128)S(1)}, f32[32,1024]{1,0:T(8,128)S(1)}, u32[]{:S(2)}, u32[]{:S(2)}) %collective-permute-start.12) | collective-permute-done | bytes 131104 | tf_op jit(solution)/shard_map/ppermute | solution.py:21
  84.5 1.4 collective-permute-done.13.refs_6_
  86.0 0.3 collective-permute-done.14.refs_7_
  86.3 0.9 collective-permute-done.9.refs_1_
  87.1 0.1 column_blocks.1
  87.2 12.9 %all_to_all.21.pieces_ref = f32[8,64,128]{2,1,0:T(8,128)S(1)} all-to-all(f32[8,64,128]{2,1,0:T(8,128)S(1)} %column_blocks.1), channel_id=1, replica_groups=mesh['batch'=2,'queue_0'=4,'queue_1'=4,'queue_2'=8] {'queue_2'}, dimensions={0} | all-to-all | bytes 524288 | tf_op jit(solution)/shard_map/all_to_all | solution.py:416
  100.1 12.9 %all_to_all.22.blocks_ref = f32[8,64,128]{2,1,0:T(8,128)S(1)} all-to-all(f32[8,64,128]{2,1,0:T(8,128)S(1)} %total.1), channel_id=1, replica_groups=mesh['batch'=2,'queue_0'=4,'queue_1'=4,'queue_2'=8] {'queue_2'}, dimensions={0} | all-to-all | bytes 524288 | tf_op jit(solution)/shard_map/all_to_all | solution.py:425
  113.0 2.1 %collective-permute-start.15 = (f32[32,1024]{1,0:T(8,128)S(1)}, f32[32,1024]{1,0:T(8,128)S(1)}, u32[]{:S(2)}, u32[]{:S(2)}) collective-permute-start(f32[32,1024]{1,0:T(8,128)S(1)} %get-tuple-element.69.refs_0_), channel_id=1, source_target_pairs={{0,16},{8,24},{16,0},{24,8},{1,17},{9,25},{17,1},{25,9},{2,18},{10... | collective-permute-start | bytes 393224 | tf_op jit(solution)/shard_map/ppermute | solution.py:21
  115.1 0.6 collective-permute-start.16
  115.7 1.5 collective-permute-start.17
  117.2 3.7 %collective-permute-start.18 = (f32[32,1024]{1,0:T(8,128)S(1)}, f32[32,1024]{1,0:T(8,128)S(1)}, u32[]{:S(2)}, u32[]{:S(2)}) collective-permute-start(f32[32,1024]{1,0:T(8,128)S(1)} %get-tuple-element.70.refs_4_), channel_id=1, source_target_pairs={{0,64},{32,96},{64,0},{96,32},{1,65},{33,97},{65,1},{97,33},{2,66}... | collective-permute-start | bytes 393224 | tf_op jit(solution)/shard_map/ppermute | solution.py:21
  121.0 0.6 collective-permute-start.20
  121.5 1.7 %collective-permute-done.17.refs_3_ = f32[32,1024]{1,0:T(8,128)S(1)} collective-permute-done((f32[32,1024]{1,0:T(8,128)S(1)}, f32[32,1024]{1,0:T(8,128)S(1)}, u32[]{:S(2)}, u32[]{:S(2)}) %collective-permute-start.17) | collective-permute-done | bytes 131104 | tf_op jit(solution)/shard_map/ppermute | solution.py:21
  123.3 1.9 %collective-permute-done.18.refs_5_ = f32[32,1024]{1,0:T(8,128)S(1)} collective-permute-done((f32[32,1024]{1,0:T(8,128)S(1)}, f32[32,1024]{1,0:T(8,128)S(1)}, u32[]{:S(2)}, u32[]{:S(2)}) %collective-permute-start.18) | collective-permute-done | bytes 131104 | tf_op jit(solution)/shard_map/ppermute | solution.py:21
  125.2 2.5 %collective-permute-done.19.refs_6_ = f32[32,1024]{1,0:T(8,128)S(1)} collective-permute-done((f32[32,1024]{1,0:T(8,128)S(1)}, f32[32,1024]{1,0:T(8,128)S(1)}, u32[]{:S(2)}, u32[]{:S(2)}) %collective-permute-start.19) | collective-permute-done | bytes 131104 | tf_op jit(solution)/shard_map/ppermute | solution.py:21
  127.7 0.0 collective-permute-done.20.refs_7_
  127.7 0.1 stacked.1
  127.8 1.6 %collective-permute-start.25 = (f32[128,1024]{1,0:T(8,128)S(1)}, f32[128,1024]{1,0:T(8,128)S(1)}, u32[]{:S(2)}, u32[]{:S(2)}) collective-permute-start(f32[128,1024]{1,0:T(8,128)S(1)} %get-tuple-element.74.refs_1_), channel_id=1, source_target_pairs={{0,24},{8,16},{16,8},{24,0},{1,25},{9,17},{17,9},{25,1},{2,26},{10... | collective-permute-start | bytes 1572872 | tf_op jit(solution)/shard_map/ppermute | solution.py:21
  129.3 0.0 collective-permute-start.26
  129.4 1.0 collective-permute-start.21
  130.3 3.1 %collective-permute-start.22 = (f32[128,1024]{1,0:T(8,128)S(1)}, f32[128,1024]{1,0:T(8,128)S(1)}, u32[]{:S(2)}, u32[]{:S(2)}) collective-permute-start(f32[128,1024]{1,0:T(8,128)S(1)} %get-tuple-element.71.refs_0_), channel_id=1, source_target_pairs={{0,32},{32,0},{64,96},{96,64},{1,33},{33,1},{65,97},{97,65},{2,34}... | collective-permute-start | bytes 1572872 | tf_op jit(solution)/shard_map/ppermute | solution.py:21
  133.5 6.0 %collective-permute-done.25.a.refs_5_ = f32[128,1024]{1,0:T(8,128)S(1)} collective-permute-done((f32[128,1024]{1,0:T(8,128)S(1)}, f32[128,1024]{1,0:T(8,128)S(1)}, u32[]{:S(2)}, u32[]{:S(2)}) %collective-permute-start.25) | collective-permute-done | bytes 524320 | tf_op jit(solution)/shard_map/ppermute | solution.py:21
  139.5 0.1 collective-permute-start.27
  139.6 2.0 %collective-permute-start.28 = (f32[64,1024]{1,0:T(8,128)S(1)}, f32[64,1024]{1,0:T(8,128)S(1)}, u32[]{:S(2)}, u32[]{:S(2)}) collective-permute-start(f32[64,1024]{1,0:T(8,128)S(1)} %get-tuple-element.76), channel_id=1, source_target_pairs={{0,24},{8,16},{16,8},{24,0},{1,25},{9,17},{17,9},{25,1},{2,26},{10... | collective-permute-start | bytes 786440 | tf_op jit(solution)/shard_map/ppermute | solution.py:21
  141.6 3.0 %collective-permute-start.23 = (f32[64,1024]{1,0:T(8,128)S(1)}, f32[64,1024]{1,0:T(8,128)S(1)}, u32[]{:S(2)}, u32[]{:S(2)}) collective-permute-start(f32[64,1024]{1,0:T(8,128)S(1)} %get-tuple-element.72), channel_id=1, source_target_pairs={{0,32},{32,0},{64,96},{96,64},{1,33},{33,1},{65,97},{97,65},{2,34}... | collective-permute-start | bytes 786440 | tf_op jit(solution)/shard_map/ppermute | solution.py:21
  144.6 0.9 collective-permute-start.24
  145.5 1.8 %assembled.2.refs_4_ = f32[1024,1024]{1,0:T(8,128)} custom-call(s32[1]{0:T(128)} %bitcast.refs_1_.x_ref, s32[1]{0:T(128)} %bitcast.1.refs_0_.y_ref, f32[128,1024]{1,0:T(8,128)S(1)} %get-tuple-element.71.refs_0_, f32[128,1024]{1,0:T(8,128)S(1)} %get-tuple-element.74.refs_1_, f32[128,1024]{1,0:T(8,128)S(1)} %collective-permute-done.22.b.refs_2_, ...), custom_call_target="tpu_custom_call" | custom-call | tf_op jit(solution)/shard_map/assembled/pallas_call | solution.py:349
  147.4 1.5 %collective-permute-done.23.refs_0_ = f32[64,1024]{1,0:T(8,128)S(1)} collective-permute-done((f32[64,1024]{1,0:T(8,128)S(1)}, f32[64,1024]{1,0:T(8,128)S(1)}, u32[]{:S(2)}, u32[]{:S(2)}) %collective-permute-start.23) | collective-permute-done | bytes 262176 | tf_op jit(solution)/shard_map/ppermute | solution.py:21
  149.0 2.0 %collective-permute-done.24.refs_1_ = f32[64,1024]{1,0:T(8,128)S(1)} collective-permute-done((f32[64,1024]{1,0:T(8,128)S(1)}, f32[64,1024]{1,0:T(8,128)S(1)}, u32[]{:S(2)}, u32[]{:S(2)}) %collective-permute-start.24) | collective-permute-done | bytes 262176 | tf_op jit(solution)/shard_map/ppermute | solution.py:21
  151.0 1.0 assembled.3
  (23 shorter events, 0.2 us)
Async XLA Ops:
  0.6 44.3 %copy-start = (bf16[1536,1024]{1,0:T(8,128)(2,1)S(1)}, bf16[1536,1024]{1,0:T(8,128)(2,1)}, u32[]{:S(2)}) copy-start(bf16[1536,1024]{1,0:T(8,128)(2,1)} %queue_ref.7) | copy-start | bytes 9437188
  0.7 44.3 %copy-start.1 = (s32[1024]{0:T(1024)S(1)}, s32[1024]{0:T(1024)}, u32[]{:S(2)}) copy-start(s32[1024]{0:T(1024)} %param.7) | copy-start | bytes 12292
  26.7 17.6 %all-to-all-start.1 = ((f32[8,32,128]{2,1,0:T(8,128)}), f32[8,32,128]{2,1,0:T(8,128)S(1)}, u32[]{:S(2)}, u32[]{:S(2)}) async-start(f32[8,32,128]{2,1,0:T(8,128)} %merge_plane.1), calls=%async_computation.1 | async-start | bytes 262144 | tf_op jit(solution)/shard_map/all_to_all | solution.py:383
  48.3 9.2 %collective-permute-start.5 = (f32[64,1024]{1,0:T(8,128)S(1)}, f32[64,1024]{1,0:T(8,128)S(1)}, u32[]{:S(2)}, u32[]{:S(2)}) collective-permute-start(f32[64,1024]{1,0:T(8,128)S(1)} %get-tuple-element.57), channel_id=1, source_target_pairs={{0,8},{8,0},{16,24},{24,16},{1,9},{9,1},{17,25},{25,17},{2,10},{10... | collective-permute-start | bytes 786440 | tf_op jit(solution)/shard_map/ppermute | solution.py:21
  48.8 8.7 %collective-permute-start.6 = (f32[64,1024]{1,0:T(8,128)S(1)}, f32[64,1024]{1,0:T(8,128)S(1)}, u32[]{:S(2)}, u32[]{:S(2)}) collective-permute-start(f32[64,1024]{1,0:T(8,128)S(1)} %get-tuple-element.58), channel_id=1, source_target_pairs={{0,24},{8,16},{16,8},{24,0},{1,25},{9,17},{17,9},{25,1},{2,26},{10... | collective-permute-start | bytes 786440 | tf_op jit(solution)/shard_map/ppermute | solution.py:21
  50.6 10.7 %collective-permute-start.1 = (f32[64,1024]{1,0:T(8,128)S(1)}, f32[64,1024]{1,0:T(8,128)S(1)}, u32[]{:S(2)}, u32[]{:S(2)}) collective-permute-start(f32[64,1024]{1,0:T(8,128)S(1)} %get-tuple-element.50), channel_id=1, source_target_pairs={{0,32},{32,0},{64,96},{96,64},{1,33},{33,1},{65,97},{97,65},{2,34}... | collective-permute-start | bytes 786440 | tf_op jit(solution)/shard_map/ppermute | solution.py:21
  52.2 9.0 %collective-permute-start.2 = (f32[64,1024]{1,0:T(8,128)S(1)}, f32[64,1024]{1,0:T(8,128)S(1)}, u32[]{:S(2)}, u32[]{:S(2)}) collective-permute-start(f32[64,1024]{1,0:T(8,128)S(1)} %get-tuple-element.51), channel_id=1, source_target_pairs={{0,96},{32,64},{64,32},{96,0},{1,97},{33,65},{65,33},{97,1},{2,98}... | collective-permute-start | bytes 786440 | tf_op jit(solution)/shard_map/ppermute | solution.py:21
  58.6 10.9 %collective-permute-start.7 = (f32[128,1024]{1,0:T(8,128)}, f32[128,1024]{1,0:T(8,128)}, u32[]{:S(2)}, u32[]{:S(2)}) collective-permute-start(f32[128,1024]{1,0:T(8,128)} %get-tuple-element.59), channel_id=1, source_target_pairs={{0,8},{8,0},{16,24},{24,16},{1,9},{9,1},{17,25},{25,17},{2,10},{10... | collective-permute-start | bytes 1572872 | tf_op jit(solution)/shard_map/ppermute | solution.py:21
  58.9 11.3 %collective-permute-start.8 = (f32[128,1024]{1,0:T(8,128)}, f32[128,1024]{1,0:T(8,128)}, u32[]{:S(2)}, u32[]{:S(2)}) collective-permute-start(f32[128,1024]{1,0:T(8,128)} %get-tuple-element.60), channel_id=1, source_target_pairs={{0,24},{8,16},{16,8},{24,0},{1,25},{9,17},{17,9},{25,1},{2,26},{10... | collective-permute-start | bytes 1572872 | tf_op jit(solution)/shard_map/ppermute | solution.py:21
  62.3 9.8 %collective-permute-start.3 = (f32[128,1024]{1,0:T(8,128)}, f32[128,1024]{1,0:T(8,128)}, u32[]{:S(2)}, u32[]{:S(2)}) collective-permute-start(f32[128,1024]{1,0:T(8,128)} %get-tuple-element.52), channel_id=1, source_target_pairs={{0,32},{32,0},{64,96},{96,64},{1,33},{33,1},{65,97},{97,65},{2,34}... | collective-permute-start | bytes 1572872 | tf_op jit(solution)/shard_map/ppermute | solution.py:21
  63.8 9.5 %collective-permute-start.4 = (f32[128,1024]{1,0:T(8,128)}, f32[128,1024]{1,0:T(8,128)}, u32[]{:S(2)}, u32[]{:S(2)}) collective-permute-start(f32[128,1024]{1,0:T(8,128)} %get-tuple-element.53), channel_id=1, source_target_pairs={{0,96},{32,64},{64,32},{96,0},{1,97},{33,65},{65,33},{97,1},{2,98}... | collective-permute-start | bytes 1572872 | tf_op jit(solution)/shard_map/ppermute | solution.py:21
  64.8 3.3 %collective-permute-start = (f32[1,1]{1,0:T(1,128)}, f32[1,1]{1,0:T(1,128)}, u32[]{:S(2)}, u32[]{:S(2)}) collective-permute-start(f32[1,1]{1,0:T(1,128)} %get-tuple-element.46), channel_id=1, source_target_pairs={{0,128},{128,0},{1,129},{129,1},{2,130},{130,2},{3,131},{131,3},{4... | collective-permute-start | bytes 20 | tf_op jit(solution)/shard_map/ppermute | solution.py:396
  74.9 7.2 %collective-permute-start.10 = (f32[32,1024]{1,0:T(8,128)S(1)}, f32[32,1024]{1,0:T(8,128)S(1)}, u32[]{:S(2)}, u32[]{:S(2)}) collective-permute-start(f32[32,1024]{1,0:T(8,128)S(1)} %get-tuple-element.63), channel_id=1, source_target_pairs={{0,16},{8,24},{16,0},{24,8},{1,17},{9,25},{17,1},{25,9},{2,18},{10... | collective-permute-start | bytes 393224 | tf_op jit(solution)/shard_map/ppermute | solution.py:21
  76.6 6.3 %collective-permute-start.11 = (f32[32,1024]{1,0:T(8,128)S(1)}, f32[32,1024]{1,0:T(8,128)S(1)}, u32[]{:S(2)}, u32[]{:S(2)}) collective-permute-start(f32[32,1024]{1,0:T(8,128)S(1)} %get-tuple-element.64), channel_id=1, source_target_pairs={{0,24},{8,16},{16,8},{24,0},{1,25},{9,17},{17,9},{25,1},{2,26},{10... | collective-permute-start | bytes 393224 | tf_op jit(solution)/shard_map/ppermute | solution.py:21
  78.1 6.5 %collective-permute-start.12 = (f32[32,1024]{1,0:T(8,128)S(1)}, f32[32,1024]{1,0:T(8,128)S(1)}, u32[]{:S(2)}, u32[]{:S(2)}) collective-permute-start(f32[32,1024]{1,0:T(8,128)S(1)} %get-tuple-element.66), channel_id=1, source_target_pairs={{0,64},{32,96},{64,0},{96,32},{1,65},{33,97},{65,1},{97,33},{2,66}... | collective-permute-start | bytes 393224 | tf_op jit(solution)/shard_map/ppermute | solution.py:21
  81.0 5.0 %collective-permute-start.13 = (f32[32,1024]{1,0:T(8,128)S(1)}, f32[32,1024]{1,0:T(8,128)S(1)}, u32[]{:S(2)}, u32[]{:S(2)}) collective-permute-start(f32[32,1024]{1,0:T(8,128)S(1)} %get-tuple-element.67), channel_id=1, source_target_pairs={{0,32},{32,0},{64,96},{96,64},{1,33},{33,1},{65,97},{97,65},{2,34}... | collective-permute-start | bytes 393224 | tf_op jit(solution)/shard_map/ppermute | solution.py:21
  81.3 5.0 %collective-permute-start.14 = (f32[32,1024]{1,0:T(8,128)S(1)}, f32[32,1024]{1,0:T(8,128)S(1)}, u32[]{:S(2)}, u32[]{:S(2)}) collective-permute-start(f32[32,1024]{1,0:T(8,128)S(1)} %get-tuple-element.68), channel_id=1, source_target_pairs={{0,96},{32,64},{64,32},{96,0},{1,97},{33,65},{65,33},{97,1},{2,98}... | collective-permute-start | bytes 393224 | tf_op jit(solution)/shard_map/ppermute | solution.py:21
  82.2 5.0 %collective-permute-start.9 = (f32[32,1024]{1,0:T(8,128)S(1)}, f32[32,1024]{1,0:T(8,128)S(1)}, u32[]{:S(2)}, u32[]{:S(2)}) collective-permute-start(f32[32,1024]{1,0:T(8,128)S(1)} %get-tuple-element.62), channel_id=1, source_target_pairs={{0,8},{8,0},{16,24},{24,16},{1,9},{9,1},{17,25},{25,17},{2,10},{10... | collective-permute-start | bytes 393224 | tf_op jit(solution)/shard_map/ppermute | solution.py:21
  113.0 7.9 %collective-permute-start.15 = (f32[32,1024]{1,0:T(8,128)S(1)}, f32[32,1024]{1,0:T(8,128)S(1)}, u32[]{:S(2)}, u32[]{:S(2)}) collective-permute-start(f32[32,1024]{1,0:T(8,128)S(1)} %get-tuple-element.69.refs_0_), channel_id=1, source_target_pairs={{0,16},{8,24},{16,0},{24,8},{1,17},{9,25},{17,1},{25,9},{2,18},{10... | collective-permute-start | bytes 393224 | tf_op jit(solution)/shard_map/ppermute | solution.py:21
  115.1 6.4 %collective-permute-start.16 = (f32[32,1024]{1,0:T(8,128)S(1)}, f32[32,1024]{1,0:T(8,128)S(1)}, u32[]{:S(2)}, u32[]{:S(2)}) collective-permute-start(f32[32,1024]{1,0:T(8,128)S(1)} %get-tuple-element.69.refs_0_), channel_id=1, source_target_pairs={{0,8},{8,0},{16,24},{24,16},{1,9},{9,1},{17,25},{25,17},{2,10},{10... | collective-permute-start | bytes 393224 | tf_op jit(solution)/shard_map/ppermute | solution.py:21
  115.7 7.6 %collective-permute-start.17 = (f32[32,1024]{1,0:T(8,128)S(1)}, f32[32,1024]{1,0:T(8,128)S(1)}, u32[]{:S(2)}, u32[]{:S(2)}) collective-permute-start(f32[32,1024]{1,0:T(8,128)S(1)} %get-tuple-element.69.refs_0_), channel_id=1, source_target_pairs={{0,24},{8,16},{16,8},{24,0},{1,25},{9,17},{17,9},{25,1},{2,26},{10... | collective-permute-start | bytes 393224 | tf_op jit(solution)/shard_map/ppermute | solution.py:21
  117.2 8.0 %collective-permute-start.18 = (f32[32,1024]{1,0:T(8,128)S(1)}, f32[32,1024]{1,0:T(8,128)S(1)}, u32[]{:S(2)}, u32[]{:S(2)}) collective-permute-start(f32[32,1024]{1,0:T(8,128)S(1)} %get-tuple-element.70.refs_4_), channel_id=1, source_target_pairs={{0,64},{32,96},{64,0},{96,32},{1,65},{33,97},{65,1},{97,33},{2,66}... | collective-permute-start | bytes 393224 | tf_op jit(solution)/shard_map/ppermute | solution.py:21
  120.9 6.7 %collective-permute-start.19 = (f32[32,1024]{1,0:T(8,128)S(1)}, f32[32,1024]{1,0:T(8,128)S(1)}, u32[]{:S(2)}, u32[]{:S(2)}) collective-permute-start(f32[32,1024]{1,0:T(8,128)S(1)} %get-tuple-element.70.refs_4_), channel_id=1, source_target_pairs={{0,32},{32,0},{64,96},{96,64},{1,33},{33,1},{65,97},{97,65},{2,34}... | collective-permute-start | bytes 393224 | tf_op jit(solution)/shard_map/ppermute | solution.py:21
  121.0 6.8 %collective-permute-start.20 = (f32[32,1024]{1,0:T(8,128)S(1)}, f32[32,1024]{1,0:T(8,128)S(1)}, u32[]{:S(2)}, u32[]{:S(2)}) collective-permute-start(f32[32,1024]{1,0:T(8,128)S(1)} %get-tuple-element.70.refs_4_), channel_id=1, source_target_pairs={{0,96},{32,64},{64,32},{96,0},{1,97},{33,65},{65,33},{97,1},{2,98}... | collective-permute-start | bytes 393224 | tf_op jit(solution)/shard_map/ppermute | solution.py:21
  127.8 11.6 %collective-permute-start.25 = (f32[128,1024]{1,0:T(8,128)S(1)}, f32[128,1024]{1,0:T(8,128)S(1)}, u32[]{:S(2)}, u32[]{:S(2)}) collective-permute-start(f32[128,1024]{1,0:T(8,128)S(1)} %get-tuple-element.74.refs_1_), channel_id=1, source_target_pairs={{0,24},{8,16},{16,8},{24,0},{1,25},{9,17},{17,9},{25,1},{2,26},{10... | collective-permute-start | bytes 1572872 | tf_op jit(solution)/shard_map/ppermute | solution.py:21
  129.3 10.1 %collective-permute-start.26 = (f32[128,1024]{1,0:T(8,128)S(1)}, f32[128,1024]{1,0:T(8,128)S(1)}, u32[]{:S(2)}, u32[]{:S(2)}) collective-permute-start(f32[128,1024]{1,0:T(8,128)S(1)} %get-tuple-element.74.refs_1_), channel_id=1, source_target_pairs={{0,8},{8,0},{16,24},{24,16},{1,9},{9,1},{17,25},{25,17},{2,10},{10... | collective-permute-start | bytes 1572872 | tf_op jit(solution)/shard_map/ppermute | solution.py:21
  129.4 12.2 %collective-permute-start.21 = (f32[128,1024]{1,0:T(8,128)S(1)}, f32[128,1024]{1,0:T(8,128)S(1)}, u32[]{:S(2)}, u32[]{:S(2)}) collective-permute-start(f32[128,1024]{1,0:T(8,128)S(1)} %get-tuple-element.71.refs_0_), channel_id=1, source_target_pairs={{0,96},{32,64},{64,32},{96,0},{1,97},{33,65},{65,33},{97,1},{2,98}... | collective-permute-start | bytes 1572872 | tf_op jit(solution)/shard_map/ppermute | solution.py:21
  130.3 11.2 %collective-permute-start.22 = (f32[128,1024]{1,0:T(8,128)S(1)}, f32[128,1024]{1,0:T(8,128)S(1)}, u32[]{:S(2)}, u32[]{:S(2)}) collective-permute-start(f32[128,1024]{1,0:T(8,128)S(1)} %get-tuple-element.71.refs_0_), channel_id=1, source_target_pairs={{0,32},{32,0},{64,96},{96,64},{1,33},{33,1},{65,97},{97,65},{2,34}... | collective-permute-start | bytes 1572872 | tf_op jit(solution)/shard_map/ppermute | solution.py:21
  139.5 7.9 %collective-permute-start.27 = (f32[64,1024]{1,0:T(8,128)S(1)}, f32[64,1024]{1,0:T(8,128)S(1)}, u32[]{:S(2)}, u32[]{:S(2)}) collective-permute-start(f32[64,1024]{1,0:T(8,128)S(1)} %get-tuple-element.75), channel_id=1, source_target_pairs={{0,8},{8,0},{16,24},{24,16},{1,9},{9,1},{17,25},{25,17},{2,10},{10... | collective-permute-start | bytes 786440 | tf_op jit(solution)/shard_map/ppermute | solution.py:21
  139.6 7.8 %collective-permute-start.28 = (f32[64,1024]{1,0:T(8,128)S(1)}, f32[64,1024]{1,0:T(8,128)S(1)}, u32[]{:S(2)}, u32[]{:S(2)}) collective-permute-start(f32[64,1024]{1,0:T(8,128)S(1)} %get-tuple-element.76), channel_id=1, source_target_pairs={{0,24},{8,16},{16,8},{24,0},{1,25},{9,17},{17,9},{25,1},{2,26},{10... | collective-permute-start | bytes 786440 | tf_op jit(solution)/shard_map/ppermute | solution.py:21
  141.6 7.3 %collective-permute-start.23 = (f32[64,1024]{1,0:T(8,128)S(1)}, f32[64,1024]{1,0:T(8,128)S(1)}, u32[]{:S(2)}, u32[]{:S(2)}) collective-permute-start(f32[64,1024]{1,0:T(8,128)S(1)} %get-tuple-element.72), channel_id=1, source_target_pairs={{0,32},{32,0},{64,96},{96,64},{1,33},{33,1},{65,97},{97,65},{2,34}... | collective-permute-start | bytes 786440 | tf_op jit(solution)/shard_map/ppermute | solution.py:21
  144.6 6.4 %collective-permute-start.24 = (f32[64,1024]{1,0:T(8,128)S(1)}, f32[64,1024]{1,0:T(8,128)S(1)}, u32[]{:S(2)}, u32[]{:S(2)}) collective-permute-start(f32[64,1024]{1,0:T(8,128)S(1)} %get-tuple-element.73), channel_id=1, source_target_pairs={{0,96},{32,64},{64,32},{96,0},{1,97},{33,65},{65,33},{97,1},{2,98}... | collective-permute-start | bytes 786440 | tf_op jit(solution)/shard_map/ppermute | solution.py:21

commit v8 on v7

--- a/solution.py
+++ b/solution.py
@@ -445,8 +445,8 @@
     places = x.reshape(1), y.reshape(1)
     kinds = (0, 0, 0), (1, 0, 0), (0, 1, 0), (0, 3, 0), (1, 1, 0), (1, 3, 0)
     query_grad = assembled(kinds, [first, second, *blocks], None, *places)
-    kinds = (0, 2, 0), (0, 2, 2), (1, 2, 0), (1, 2, 2)
-    query_grad = assembled(kinds, far, query_grad, *places)
+    query_grad = assembled(((1, 2, 0), (1, 2, 2)), far[2:], query_grad, *places)
+    query_grad = assembled(((0, 2, 0), (0, 2, 2)), far[:2], query_grad, *places)
     return (query_grad, loss_value.reshape(()))
 
 

time: 154 us -> 154 us (level)
    pallas_call x2 -> x3, Pallas kernels: 2.87 us -> 3.49 us  [assembled(): pl.pallas_call(functools.partial(assemble_kernel, kinds), in_specs=[pl.Bl...]
where the time goes in v8:
time: 154 us; the launch traced here: 153 us
  starting transfers between devices  45.9 us (30%)
  blocking collectives  40 us (26%)
  waiting for transfers between devices  32.1 us (21%)
  Pallas kernels  31.4 us (20%)
  between operations  3.22 us (2%)
    ppermute x28, starting transfers between devices, exchanged(): return lax.ppermute(part, axis, [(i, i ^ k) for i in range(n)])  37.4 us
    ppermute x28, waiting for transfers between devices, exchanged(): return lax.ppermute(part, axis, [(i, i ^ k) for i in range(n)])  23.1 us
    all_to_all x1, blocking collectives, local(): pieces = lax.all_to_all(sent, (X, Y), 0, 0)  14.3 us
    all_to_all x1, blocking collectives, local(): pieces = lax.all_to_all(blocks, Z, 0, 0)  12.9 us
    all_to_all x1, blocking collectives, local(): blocks = lax.all_to_all(total, Z, 0, 0)  12.9 us
    pallas_call x3, Pallas kernels, shares(): pl.pallas_call(share_kernel, in_specs=[pl.BlockSpec(memory_space=pltpu.SM...  11.4 us
    pallas_call x1, Pallas kernels, local_stats(): pl.pallas_call(stats_kernel, grid=(rows // TILE,), in_specs=[pl.BlockSpec...  11.1 us
    all_to_all x1, waiting for transfers between devices, local(): pieces = lax.all_to_all(sent, Z, 0, 0)  9 us
  transfers between devices with their start and end apart: 30, of which 15 were waited for; matrix products, arithmetic and copies ran while one was open for 0% of the time, Pallas kernels for 8%

profile of v8, /device:TPU:2, one launch (start us, length us, event | category | flops | bytes accessed | tf_op | source)
XLA Modules:
  0.0 152.9 jit_solution(854315673944554903)
XLA Ops:
  0.7 11.1 %local_stats.1 = (f32[3,1024,1536]{2,1,0:T(8,128)}, bf16[6,1024,1536]{2,1,0:T(8,128)(2,1)}, f32[16,32,128]{2,1,0:T(8,128)}) custom-call(s32[1]{0:T(128)} %bitcast.3.base_ref, bf16[1024,1024]{1,0:T(8,128)(2,1)} %queries_ref.1, bf16[1536,1024]{1,0:T(8,128)(2,1)} %queue_ref.7, bf16[1024,1536]{1,0:T(8,128)(2,1)} %mentor_ref.1, s32[8,128]{1,0:T(8,128)} %bitcast.12), custom_call_target="tpu_custom_call" | custom-call | tf_op jit(solution)/shard_map/local_stats/pallas_call | solution.py:88
  11.7 14.3 %all_to_all.20.pieces_ref = f32[16,32,128]{2,1,0:T(8,128)S(1)} all-to-all(f32[16,32,128]{2,1,0:T(8,128)} %get-tuple-element.40), channel_id=1, replica_groups=mesh['batch'=2,'queue_0'=4,'queue_1'=4,'queue_2'=8] {'queue_0','queue_1'}, dimensions={0} | all-to-all | bytes 524288 | tf_op jit(solution)/shard_map/all_to_all | solution.py:374
  26.0 0.7 merge_plane.1
  26.7 8.5 %all-to-all-start.1 = ((f32[8,32,128]{2,1,0:T(8,128)}), f32[8,32,128]{2,1,0:T(8,128)S(1)}, u32[]{:S(2)}, u32[]{:S(2)}) async-start(f32[8,32,128]{2,1,0:T(8,128)} %merge_plane.1), calls=%async_computation.1 | async-start | bytes 262144 | tf_op jit(solution)/shard_map/all_to_all | solution.py:383
  35.2 0.1 pad_add_fusion.2.numbers_ref
  35.3 9.0 %all-to-all-done.1.pieces_ref = f32[8,32,128]{2,1,0:T(8,128)S(1)} async-done(((f32[8,32,128]{2,1,0:T(8,128)}), f32[8,32,128]{2,1,0:T(8,128)S(1)}, u32[]{:S(2)}, u32[]{:S(2)}) %all-to-all-start.1) | async-done | bytes 131104 | tf_op jit(solution)/shard_map/all_to_all | solution.py:383
  44.3 0.7 merge_all.1
  45.0 3.3 %shares.5 = (f32[64,1024]{1,0:T(8,128)S(1)}, f32[64,1024]{1,0:T(8,128)S(1)}, f32[64,1024]{1,0:T(8,128)S(1)}, f32[64,1024]{1,0:T(8,128)S(1)}) custom-call(s32[2]{0:T(128)S(1)} %pad_add_fusion.2.numbers_ref, s32[1]{0:T(128)} %bitcast.3.base_ref, f32[16,128]{1,0:T(8,128)S(1)} %get-tuple-element.41.logs_ref, s32[8,128]{1,0:T(8,128)S(1)} %bitcast.13, ...), custom_call_target="tpu_custom_call" | custom-call | flops 805306368 | bytes 6553600 | tf_op jit(solution)/shard_map/shares/pallas_call | solution.py:184
  48.3 0.5 collective-permute-start.5
  48.8 1.7 %collective-permute-start.6 = (f32[64,1024]{1,0:T(8,128)S(1)}, f32[64,1024]{1,0:T(8,128)S(1)}, u32[]{:S(2)}, u32[]{:S(2)}) collective-permute-start(f32[64,1024]{1,0:T(8,128)S(1)} %get-tuple-element.58), channel_id=1, source_target_pairs={{0,24},{8,16},{16,8},{24,0},{1,25},{9,17},{17,9},{25,1},{2,26},{10... | collective-permute-start | bytes 786440 | tf_op jit(solution)/shard_map/ppermute | solution.py:21
  50.6 1.6 %collective-permute-start.1 = (f32[64,1024]{1,0:T(8,128)S(1)}, f32[64,1024]{1,0:T(8,128)S(1)}, u32[]{:S(2)}, u32[]{:S(2)}) collective-permute-start(f32[64,1024]{1,0:T(8,128)S(1)} %get-tuple-element.50), channel_id=1, source_target_pairs={{0,32},{32,0},{64,96},{96,64},{1,33},{33,1},{65,97},{97,65},{2,34}... | collective-permute-start | bytes 786440 | tf_op jit(solution)/shard_map/ppermute | solution.py:21
  52.2 0.4 collective-permute-start.2
  52.6 0.1 pad_add_fusion.1.numbers_ref
  52.7 4.8 %shares.4 = (f32[128,1024]{1,0:T(8,128)S(1)}, f32[128,1024]{1,0:T(8,128)S(1)}, f32[128,1024]{1,0:T(8,128)S(1)}, f32[128,1024]{1,0:T(8,128)S(1)}) custom-call(s32[4]{0:T(128)S(1)} %pad_add_fusion.1.numbers_ref, s32[1]{0:T(128)} %bitcast.3.base_ref, f32[16,128]{1,0:T(8,128)S(1)} %get-tuple-element.41.logs_ref, s32[8,128]{1,0:T(8,128)S(1)} %bitcast.14, ...), custom_call_target="tpu_custom_call" | custom-call | flops 1610612736 | bytes 9961472 | tf_op jit(solution)/shard_map/shares/pallas_call | solution.py:184
  57.5 1.1 relayed.3
  58.6 0.3 collective-permute-start.7
  58.9 2.4 %collective-permute-start.8 = (f32[128,1024]{1,0:T(8,128)}, f32[128,1024]{1,0:T(8,128)}, u32[]{:S(2)}, u32[]{:S(2)}) collective-permute-start(f32[128,1024]{1,0:T(8,128)} %get-tuple-element.60), channel_id=1, source_target_pairs={{0,24},{8,16},{16,8},{24,0},{1,25},{9,17},{17,9},{25,1},{2,26},{10... | collective-permute-start | bytes 1572872 | tf_op jit(solution)/shard_map/ppermute | solution.py:21
  61.3 1.1 relayed.2
  62.3 1.4 collective-permute-start.3
  63.8 1.0 collective-permute-start.4
  64.7 0.1 pad_add_fusion.numbers_ref
  64.8 0.0 collective-permute-start
  64.8 3.3 %shares.3 = (f32[128,1024]{1,0:T(8,128)S(1)}, f32[128,1024]{1,0:T(8,128)S(1)}) custom-call(s32[2]{0:T(128)S(1)} %pad_add_fusion.numbers_ref, s32[1]{0:T(128)} %bitcast.3.base_ref, f32[16,128]{1,0:T(8,128)S(1)} %get-tuple-element.41.logs_ref, s32[8,128]{1,0:T(8,128)S(1)} %bitcast.15, bf16[1536,1024]{1,0:T(8,128)(2,1)S(1)} %copy-done, ...), custom_call_target="tpu_custom_call" | custom-call | flops 805306368 | bytes 6553600 | tf_op jit(solution)/shard_map/shares/pallas_call | solution.py:184
  69.4 0.8 collective-permute-done.8.refs_7_
  70.2 1.9 %collective-permute-done.3.refs_3_ = f32[128,1024]{1,0:T(8,128)} collective-permute-done((f32[128,1024]{1,0:T(8,128)}, f32[128,1024]{1,0:T(8,128)}, u32[]{:S(2)}, u32[]{:S(2)}) %collective-permute-start.3) | collective-permute-done | bytes 524320 | tf_op jit(solution)/shard_map/ppermute | solution.py:21
  72.1 1.1 collective-permute-done.4.refs_4_
  73.3 1.7 %split_sums.1 = (f32[32,1024]{1,0:T(8,128)S(1)}, f32[32,1024]{1,0:T(8,128)S(1)}, f32[32,1024]{1,0:T(8,128)S(1)}, f32[32,1024]{1,0:T(8,128)S(1)}, f32[32,1024]{1,...) custom-call(s32[1]{0:T(128)} %bitcast.1.refs_0_.y_ref, ...), custom_call_target="tpu_custom_call" | custom-call | bytes 4194304 | tf_op jit(solution)/shard_map/split_sums/pallas_call | solution.py:238
  74.9 1.6 %collective-permute-start.10 = (f32[32,1024]{1,0:T(8,128)S(1)}, f32[32,1024]{1,0:T(8,128)S(1)}, u32[]{:S(2)}, u32[]{:S(2)}) collective-permute-start(f32[32,1024]{1,0:T(8,128)S(1)} %get-tuple-element.63), channel_id=1, source_target_pairs={{0,16},{8,24},{16,0},{24,8},{1,17},{9,25},{17,1},{25,9},{2,18},{10... | collective-permute-start | bytes 393224 | tf_op jit(solution)/shard_map/ppermute | solution.py:21
  76.6 1.5 collective-permute-start.11
  78.1 2.9 %collective-permute-start.12 = (f32[32,1024]{1,0:T(8,128)S(1)}, f32[32,1024]{1,0:T(8,128)S(1)}, u32[]{:S(2)}, u32[]{:S(2)}) collective-permute-start(f32[32,1024]{1,0:T(8,128)S(1)} %get-tuple-element.66), channel_id=1, source_target_pairs={{0,64},{32,96},{64,0},{96,32},{1,65},{33,97},{65,1},{97,33},{2,66}... | collective-permute-start | bytes 393224 | tf_op jit(solution)/shard_map/ppermute | solution.py:21
  81.0 0.3 collective-permute-start.13
  81.3 0.9 collective-permute-start.14
  82.2 0.6 collective-permute-start.9
  82.8 0.1 collective-permute-done.11.refs_3_
  82.9 1.7 %collective-permute-done.12.refs_5_ = f32[32,1024]{1,0:T(8,128)S(1)} collective-permute-done((f32[32,1024]{1,0:T(8,128)S(1)}, f32[32,1024]{1,0:T(8,128)S(1)}, u32[]{:S(2)}, u32[]{:S(2)}) %collective-permute-start.12) | collective-permute-done | bytes 131104 | tf_op jit(solution)/shard_map/ppermute | solution.py:21
  84.5 1.4 collective-permute-done.13.refs_6_
  86.0 0.3 collective-permute-done.14.refs_7_
  86.3 0.9 collective-permute-done.9.refs_1_
  87.1 0.1 column_blocks.1
  87.2 12.9 %all_to_all.21.pieces_ref = f32[8,64,128]{2,1,0:T(8,128)S(1)} all-to-all(f32[8,64,128]{2,1,0:T(8,128)S(1)} %column_blocks.1), channel_id=1, replica_groups=mesh['batch'=2,'queue_0'=4,'queue_1'=4,'queue_2'=8] {'queue_2'}, dimensions={0} | all-to-all | bytes 524288 | tf_op jit(solution)/shard_map/all_to_all | solution.py:416
  100.1 12.9 %all_to_all.22.blocks_ref = f32[8,64,128]{2,1,0:T(8,128)S(1)} all-to-all(f32[8,64,128]{2,1,0:T(8,128)S(1)} %total.1), channel_id=1, replica_groups=mesh['batch'=2,'queue_0'=4,'queue_1'=4,'queue_2'=8] {'queue_2'}, dimensions={0} | all-to-all | bytes 524288 | tf_op jit(solution)/shard_map/all_to_all | solution.py:425
  113.0 2.1 %collective-permute-start.15 = (f32[32,1024]{1,0:T(8,128)S(1)}, f32[32,1024]{1,0:T(8,128)S(1)}, u32[]{:S(2)}, u32[]{:S(2)}) collective-permute-start(f32[32,1024]{1,0:T(8,128)S(1)} %get-tuple-element.69.refs_0_), channel_id=1, source_target_pairs={{0,16},{8,24},{16,0},{24,8},{1,17},{9,25},{17,1},{25,9},{2,18},{10... | collective-permute-start | bytes 393224 | tf_op jit(solution)/shard_map/ppermute | solution.py:21
  115.1 0.6 collective-permute-start.16
  115.7 1.5 collective-permute-start.17
  117.2 3.7 %collective-permute-start.18 = (f32[32,1024]{1,0:T(8,128)S(1)}, f32[32,1024]{1,0:T(8,128)S(1)}, u32[]{:S(2)}, u32[]{:S(2)}) collective-permute-start(f32[32,1024]{1,0:T(8,128)S(1)} %get-tuple-element.70.refs_4_), channel_id=1, source_target_pairs={{0,64},{32,96},{64,0},{96,32},{1,65},{33,97},{65,1},{97,33},{2,66}... | collective-permute-start | bytes 393224 | tf_op jit(solution)/shard_map/ppermute | solution.py:21
  121.0 0.6 collective-permute-start.20
  121.5 1.7 %collective-permute-done.17.refs_3_ = f32[32,1024]{1,0:T(8,128)S(1)} collective-permute-done((f32[32,1024]{1,0:T(8,128)S(1)}, f32[32,1024]{1,0:T(8,128)S(1)}, u32[]{:S(2)}, u32[]{:S(2)}) %collective-permute-start.17) | collective-permute-done | bytes 131104 | tf_op jit(solution)/shard_map/ppermute | solution.py:21
  123.3 1.9 %collective-permute-done.18.refs_5_ = f32[32,1024]{1,0:T(8,128)S(1)} collective-permute-done((f32[32,1024]{1,0:T(8,128)S(1)}, f32[32,1024]{1,0:T(8,128)S(1)}, u32[]{:S(2)}, u32[]{:S(2)}) %collective-permute-start.18) | collective-permute-done | bytes 131104 | tf_op jit(solution)/shard_map/ppermute | solution.py:21
  125.2 2.5 %collective-permute-done.19.refs_6_ = f32[32,1024]{1,0:T(8,128)S(1)} collective-permute-done((f32[32,1024]{1,0:T(8,128)S(1)}, f32[32,1024]{1,0:T(8,128)S(1)}, u32[]{:S(2)}, u32[]{:S(2)}) %collective-permute-start.19) | collective-permute-done | bytes 131104 | tf_op jit(solution)/shard_map/ppermute | solution.py:21
  127.7 0.0 collective-permute-done.20.refs_7_
  127.7 0.1 stacked.1
  127.8 1.6 %collective-permute-start.25 = (f32[128,1024]{1,0:T(8,128)S(1)}, f32[128,1024]{1,0:T(8,128)S(1)}, u32[]{:S(2)}, u32[]{:S(2)}) collective-permute-start(f32[128,1024]{1,0:T(8,128)S(1)} %get-tuple-element.74.refs_1_), channel_id=1, source_target_pairs={{0,24},{8,16},{16,8},{24,0},{1,25},{9,17},{17,9},{25,1},{2,26},{10... | collective-permute-start | bytes 1572872 | tf_op jit(solution)/shard_map/ppermute | solution.py:21
  129.4 1.0 collective-permute-start.21
  130.3 3.1 %collective-permute-start.22 = (f32[128,1024]{1,0:T(8,128)S(1)}, f32[128,1024]{1,0:T(8,128)S(1)}, u32[]{:S(2)}, u32[]{:S(2)}) collective-permute-start(f32[128,1024]{1,0:T(8,128)S(1)} %get-tuple-element.71.refs_0_), channel_id=1, source_target_pairs={{0,32},{32,0},{64,96},{96,64},{1,33},{33,1},{65,97},{97,65},{2,34}... | collective-permute-start | bytes 1572872 | tf_op jit(solution)/shard_map/ppermute | solution.py:21
  133.5 6.0 %collective-permute-done.25.a.refs_5_ = f32[128,1024]{1,0:T(8,128)S(1)} collective-permute-done((f32[128,1024]{1,0:T(8,128)S(1)}, f32[128,1024]{1,0:T(8,128)S(1)}, u32[]{:S(2)}, u32[]{:S(2)}) %collective-permute-start.25) | collective-permute-done | bytes 524320 | tf_op jit(solution)/shard_map/ppermute | solution.py:21
  139.5 0.1 collective-permute-start.27
  139.6 2.0 %collective-permute-start.28 = (f32[64,1024]{1,0:T(8,128)S(1)}, f32[64,1024]{1,0:T(8,128)S(1)}, u32[]{:S(2)}, u32[]{:S(2)}) collective-permute-start(f32[64,1024]{1,0:T(8,128)S(1)} %get-tuple-element.76), channel_id=1, source_target_pairs={{0,24},{8,16},{16,8},{24,0},{1,25},{9,17},{17,9},{25,1},{2,26},{10... | collective-permute-start | bytes 786440 | tf_op jit(solution)/shard_map/ppermute | solution.py:21
  141.6 3.0 %collective-permute-start.23 = (f32[64,1024]{1,0:T(8,128)S(1)}, f32[64,1024]{1,0:T(8,128)S(1)}, u32[]{:S(2)}, u32[]{:S(2)}) collective-permute-start(f32[64,1024]{1,0:T(8,128)S(1)} %get-tuple-element.72), channel_id=1, source_target_pairs={{0,32},{32,0},{64,96},{96,64},{1,33},{33,1},{65,97},{97,65},{2,34}... | collective-permute-start | bytes 786440 | tf_op jit(solution)/shard_map/ppermute | solution.py:21
  144.6 0.9 collective-permute-start.24
  145.5 1.8 %assembled.3.refs_2_ = f32[1024,1024]{1,0:T(8,128)} custom-call(s32[1]{0:T(128)} %bitcast.refs_1_.x_ref, s32[1]{0:T(128)} %bitcast.1.refs_0_.y_ref, f32[128,1024]{1,0:T(8,128)S(1)} %get-tuple-element.71.refs_0_, f32[128,1024]{1,0:T(8,128)S(1)} %get-tuple-element.74.refs_1_, f32[128,1024]{1,0:T(8,128)S(1)} %collective-permute-done.22.b.refs_2_, ...), custom_call_target="tpu_custom_call" | custom-call | tf_op jit(solution)/shard_map/assembled/pallas_call | solution.py:349
  147.4 0.8 assembled.4.refs_2_
  148.2 0.7 collective-permute-done.23.refs_0_
  149.0 2.0 %collective-permute-done.24.refs_1_ = f32[64,1024]{1,0:T(8,128)S(1)} collective-permute-done((f32[64,1024]{1,0:T(8,128)S(1)}, f32[64,1024]{1,0:T(8,128)S(1)}, u32[]{:S(2)}, u32[]{:S(2)}) %collective-permute-start.24) | collective-permute-done | bytes 262176 | tf_op jit(solution)/shard_map/ppermute | solution.py:21
  151.0 0.8 assembled.5
  (24 shorter events, 0.2 us)
Async XLA Ops:
  0.6 44.3 %copy-start = (bf16[1536,1024]{1,0:T(8,128)(2,1)S(1)}, bf16[1536,1024]{1,0:T(8,128)(2,1)}, u32[]{:S(2)}) copy-start(bf16[1536,1024]{1,0:T(8,128)(2,1)} %queue_ref.7) | copy-start | bytes 9437188
  0.7 44.3 %copy-start.1 = (s32[1024]{0:T(1024)S(1)}, s32[1024]{0:T(1024)}, u32[]{:S(2)}) copy-start(s32[1024]{0:T(1024)} %param.7) | copy-start | bytes 12292
  26.7 17.6 %all-to-all-start.1 = ((f32[8,32,128]{2,1,0:T(8,128)}), f32[8,32,128]{2,1,0:T(8,128)S(1)}, u32[]{:S(2)}, u32[]{:S(2)}) async-start(f32[8,32,128]{2,1,0:T(8,128)} %merge_plane.1), calls=%async_computation.1 | async-start | bytes 262144 | tf_op jit(solution)/shard_map/all_to_all | solution.py:383
  48.3 9.2 %collective-permute-start.5 = (f32[64,1024]{1,0:T(8,128)S(1)}, f32[64,1024]{1,0:T(8,128)S(1)}, u32[]{:S(2)}, u32[]{:S(2)}) collective-permute-start(f32[64,1024]{1,0:T(8,128)S(1)} %get-tuple-element.57), channel_id=1, source_target_pairs={{0,8},{8,0},{16,24},{24,16},{1,9},{9,1},{17,25},{25,17},{2,10},{10... | collective-permute-start | bytes 786440 | tf_op jit(solution)/shard_map/ppermute | solution.py:21
  48.8 8.7 %collective-permute-start.6 = (f32[64,1024]{1,0:T(8,128)S(1)}, f32[64,1024]{1,0:T(8,128)S(1)}, u32[]{:S(2)}, u32[]{:S(2)}) collective-permute-start(f32[64,1024]{1,0:T(8,128)S(1)} %get-tuple-element.58), channel_id=1, source_target_pairs={{0,24},{8,16},{16,8},{24,0},{1,25},{9,17},{17,9},{25,1},{2,26},{10... | collective-permute-start | bytes 786440 | tf_op jit(solution)/shard_map/ppermute | solution.py:21
  50.6 10.7 %collective-permute-start.1 = (f32[64,1024]{1,0:T(8,128)S(1)}, f32[64,1024]{1,0:T(8,128)S(1)}, u32[]{:S(2)}, u32[]{:S(2)}) collective-permute-start(f32[64,1024]{1,0:T(8,128)S(1)} %get-tuple-element.50), channel_id=1, source_target_pairs={{0,32},{32,0},{64,96},{96,64},{1,33},{33,1},{65,97},{97,65},{2,34}... | collective-permute-start | bytes 786440 | tf_op jit(solution)/shard_map/ppermute | solution.py:21
  52.2 9.0 %collective-permute-start.2 = (f32[64,1024]{1,0:T(8,128)S(1)}, f32[64,1024]{1,0:T(8,128)S(1)}, u32[]{:S(2)}, u32[]{:S(2)}) collective-permute-start(f32[64,1024]{1,0:T(8,128)S(1)} %get-tuple-element.51), channel_id=1, source_target_pairs={{0,96},{32,64},{64,32},{96,0},{1,97},{33,65},{65,33},{97,1},{2,98}... | collective-permute-start | bytes 786440 | tf_op jit(solution)/shard_map/ppermute | solution.py:21
  58.6 10.9 %collective-permute-start.7 = (f32[128,1024]{1,0:T(8,128)}, f32[128,1024]{1,0:T(8,128)}, u32[]{:S(2)}, u32[]{:S(2)}) collective-permute-start(f32[128,1024]{1,0:T(8,128)} %get-tuple-element.59), channel_id=1, source_target_pairs={{0,8},{8,0},{16,24},{24,16},{1,9},{9,1},{17,25},{25,17},{2,10},{10... | collective-permute-start | bytes 1572872 | tf_op jit(solution)/shard_map/ppermute | solution.py:21
  58.9 11.3 %collective-permute-start.8 = (f32[128,1024]{1,0:T(8,128)}, f32[128,1024]{1,0:T(8,128)}, u32[]{:S(2)}, u32[]{:S(2)}) collective-permute-start(f32[128,1024]{1,0:T(8,128)} %get-tuple-element.60), channel_id=1, source_target_pairs={{0,24},{8,16},{16,8},{24,0},{1,25},{9,17},{17,9},{25,1},{2,26},{10... | collective-permute-start | bytes 1572872 | tf_op jit(solution)/shard_map/ppermute | solution.py:21
  62.3 9.8 %collective-permute-start.3 = (f32[128,1024]{1,0:T(8,128)}, f32[128,1024]{1,0:T(8,128)}, u32[]{:S(2)}, u32[]{:S(2)}) collective-permute-start(f32[128,1024]{1,0:T(8,128)} %get-tuple-element.52), channel_id=1, source_target_pairs={{0,32},{32,0},{64,96},{96,64},{1,33},{33,1},{65,97},{97,65},{2,34}... | collective-permute-start | bytes 1572872 | tf_op jit(solution)/shard_map/ppermute | solution.py:21
  63.8 9.5 %collective-permute-start.4 = (f32[128,1024]{1,0:T(8,128)}, f32[128,1024]{1,0:T(8,128)}, u32[]{:S(2)}, u32[]{:S(2)}) collective-permute-start(f32[128,1024]{1,0:T(8,128)} %get-tuple-element.53), channel_id=1, source_target_pairs={{0,96},{32,64},{64,32},{96,0},{1,97},{33,65},{65,33},{97,1},{2,98}... | collective-permute-start | bytes 1572872 | tf_op jit(solution)/shard_map/ppermute | solution.py:21
  64.8 3.3 %collective-permute-start = (f32[1,1]{1,0:T(1,128)}, f32[1,1]{1,0:T(1,128)}, u32[]{:S(2)}, u32[]{:S(2)}) collective-permute-start(f32[1,1]{1,0:T(1,128)} %get-tuple-element.46), channel_id=1, source_target_pairs={{0,128},{128,0},{1,129},{129,1},{2,130},{130,2},{3,131},{131,3},{4... | collective-permute-start | bytes 20 | tf_op jit(solution)/shard_map/ppermute | solution.py:396
  74.9 7.2 %collective-permute-start.10 = (f32[32,1024]{1,0:T(8,128)S(1)}, f32[32,1024]{1,0:T(8,128)S(1)}, u32[]{:S(2)}, u32[]{:S(2)}) collective-permute-start(f32[32,1024]{1,0:T(8,128)S(1)} %get-tuple-element.63), channel_id=1, source_target_pairs={{0,16},{8,24},{16,0},{24,8},{1,17},{9,25},{17,1},{25,9},{2,18},{10... | collective-permute-start | bytes 393224 | tf_op jit(solution)/shard_map/ppermute | solution.py:21
  76.6 6.3 %collective-permute-start.11 = (f32[32,1024]{1,0:T(8,128)S(1)}, f32[32,1024]{1,0:T(8,128)S(1)}, u32[]{:S(2)}, u32[]{:S(2)}) collective-permute-start(f32[32,1024]{1,0:T(8,128)S(1)} %get-tuple-element.64), channel_id=1, source_target_pairs={{0,24},{8,16},{16,8},{24,0},{1,25},{9,17},{17,9},{25,1},{2,26},{10... | collective-permute-start | bytes 393224 | tf_op jit(solution)/shard_map/ppermute | solution.py:21
  78.1 6.5 %collective-permute-start.12 = (f32[32,1024]{1,0:T(8,128)S(1)}, f32[32,1024]{1,0:T(8,128)S(1)}, u32[]{:S(2)}, u32[]{:S(2)}) collective-permute-start(f32[32,1024]{1,0:T(8,128)S(1)} %get-tuple-element.66), channel_id=1, source_target_pairs={{0,64},{32,96},{64,0},{96,32},{1,65},{33,97},{65,1},{97,33},{2,66}... | collective-permute-start | bytes 393224 | tf_op jit(solution)/shard_map/ppermute | solution.py:21
  81.0 5.0 %collective-permute-start.13 = (f32[32,1024]{1,0:T(8,128)S(1)}, f32[32,1024]{1,0:T(8,128)S(1)}, u32[]{:S(2)}, u32[]{:S(2)}) collective-permute-start(f32[32,1024]{1,0:T(8,128)S(1)} %get-tuple-element.67), channel_id=1, source_target_pairs={{0,32},{32,0},{64,96},{96,64},{1,33},{33,1},{65,97},{97,65},{2,34}... | collective-permute-start | bytes 393224 | tf_op jit(solution)/shard_map/ppermute | solution.py:21
  81.3 5.0 %collective-permute-start.14 = (f32[32,1024]{1,0:T(8,128)S(1)}, f32[32,1024]{1,0:T(8,128)S(1)}, u32[]{:S(2)}, u32[]{:S(2)}) collective-permute-start(f32[32,1024]{1,0:T(8,128)S(1)} %get-tuple-element.68), channel_id=1, source_target_pairs={{0,96},{32,64},{64,32},{96,0},{1,97},{33,65},{65,33},{97,1},{2,98}... | collective-permute-start | bytes 393224 | tf_op jit(solution)/shard_map/ppermute | solution.py:21
  82.2 5.0 %collective-permute-start.9 = (f32[32,1024]{1,0:T(8,128)S(1)}, f32[32,1024]{1,0:T(8,128)S(1)}, u32[]{:S(2)}, u32[]{:S(2)}) collective-permute-start(f32[32,1024]{1,0:T(8,128)S(1)} %get-tuple-element.62), channel_id=1, source_target_pairs={{0,8},{8,0},{16,24},{24,16},{1,9},{9,1},{17,25},{25,17},{2,10},{10... | collective-permute-start | bytes 393224 | tf_op jit(solution)/shard_map/ppermute | solution.py:21
  113.0 7.9 %collective-permute-start.15 = (f32[32,1024]{1,0:T(8,128)S(1)}, f32[32,1024]{1,0:T(8,128)S(1)}, u32[]{:S(2)}, u32[]{:S(2)}) collective-permute-start(f32[32,1024]{1,0:T(8,128)S(1)} %get-tuple-element.69.refs_0_), channel_id=1, source_target_pairs={{0,16},{8,24},{16,0},{24,8},{1,17},{9,25},{17,1},{25,9},{2,18},{10... | collective-permute-start | bytes 393224 | tf_op jit(solution)/shard_map/ppermute | solution.py:21
  115.1 6.4 %collective-permute-start.16 = (f32[32,1024]{1,0:T(8,128)S(1)}, f32[32,1024]{1,0:T(8,128)S(1)}, u32[]{:S(2)}, u32[]{:S(2)}) collective-permute-start(f32[32,1024]{1,0:T(8,128)S(1)} %get-tuple-element.69.refs_0_), channel_id=1, source_target_pairs={{0,8},{8,0},{16,24},{24,16},{1,9},{9,1},{17,25},{25,17},{2,10},{10... | collective-permute-start | bytes 393224 | tf_op jit(solution)/shard_map/ppermute | solution.py:21
  115.7 7.6 %collective-permute-start.17 = (f32[32,1024]{1,0:T(8,128)S(1)}, f32[32,1024]{1,0:T(8,128)S(1)}, u32[]{:S(2)}, u32[]{:S(2)}) collective-permute-start(f32[32,1024]{1,0:T(8,128)S(1)} %get-tuple-element.69.refs_0_), channel_id=1, source_target_pairs={{0,24},{8,16},{16,8},{24,0},{1,25},{9,17},{17,9},{25,1},{2,26},{10... | collective-permute-start | bytes 393224 | tf_op jit(solution)/shard_map/ppermute | solution.py:21
  117.2 8.0 %collective-permute-start.18 = (f32[32,1024]{1,0:T(8,128)S(1)}, f32[32,1024]{1,0:T(8,128)S(1)}, u32[]{:S(2)}, u32[]{:S(2)}) collective-permute-start(f32[32,1024]{1,0:T(8,128)S(1)} %get-tuple-element.70.refs_4_), channel_id=1, source_target_pairs={{0,64},{32,96},{64,0},{96,32},{1,65},{33,97},{65,1},{97,33},{2,66}... | collective-permute-start | bytes 393224 | tf_op jit(solution)/shard_map/ppermute | solution.py:21
  120.9 6.7 %collective-permute-start.19 = (f32[32,1024]{1,0:T(8,128)S(1)}, f32[32,1024]{1,0:T(8,128)S(1)}, u32[]{:S(2)}, u32[]{:S(2)}) collective-permute-start(f32[32,1024]{1,0:T(8,128)S(1)} %get-tuple-element.70.refs_4_), channel_id=1, source_target_pairs={{0,32},{32,0},{64,96},{96,64},{1,33},{33,1},{65,97},{97,65},{2,34}... | collective-permute-start | bytes 393224 | tf_op jit(solution)/shard_map/ppermute | solution.py:21
  121.0 6.8 %collective-permute-start.20 = (f32[32,1024]{1,0:T(8,128)S(1)}, f32[32,1024]{1,0:T(8,128)S(1)}, u32[]{:S(2)}, u32[]{:S(2)}) collective-permute-start(f32[32,1024]{1,0:T(8,128)S(1)} %get-tuple-element.70.refs_4_), channel_id=1, source_target_pairs={{0,96},{32,64},{64,32},{96,0},{1,97},{33,65},{65,33},{97,1},{2,98}... | collective-permute-start | bytes 393224 | tf_op jit(solution)/shard_map/ppermute | solution.py:21
  127.8 11.6 %collective-permute-start.25 = (f32[128,1024]{1,0:T(8,128)S(1)}, f32[128,1024]{1,0:T(8,128)S(1)}, u32[]{:S(2)}, u32[]{:S(2)}) collective-permute-start(f32[128,1024]{1,0:T(8,128)S(1)} %get-tuple-element.74.refs_1_), channel_id=1, source_target_pairs={{0,24},{8,16},{16,8},{24,0},{1,25},{9,17},{17,9},{25,1},{2,26},{10... | collective-permute-start | bytes 1572872 | tf_op jit(solution)/shard_map/ppermute | solution.py:21
  129.3 10.1 %collective-permute-start.26 = (f32[128,1024]{1,0:T(8,128)S(1)}, f32[128,1024]{1,0:T(8,128)S(1)}, u32[]{:S(2)}, u32[]{:S(2)}) collective-permute-start(f32[128,1024]{1,0:T(8,128)S(1)} %get-tuple-element.74.refs_1_), channel_id=1, source_target_pairs={{0,8},{8,0},{16,24},{24,16},{1,9},{9,1},{17,25},{25,17},{2,10},{10... | collective-permute-start | bytes 1572872 | tf_op jit(solution)/shard_map/ppermute | solution.py:21
  129.4 12.2 %collective-permute-start.21 = (f32[128,1024]{1,0:T(8,128)S(1)}, f32[128,1024]{1,0:T(8,128)S(1)}, u32[]{:S(2)}, u32[]{:S(2)}) collective-permute-start(f32[128,1024]{1,0:T(8,128)S(1)} %get-tuple-element.71.refs_0_), channel_id=1, source_target_pairs={{0,96},{32,64},{64,32},{96,0},{1,97},{33,65},{65,33},{97,1},{2,98}... | collective-permute-start | bytes 1572872 | tf_op jit(solution)/shard_map/ppermute | solution.py:21
  130.3 11.2 %collective-permute-start.22 = (f32[128,1024]{1,0:T(8,128)S(1)}, f32[128,1024]{1,0:T(8,128)S(1)}, u32[]{:S(2)}, u32[]{:S(2)}) collective-permute-start(f32[128,1024]{1,0:T(8,128)S(1)} %get-tuple-element.71.refs_0_), channel_id=1, source_target_pairs={{0,32},{32,0},{64,96},{96,64},{1,33},{33,1},{65,97},{97,65},{2,34}... | collective-permute-start | bytes 1572872 | tf_op jit(solution)/shard_map/ppermute | solution.py:21
  139.5 7.9 %collective-permute-start.27 = (f32[64,1024]{1,0:T(8,128)S(1)}, f32[64,1024]{1,0:T(8,128)S(1)}, u32[]{:S(2)}, u32[]{:S(2)}) collective-permute-start(f32[64,1024]{1,0:T(8,128)S(1)} %get-tuple-element.75), channel_id=1, source_target_pairs={{0,8},{8,0},{16,24},{24,16},{1,9},{9,1},{17,25},{25,17},{2,10},{10... | collective-permute-start | bytes 786440 | tf_op jit(solution)/shard_map/ppermute | solution.py:21
  139.6 7.8 %collective-permute-start.28 = (f32[64,1024]{1,0:T(8,128)S(1)}, f32[64,1024]{1,0:T(8,128)S(1)}, u32[]{:S(2)}, u32[]{:S(2)}) collective-permute-start(f32[64,1024]{1,0:T(8,128)S(1)} %get-tuple-element.76), channel_id=1, source_target_pairs={{0,24},{8,16},{16,8},{24,0},{1,25},{9,17},{17,9},{25,1},{2,26},{10... | collective-permute-start | bytes 786440 | tf_op jit(solution)/shard_map/ppermute | solution.py:21
  141.6 7.3 %collective-permute-start.23 = (f32[64,1024]{1,0:T(8,128)S(1)}, f32[64,1024]{1,0:T(8,128)S(1)}, u32[]{:S(2)}, u32[]{:S(2)}) collective-permute-start(f32[64,1024]{1,0:T(8,128)S(1)} %get-tuple-element.72), channel_id=1, source_target_pairs={{0,32},{32,0},{64,96},{96,64},{1,33},{33,1},{65,97},{97,65},{2,34}... | collective-permute-start | bytes 786440 | tf_op jit(solution)/shard_map/ppermute | solution.py:21
  144.6 6.4 %collective-permute-start.24 = (f32[64,1024]{1,0:T(8,128)S(1)}, f32[64,1024]{1,0:T(8,128)S(1)}, u32[]{:S(2)}, u32[]{:S(2)}) collective-permute-start(f32[64,1024]{1,0:T(8,128)S(1)} %get-tuple-element.73), channel_id=1, source_target_pairs={{0,96},{32,64},{64,32},{96,0},{1,97},{33,65},{65,33},{97,1},{2,98}... | collective-permute-start | bytes 786440 | tf_op jit(solution)/shard_map/ppermute | solution.py:21
